TPU v7x, 256 devices: a whole 4x4x8 slice. The times are simulated.
256 devices in a mesh: blk: 64 (over x_hi, z, y), head: 4 (over x_lo, core).
Axes of the slice: x: 4 (x_hi: 2, x_lo: 2; x = x_hi * 2 + x_lo), y: 4, z: 8, core: 2. Of those that a mesh axis runs over, the one named last changes fastest.
Arguments:
- context_q: bfloat16 [8192, 8192], P('blk', 'head'), may hold values from -200 to 200
- context_k: bfloat16 [8192, 1024], P('blk', 'head'), may hold values from -6 to 6
- context_v: bfloat16 [8192, 1024], P('blk', 'head'), may hold values from -6 to 6
- anchor_k: bfloat16 [1024, 1024], P('blk', 'head'), may hold values from -6 to 6
- anchor_v: bfloat16 [1024, 1024], P('blk', 'head'), may hold values from -6 to 6
- parent_q: bfloat16 [256, 8192], P('blk', 'head'), may hold values from -200 to 200
- block_of_slot: int32 [64], replicated, may hold values from 0 to 63, each once
- agent_lengths: int32 [8], replicated, may hold values from 1 to 2048, 8192 in all
- query_pos: int32 [256], replicated, may hold values from 1 to 8192
Outputs:
- context_out: bfloat16 [8192, 8192], P('blk', 'head')
- parent_out: bfloat16 [256, 8192], P(('blk', 'head'))
All inputs are finite; a program needn't handle non-finite values.
Results may differ from a plain program's by a relative error of at most 0.008.
Values may be sent and summed in bfloat16 or wider, within the bound.
No kernel may reach another device: no remote copies, remote signals or barrier semaphores. Data moves between devices by JAX's collectives and lax.ppermute only.
A program may use at most 64 MiB of HBM per device.

v0:
```python
import math

import jax
import jax.numpy as jnp
from jax import lax
from jax.sharding import PartitionSpec as P

HD = 128


def partial_attend(grouped_q, keys, values, visible, per_group):
    scale = 1.0 / math.sqrt(HD)
    keys_t = jnp.transpose(keys, (1, 0, 2))
    vals_t = jnp.transpose(values, (1, 0, 2))
    scores = (
        jnp.einsum("gqd,gkd->gqk", grouped_q, keys_t, preferred_element_type=jnp.float32) * scale
    )
    groups, flat_rows, width = scores.shape
    query_rows = visible.shape[0]
    scores = scores.reshape(groups, query_rows, per_group, width)
    scores = jnp.where(visible[None, :, None, :], scores, -jnp.inf).reshape(
        groups, flat_rows, width
    )
    peak = jnp.max(scores, axis=-1)
    expo = jnp.exp(scores - peak[..., None])
    total = jnp.sum(expo, axis=-1)
    summed = jnp.einsum(
        "gqk,gkd->gqd", expo.astype(jnp.bfloat16), vals_t, preferred_element_type=jnp.float32
    )
    return (peak, total, summed)


def combine_parts(first, second):
    peak = jnp.maximum(first[0], second[0])
    left = jnp.exp(first[0] - peak)
    right = jnp.exp(second[0] - peak)
    total = first[1] * left + second[1] * right
    summed = first[2] * left[..., None] + second[2] * right[..., None]
    return (peak, total, summed)


def to_grouped(matrix, groups, per_group):
    count = matrix.shape[0]
    return jnp.transpose(matrix.reshape(count, groups, per_group, HD), (1, 0, 2, 3)).reshape(
        groups, count * per_group, HD
    )


def from_grouped(summed, total, groups, per_group):
    count = summed.shape[1] // per_group
    result = (summed / total[..., None]).reshape(groups, count, per_group, HD)
    return jnp.transpose(result, (1, 0, 2, 3)).reshape(count, groups * per_group * HD)


def on_device(
    context_q,
    context_k,
    context_v,
    anchor_k,
    anchor_v,
    parent_q,
    block_of_slot,
    agent_lengths,
    query_pos,
):
    rows = context_q.shape[0]
    width = context_q.shape[1]
    groups = context_k.shape[1] // HD
    per_group = width // (HD * groups)
    slot = lax.axis_index("blk")
    positions = block_of_slot[slot] * rows + jnp.arange(rows, dtype=jnp.int32)
    ends = jnp.cumsum(agent_lengths)
    agents = jnp.sum((positions[:, None] >= ends[None, :]).astype(jnp.int32), axis=1)
    gathered_k, gathered_v = (
        lax.all_gather(anchor_k, "blk", axis=0, tiled=True),
        lax.all_gather(anchor_v, "blk", axis=0, tiled=True),
    )
    anchor_len = gathered_k.shape[0]
    keys_all = jnp.concatenate([gathered_k, context_k], 0).reshape(anchor_len + rows, groups, HD)
    vals_all = jnp.concatenate([gathered_v, context_v], 0).reshape(anchor_len + rows, groups, HD)
    key_pos = jnp.concatenate([jnp.full((anchor_len,), -1, jnp.int32), positions])
    key_agent = jnp.concatenate([jnp.full((anchor_len,), -1, jnp.int32), agents])
    queries = to_grouped(context_q, groups, per_group)
    step_keys = min(512, rows)
    count = (anchor_len + rows) // step_keys

    def key_block(index, carry):
        start = index * step_keys
        keys = lax.dynamic_slice_in_dim(keys_all, start, step_keys, 0)
        values = lax.dynamic_slice_in_dim(vals_all, start, step_keys, 0)
        where_pos = lax.dynamic_slice_in_dim(key_pos, start, step_keys, 0)
        where_agent = lax.dynamic_slice_in_dim(key_agent, start, step_keys, 0)
        visible = (where_pos[None, :] < 0) | (where_pos[None, :] <= positions[:, None]) & (
            where_agent[None, :] == agents[:, None]
        )
        return combine_parts(carry, partial_attend(queries, keys, values, visible, per_group))

    flat = rows * per_group
    start_carry = (
        jnp.full((groups, flat), -jnp.inf, jnp.float32),
        jnp.zeros((groups, flat), jnp.float32),
        jnp.zeros((groups, flat, HD), jnp.float32),
    )
    peak, total, summed = lax.fori_loop(0, count, key_block, start_carry)
    context_out = from_grouped(summed, total, groups, per_group).astype(jnp.bfloat16)
    parent_all = lax.all_gather(parent_q, "blk", axis=0, tiled=True)
    parent_rows = parent_all.shape[0]
    own_rows = parent_q.shape[0]
    local_anchor = anchor_k.shape[0]
    near_keys = jnp.concatenate([anchor_k, context_k], 0).reshape(local_anchor + rows, groups, HD)
    near_vals = jnp.concatenate([anchor_v, context_v], 0).reshape(local_anchor + rows, groups, HD)
    near_pos = jnp.concatenate([jnp.full((local_anchor,), -1, jnp.int32), positions])
    visible = near_pos[None, :] < query_pos[:, None]
    part = partial_attend(
        to_grouped(parent_all, groups, per_group), near_keys, near_vals, visible, per_group
    )
    peak = lax.pmax(part[0], "blk")
    factor = jnp.exp(part[0] - peak)
    numer = (part[2] * factor[..., None]).reshape(groups, parent_rows, per_group, HD)
    numer = jnp.transpose(numer, (1, 0, 2, 3)).reshape(parent_rows, width)
    denom = (part[1] * factor).reshape(groups, parent_rows, per_group)
    denom = jnp.transpose(denom, (1, 0, 2)).reshape(parent_rows, groups * per_group)
    numer, denom = (
        lax.psum_scatter(numer, "blk", scatter_dimension=0, tiled=True),
        lax.psum_scatter(denom, "blk", scatter_dimension=0, tiled=True),
    )
    result = (
        (
            numer.reshape(own_rows, groups, per_group, HD)
            / denom.reshape(own_rows, groups, per_group)[..., None]
        )
        .reshape(own_rows, width)
        .astype(jnp.bfloat16)
    )
    parent_out = lax.all_to_all(result, "head", split_axis=0, concat_axis=1, tiled=True)
    return (context_out, parent_out)


def solution(mesh):
    return jax.shard_map(
        on_device,
        mesh=mesh,
        in_specs=(
            P("blk", "head"),
            P("blk", "head"),
            P("blk", "head"),
            P("blk", "head"),
            P("blk", "head"),
            P("blk", "head"),
            P(),
            P(),
            P(),
        ),
        out_specs=(P("blk", "head"), P(("blk", "head"), None)),
        check_vma=False,
    )
```

profile of v0, /device:TPU:1, one launch (start us, length us, event | category | flops | bytes accessed | tf_op | source)
XLA Modules:
  0.0 1458.4 jit_solution(11708891389166072867)
XLA Ops:
  8.0 1.2 dynamic_slice.31
  13.9 160.9 %all_gather.9 = bf16[1024,256]{1,0:T(8,128)(2,1)S(1)} all-gather(bf16[16,256]{1,0:T(8,128)(2,1)} %param.14), channel_id=1, replica_groups=mesh['blk'=64,'head'=4] {'blk'}, dimensions={0}, use_global_device_ids=true | all-gather | bytes 532480 | tf_op jit(solution)/shard_map/all_gather | solution.py:75
  175.8 149.0 %all_gather.10 = bf16[1024,256]{1,0:T(8,128)(2,1)S(1)} all-gather(bf16[16,256]{1,0:T(8,128)(2,1)S(1)} %copy-done.5), channel_id=1, replica_groups=mesh['blk'=64,'head'=4] {'blk'}, dimensions={0}, use_global_device_ids=true | all-gather | bytes 532480 | tf_op jit(solution)/shard_map/all_gather | solution.py:76
  325.7 1.2 copy.101
  326.9 0.9 pad_maximum_fusion
  327.8 0.9 pad_maximum_fusion.1
  328.7 1.7 reshape.204
  330.4 2.9 fusion.29
  333.3 297.9 %pmax.7 = f32[2,2048]{1,0:T(2,128)S(1)} all-reduce(f32[2,2048]{1,0:T(2,128)S(1)} %get-tuple-element.306), channel_id=1, replica_groups=mesh['blk'=64,'head'=4] {'blk'}, use_global_device_ids=true, to_apply=%region_7.8 | all-reduce | flops 4096 | bytes 32768 | tf_op jit(solution)/shard_map/pmax | solution.py:117
  631.2 2.2 fusion.15
  633.6 2.3 fusion.17
  635.9 2.9 copy.86
  638.9 43.4 %while.18 = (s32[]{:T(128)}, f32[2,1024]{1,0:T(2,128)S(1)}, f32[2,1024]{1,0:T(2,128)S(1)}, f32[2,1024,128]{2,1,0:T(8,128)S(1)}, s32[1152]{0:T(1024)}, /*index=5*...) while((s32[]{:T(128)}, f32[2,1024]{1,0:T(2,128)S(1)}, ...), condition=%wide.region_5.6_spmd.clone, body=%wide.region_2.5_spmd.clone.sunk | while | flops 137179392 | bytes 7099350 | solution.py:104
  642.6 1.2 fusion.44
  647.4 1.2 fusion.44
  650.5 0.9 constant_dynamic-slice_fusion.3
  652.2 1.2 fusion.44
  655.3 0.9 constant_dynamic-slice_fusion.3
  657.0 1.2 fusion.44
  660.2 0.9 constant_dynamic-slice_fusion.3
  661.8 1.2 fusion.44
  666.7 1.2 fusion.44
  671.5 1.2 fusion.44
  676.3 1.2 fusion.44
  681.1 1.2 fusion.44
  683.8 299.2 %all-reduce.4 = f32[256,16]{0,1:T(8,128)S(1)} all-reduce(f32[256,16]{0,1:T(8,128)S(1)} %bitcast.109), channel_id=3, replica_groups=mesh['blk'=64,'head'=4] {'blk'}, use_global_device_ids=true, to_apply=%region_10.11.clone | all-reduce | flops 4096 | bytes 32768
  983.1 411.0 %all-reduce.7.cloned.1.call-done = f32[256,2048]{0,1:T(8,128)} async-done(((f32[256,2048]{0,1:T(8,128)}), f32[256,2048]{0,1:T(8,128)}) %all-reduce.7.cloned.1.call-update) | async-done | bytes 2097168
  1394.2 1.6 fusion.21
  1396.2 1.1 reduce
  1398.2 49.6 %all-to-all-start = ((bf16[4,2,1024]{2,1,0:T(2,128)(2,1)}), bf16[4,2,1024]{2,1,0:T(2,128)(2,1)S(1)}, u32[]{:S(2)}, u32[]{:S(2)}) async-start(bf16[4,2,1024]{2,1,0:T(2,128)(2,1)} %reshape.220), calls=%async_computation | async-start | bytes 32768 | tf_op jit(solution)/shard_map/all_to_all | solution.py:135
  1448.3 0.9 copy.121
  1449.2 1.8 all-to-all-done
  (152 shorter events, 40.0 us)
Async XLA Ops:
  7.2 167.8 %copy-start.4 = (bf16[128,256]{1,0:T(8,128)(2,1)S(1)}, bf16[128,256]{1,0:T(8,128)(2,1)}, u32[]{:S(2)}) copy-start(bf16[128,256]{1,0:T(8,128)(2,1)} %param.12) | copy-start | bytes 196612
  7.2 168.6 %copy-start.5 = (bf16[16,256]{1,0:T(8,128)(2,1)S(1)}, bf16[16,256]{1,0:T(8,128)(2,1)}, u32[]{:S(2)}) copy-start(bf16[16,256]{1,0:T(8,128)(2,1)} %param.15) | copy-start | bytes 24580
  7.2 321.5 %all-gather.3.cloned.1.call-start = ((), (), s32[]{:S(2)}) async-start(), calls=%async_computation.1 | async-start | bytes 1064960 | tf_op jit(solution)/shard_map/all_gather | solution.py:106
  7.9 1386.3 %all-reduce.7.cloned.1.call-start = ((), (), s32[]{:S(2)}) async-start(), calls=%async_computation.2 | async-start | bytes 4194304
  11.3 313.6 %copy-start.1 = (bf16[128,256]{1,0:T(8,128)(2,1)S(1)}, bf16[128,256]{1,0:T(8,128)(2,1)}, u32[]{:S(2)}) copy-start(bf16[128,256]{1,0:T(8,128)(2,1)} %param.13) | copy-start | bytes 196612
  325.7 2.1 copy-start.3
  333.3 300.1 %copy-start.2 = (bf16[128,256]{1,0:T(8,128)(2,1)S(1)}, bf16[128,256]{1,0:T(8,128)(2,1)}, u32[]{:S(2)}) copy-start(bf16[128,256]{1,0:T(8,128)(2,1)} %param.13) | copy-start | bytes 196612
  631.2 2.4 copy-start
  638.9 43.4 %copy-start.6 = (u32[256]{0:T(256)S(1)}, u32[256]{0:T(256)}, u32[]{:S(2)}) copy-start(u32[256]{0:T(256)} %constant.86) | copy-start | bytes 3076
  1398.2 52.7 %all-to-all-start = ((bf16[4,2,1024]{2,1,0:T(2,128)(2,1)}), bf16[4,2,1024]{2,1,0:T(2,128)(2,1)S(1)}, u32[]{:S(2)}, u32[]{:S(2)}) async-start(bf16[4,2,1024]{2,1,0:T(2,128)(2,1)} %reshape.220), calls=%async_computation | async-start | bytes 32768 | tf_op jit(solution)/shard_map/all_to_all | solution.py:135
Sparse Core Ops, SparseCore 0:
  11.8 114.0 all-gather.2
  639.0 755.0 all-reduce.6
where the time goes:
time: 1460 us
  blocking collectives  907 us (62%)
  waiting for transfers between devices  413 us (28%)
  starting transfers between devices  49.7 us (3%)
  local copies, waits for them, and re-layouts  34.8 us (2%)
  matrix products  18.9 us (1%)
  other arithmetic  18.3 us (1%)
  between operations  15.6 us (1%)
    unnamed x3, waiting for transfers between devices  412 us
    unnamed x1, blocking collectives  299 us
    pmax x1, blocking collectives, on_device(): peak = lax.pmax(part[0], 'blk')  298 us
    all_gather x1, blocking collectives, on_device(): lax.all_gather(anchor_k, 'blk', axis=0, tiled=True)  161 us
    all_gather x1, blocking collectives, on_device(): lax.all_gather(anchor_v, 'blk', axis=0, tiled=True)  149 us
    all_to_all x1, starting transfers between devices, on_device(): lax.all_to_all(result, 'head', split_axis=0, concat_axis=1, tiled=True)  49.6 us
  transfers between devices with their start and end apart: 3, of which 2 were waited for; matrix products, arithmetic and copies ran while one was open for 4% of the time, Pallas kernels for 0%

commit v1 on v0

v1 whole, which is shorter than its diff:
```python
import functools
import math

import jax
import jax.numpy as jnp
from jax import lax
from jax.experimental import pallas as pl
from jax.experimental.pallas import tpu as pltpu
from jax.sharding import Mesh
from jax.sharding import PartitionSpec as P

HD = 128
NX, NZ, NY, NL, NC = 2, 8, 4, 2, 2
NB = NX * NZ
NH = NL * NC
GROUPS = 2
PER = 8
GH = GROUPS * PER
TOK = 128
ANC = 16
QR = 4
KVR = TOK + ANC
KEYS = 640
STRIDE = 4 * ANC
LOG2E = 1.4426950408889634
SCALE = LOG2E / math.sqrt(HD)
BF = jnp.bfloat16
F32 = jnp.float32
VMEM = pl.BlockSpec(memory_space=pltpu.VMEM)
SMEM = pl.BlockSpec(memory_space=pltpu.SMEM)


def params():
    return pltpu.CompilerParams(vmem_limit_bytes=40 * 1024 * 1024)


def nt(a, b):
    return lax.dot_general(a, b, (((1,), (1,)), ((), ())), preferred_element_type=F32)


def prep_kernel(ak, av, pq, ck, cv, send, kv, scr):
    q = pq[...].astype(F32)
    for g in range(GROUPS):
        for r in range(QR):
            for h in range(PER):
                col = (g * PER + h) * HD
                row = (g * QR + r) * PER + h
                scr[row : row + 1, :] = q[r : r + 1, col : col + HD]
    parts = [ak[:, :HD], ak[:, HD:], av[:, :HD], av[:, HD:]]
    chunk = jnp.concatenate(parts + [scr[...].astype(BF)], 0)
    for b in range(NB):
        send[b] = chunk
    ctx = [ck[:, :HD], ck[:, HD:], cv[:, :HD], cv[:, HD:]]
    for i in range(4):
        kv[i, :TOK, :] = ctx[i]
        kv[i, TOK:, :] = parts[i]


def parent_kernel(bos, qp, got, kv0, kv1, kv2, kv3, out, stat, keys, vals, qpos):
    slot = (lax.axis_index("xh") * NZ + lax.axis_index("z")) * NY
    y = lax.axis_index("y")
    blocks = [kv0, kv1, kv2, kv3]
    pad = jnp.zeros((KEYS - NY * KVR, HD), BF)
    for g in range(GROUPS):
        for i in range(NY):
            keys[g, i * TOK : (i + 1) * TOK, :] = blocks[i][g, :TOK, :]
            vals[g, i * TOK : (i + 1) * TOK, :] = blocks[i][2 + g, :TOK, :]
            at = NY * TOK + i * ANC
            keys[g, at : at + ANC, :] = blocks[i][g, TOK:, :]
            vals[g, at : at + ANC, :] = blocks[i][2 + g, TOK:, :]
        keys[g, NY * KVR :, :] = pad
        vals[g, NY * KVR :, :] = pad
    for b in range(NB):
        for r in range(QR):
            row = (b * QR + r) * PER
            qpos[row : row + PER, :] = jnp.full((PER, HD), qp[(b * NY + y) * QR + r], jnp.int32)
    lane = lax.broadcasted_iota(jnp.int32, (1, KEYS), 1)
    kpos = jnp.where(lane < NY * KVR, -1, 1 << 30)
    for i in range(NY):
        src = slot + lax.rem(y + NY - i, NY)
        base = bos[src] * TOK - i * TOK
        kpos = jnp.where((lane >= i * TOK) & (lane < (i + 1) * TOK), lane + base, kpos)
    visible = kpos < qpos[:, :1]
    rows = NB * QR * PER
    parts, stats = [], jnp.zeros((NB * QR, HD), F32)
    lanes = lax.broadcasted_iota(jnp.int32, (1, PER, HD), 2)
    heads = lax.broadcasted_iota(jnp.int32, (1, PER, HD), 1)
    for g in range(GROUPS):
        lo = STRIDE + g * QR * PER
        q = got[:, lo : lo + QR * PER, :].reshape(rows, HD)
        s = nt(q, keys[g]) * SCALE
        s = jnp.where(visible, s, -1e30)
        m = jnp.max(s, axis=1, keepdims=True)
        p = jnp.exp2(s - m)
        total = jnp.sum(p, axis=1, keepdims=True)
        o = jnp.dot(p.astype(BF), vals[g], preferred_element_type=F32)
        o = o / total
        parts.append(o.reshape(NB * QR, PER, HD))
        lse = m + jnp.log2(total)
        hi = lse.astype(BF).astype(F32)
        mid = (lse - hi).astype(BF).astype(F32)
        low = lse - hi - mid
        pick = lanes - g * PER
        for k, part in enumerate((hi, mid, low)):
            wide = jnp.broadcast_to(part, (rows, HD)).reshape(NB * QR, PER, HD)
            stats = stats + jnp.sum(jnp.where(pick - k * GH == heads, wide, 0.0), axis=1)
    out[...] = jnp.concatenate(parts, 1).astype(BF)
    stat[...] = stats.astype(BF)


def context_kernel(bos, lens, q_ref, ck, cv, a0, a1, a2, a3, out, keys, vals):
    slot = (lax.axis_index("xh") * NZ + lax.axis_index("z")) * NY + lax.axis_index("y")
    base = bos[slot] * TOK
    count = NB * ANC
    for i, a in enumerate((a0, a1, a2, a3)):
        for g in range(GROUPS):
            k, v = g * ANC, (GROUPS + g) * ANC
            keys[g, i * count : (i + 1) * count, :] = a[:, k : k + ANC, :].reshape(count, HD)
            vals[g, i * count : (i + 1) * count, :] = a[:, v : v + ANC, :].reshape(count, HD)
    mine = lax.broadcasted_iota(jnp.int32, (TOK, TOK), 0)
    other = lax.broadcasted_iota(jnp.int32, (TOK, TOK), 1)
    visible = other <= mine
    end = jnp.int32(0)
    for j in range(lens.shape[0]):
        end = end + lens[j]
        visible = visible & ((mine + base >= end) == (other + base >= end))
    for g in range(GROUPS):
        own_k = ck[:, g * HD : (g + 1) * HD]
        own_v = cv[:, g * HD : (g + 1) * HD]
        for half in range(4):
            hs = [g * PER + half * 2 + j for j in range(2)]
            q = jnp.concatenate([q_ref[:, h * HD : (h + 1) * HD] for h in hs], 0)
            sa = nt(q, keys[g]) * SCALE
            so = nt(q, own_k) * SCALE
            so = jnp.where(visible[None], so.reshape(2, TOK, TOK), -1e30).reshape(2 * TOK, TOK)
            m = jnp.maximum(jnp.max(sa, axis=1, keepdims=True), jnp.max(so, axis=1, keepdims=True))
            pa = jnp.exp2(sa - m)
            po = jnp.exp2(so - m)
            total = jnp.sum(pa, axis=1, keepdims=True) + jnp.sum(po, axis=1, keepdims=True)
            o = jnp.dot(pa.astype(BF), vals[g], preferred_element_type=F32)
            o = o + jnp.dot(po.astype(BF), own_v, preferred_element_type=F32)
            o = (o / total).astype(BF)
            for j, h in enumerate(hs):
                out[:, h * HD : (h + 1) * HD] = o[j * TOK : (j + 1) * TOK]


def combine_kernel(got, out):
    st = got[:, GH * HD :].astype(F32)
    lse = st + pltpu.roll(st, HD - GH, 1) + pltpu.roll(st, HD - 2 * GH, 1)
    tiles = lse.reshape(NB * NH // 8, 8, HD)
    top = jnp.max(tiles, axis=0)
    top = jnp.maximum(top, pltpu.roll(top, 4, 0))
    w = jnp.exp2(tiles - top[None])
    total = jnp.sum(w, axis=0)
    total = total + pltpu.roll(total, 4, 0)
    w = (w / total[None]).reshape(NB * NH, HD)
    for h in range(GH):
        x = got[:, h * HD : (h + 1) * HD].astype(F32) * w[:, h : h + 1]
        x = jnp.sum(x.reshape(NB * NH // 8, 8, HD), axis=0)
        x = x + pltpu.roll(x, 4, 0)
        for k in range(NH):
            at = (k * GH + h) * HD
            out[:, at : at + HD] = x[k : k + 1].astype(BF)


def on_device(cq, ck, cv, ak, av, pq, bos, lens, qp):
    send, kv = pl.pallas_call(
        prep_kernel,
        out_shape=(
            jax.ShapeDtypeStruct((NB, 2 * STRIDE, HD), BF),
            jax.ShapeDtypeStruct((4, KVR, HD), BF),
        ),
        in_specs=[VMEM] * 5,
        out_specs=(VMEM, VMEM),
        scratch_shapes=[pltpu.VMEM((STRIDE, HD), F32)],
        compiler_params=params(),
        name="prep",
    )(ak, av, pq, ck, cv)

    def turn(x, shift):
        return lax.ppermute(x, "y", [(i, (i + shift) % NY) for i in range(NY)])

    kvs = [kv] + [turn(kv, s) for s in (1, 2, 3)]
    got = lax.all_to_all(send, ("xh", "z"), 0, 0, tiled=True)
    anchors = got[:, :STRIDE]
    anchors = [anchors] + [turn(anchors, s) for s in (1, 2, 3)]
    part, stat = pl.pallas_call(
        parent_kernel,
        out_shape=(
            jax.ShapeDtypeStruct((NB * QR, GH, HD), BF),
            jax.ShapeDtypeStruct((NB * QR, HD), BF),
        ),
        in_specs=[SMEM] * 2 + [VMEM] * 5,
        out_specs=(VMEM, VMEM),
        scratch_shapes=[
            pltpu.VMEM((GROUPS, KEYS, HD), BF),
            pltpu.VMEM((GROUPS, KEYS, HD), BF),
            pltpu.VMEM((NB * QR * PER, HD), jnp.int32),
        ],
        compiler_params=params(),
        cost_estimate=pl.CostEstimate(flops=10**9, bytes_accessed=2 * 10**6, transcendentals=10**6),
        name="parent",
    )(bos, qp, got, *kvs)
    packed = jnp.concatenate([part.reshape(NB * QR, GH * HD), stat], 1)
    back = lax.all_to_all(packed, ("xh", "z", "xl", "c"), 0, 0, tiled=True)
    context = pl.pallas_call(
        context_kernel,
        out_shape=jax.ShapeDtypeStruct((TOK, GH * HD), BF),
        in_specs=[SMEM] * 2 + [VMEM] * 7,
        out_specs=VMEM,
        scratch_shapes=[
            pltpu.VMEM((GROUPS, NY * NB * ANC, HD), BF),
            pltpu.VMEM((GROUPS, NY * NB * ANC, HD), BF),
        ],
        compiler_params=params(),
        cost_estimate=pl.CostEstimate(flops=3 * 10**9, bytes_accessed=4 * 10**6, transcendentals=3 * 10**6),
        name="context",
    )(bos, lens, cq, ck, cv, *anchors)
    parent = pl.pallas_call(
        combine_kernel,
        out_shape=jax.ShapeDtypeStruct((1, NH * GH * HD), BF),
        in_specs=[VMEM],
        out_specs=VMEM,
        compiler_params=params(),
        name="combine",
    )(back)
    return context, parent


def solution(mesh):
    fine = Mesh(mesh.devices.reshape(NX, NZ, NY, NL, NC), ("xh", "z", "y", "xl", "c"))
    blk, head = ("xh", "z", "y"), ("xl", "c")
    both = P(blk, head)
    return jax.shard_map(
        on_device,
        mesh=fine,
        in_specs=(both,) * 6 + (P(), P(), P()),
        out_specs=(both, P(blk + head, None)),
        check_vma=False,
    )
```

time: 1460 us -> 71.4 us (0.05)
  blocking collectives: 907 us -> 0 us
  waiting for transfers between devices: 413 us -> 25.7 us
  local copies, waits for them, and re-layouts: 34.8 us -> 5.78 us
  starting transfers between devices: 49.7 us -> 27.3 us
  matrix products: 18.9 us -> 0 us
  other arithmetic: 18.3 us -> 0.78 us
  between operations: 15.6 us -> 0.77 us
    unnamed x3 -> x0, waiting for transfers between devices: 412 us -> none
    all_gather x2 -> x0, blocking collectives: 310 us -> none  [the longest x1 161 us: on_device(): lax.all_gather(anchor_k, 'blk', axis=0, tiled=True)]
    unnamed x1 -> x0, blocking collectives: 299 us -> none
    pmax x1 -> x0, blocking collectives: 298 us -> none  [on_device(): peak = lax.pmax(part[0], 'blk')]
    all_to_all x1 -> x2, starting transfers between devices: 49.6 us -> 20 us  [the longest x1 11.6 us: on_device(): got = lax.all_to_all(send, ('xh', 'z'), 0, 0, tiled=True)]
    ppermute x0 -> x6, waiting for transfers between devices: none -> 23.5 us  [turn(): return lax.ppermute(x, 'y', [(i, (i + shift) % NY) for i in range(NY)])]
    dot_general x20 -> x0, matrix products: 18.9 us -> none  [the longest x10 12.7 us: partial_attend(): jnp.einsum('gqk,gkd->gqd', expo.astype(jnp.bfloat16), vals_t, preferred_e...]
    dynamic_slice x37 -> x0, local copies, waits for them, and re-layouts: 17.9 us -> none  [the longest x18 8.85 us: key_block(): values = lax.dynamic_slice_in_dim(vals_all, start, step_keys, 0)]
  transfers between devices with their start and end apart: 3 -> 8, of which waited for: 2 -> 7; matrix products, arithmetic and copies ran while one was open for 4% -> 0% of each run, Pallas kernels for 0% -> 9%
where the time goes in v1:
time: 71.4 us; the launch traced here: 70.9 us
  starting transfers between devices  27.3 us (38%)
  waiting for transfers between devices  25.7 us (36%)
  Pallas kernels  10.6 us (15%)
  local copies, waits for them, and re-layouts  5.78 us (8%)
  other arithmetic  0.78 us (1%)
  between operations  0.77 us (1%)
    ppermute x6, waiting for transfers between devices, turn(): return lax.ppermute(x, 'y', [(i, (i + shift) % NY) for i in range(NY)])  23.5 us
    all_to_all x1, starting transfers between devices, on_device(): got = lax.all_to_all(send, ('xh', 'z'), 0, 0, tiled=True)  11.6 us
    all_to_all x1, starting transfers between devices, on_device(): back = lax.all_to_all(packed, ('xh', 'z', 'xl', 'c'), 0, 0, tiled=True)  8.44 us
    ppermute x6, starting transfers between devices, turn(): return lax.ppermute(x, 'y', [(i, (i + shift) % NY) for i in range(NY)])  7.3 us
    pallas_call x1, Pallas kernels, on_device(): pl.pallas_call(context_kernel, out_shape=jax.ShapeDtypeStruct((TOK, GH *...  6.13 us
    unnamed x26, local copies, waits for them, and re-layouts  5.24 us
    pallas_call x1, Pallas kernels, on_device(): pl.pallas_call(parent_kernel, out_shape=(jax.ShapeDtypeStruct((NB * QR, G...  2.59 us
    all_to_all x1, waiting for transfers between devices, on_device(): got = lax.all_to_all(send, ('xh', 'z'), 0, 0, tiled=True)  2.2 us
  transfers between devices with their start and end apart: 8, of which 7 were waited for; matrix products, arithmetic and copies ran while one was open for 0% of the time, Pallas kernels for 9%

profile of v1, /device:TPU:1, one launch (start us, length us, event | category | flops | bytes accessed | tf_op | source)
XLA Modules:
  0.0 70.9 jit_solution(2030318238798749291)
XLA Ops:
  0.6 0.0 copy-start
  0.6 0.8 %copy-done = bf16[128,256]{1,0:T(8,128)(2,1)S(1)} copy-done((bf16[128,256]{1,0:T(8,128)(2,1)S(1)}, bf16[128,256]{1,0:T(8,128)(2,1)}, u32[]{:S(2)}) %copy-start) | copy-done | bytes 65560
  1.5 0.8 %copy-done.2 = bf16[128,256]{1,0:T(8,128)(2,1)S(1)} copy-done((bf16[128,256]{1,0:T(8,128)(2,1)S(1)}, bf16[128,256]{1,0:T(8,128)(2,1)}, u32[]{:S(2)}) %copy-start.2) | copy-done | bytes 65560
  2.3 0.7 %copy-done.4 = bf16[4,2048]{1,0:T(4,128)(2,1)S(1)} copy-done((bf16[4,2048]{1,0:T(4,128)(2,1)S(1)}, bf16[4,2048]{1,0:T(4,128)(2,1)}, u32[]{:S(2)}) %copy-start.4) | copy-done | bytes 16408
  3.0 0.7 copy-done.5
  3.7 0.7 copy-done.6
  4.4 0.9 %prep.1 = (bf16[16,128,128]{2,1,0:T(8,128)(2,1)}, bf16[4,144,128]{2,1,0:T(8,128)(2,1)S(1)}) custom-call(bf16[16,256]{1,0:T(8,128)(2,1)S(1)} %copy-done.5, bf16[16,256]{1,0:T(8,128)(2,1)S(1)} %copy-done.6, bf16[4,2048]{1,0:T(4,128)(2,1)S(1)} %copy-done.4, bf16[128,256]{1,0:T(8,128)(2,1)S(1)} %copy-done, bf16[128,256]{1,0:T(8,128)(2,1)S(1)} %copy-done.2), custom_call_target="tpu_custom_call" | custom-call | tf_op jit(solution)/shard_map/prep/pallas_call | solution.py:167
  5.3 11.6 %all-to-all-start = ((bf16[16,128,128]{2,1,0:T(8,128)(2,1)}), bf16[16,128,128]{2,1,0:T(8,128)(2,1)S(1)}, u32[]{:S(2)}, u32[]{:S(2)}) async-start(bf16[16,128,128]{2,1,0:T(8,128)(2,1)} %get-tuple-element.6), calls=%async_computation | async-start | bytes 1048576 | tf_op jit(solution)/shard_map/all_to_all | solution.py:184
  16.9 0.0 copy-start.9
  16.9 2.8 %collective-permute-start.5 = (bf16[4,144,128]{2,1,0:T(8,128)(2,1)S(1)}, bf16[4,144,128]{2,1,0:T(8,128)(2,1)S(1)}, u32[]{:S(2)}, u32[]{:S(2)}) collective-permute-start(bf16[4,144,128]{2,1,0:T(8,128)(2,1)S(1)} %get-tuple-element.7.kv0), channel_id=1, source_target_pairs={{0,12},{4,0},{8,4},{12,8},{1,13},{5,1},{9,5},{13,9},{2,14},{6,2},{... | collective-permute-start | bytes 442376 | tf_op jit(solution)/shard_map/ppermute | solution.py:181
  19.8 0.3 collective-permute-start.4
  20.1 0.7 collective-permute-start.3
  20.8 4.5 %collective-permute-done.5.kv3 = bf16[4,144,128]{2,1,0:T(8,128)(2,1)S(1)} collective-permute-done((bf16[4,144,128]{2,1,0:T(8,128)(2,1)S(1)}, bf16[4,144,128]{2,1,0:T(8,128)(2,1)S(1)}, u32[]{:S(2)}, u32[]{:S(2)}) %collective-permute-start.5) | collective-permute-done | bytes 147488 | tf_op jit(solution)/shard_map/ppermute | solution.py:181
  25.3 0.2 collective-permute-done.4.kv2
  25.6 4.4 %collective-permute-done.3.kv1 = bf16[4,144,128]{2,1,0:T(8,128)(2,1)S(1)} collective-permute-done((bf16[4,144,128]{2,1,0:T(8,128)(2,1)S(1)}, bf16[4,144,128]{2,1,0:T(8,128)(2,1)S(1)}, u32[]{:S(2)}, u32[]{:S(2)}) %collective-permute-start.3) | collective-permute-done | bytes 147488 | tf_op jit(solution)/shard_map/ppermute | solution.py:181
  30.0 2.2 %all-to-all-done.got = bf16[16,128,128]{2,1,0:T(8,128)(2,1)S(1)} async-done(((bf16[16,128,128]{2,1,0:T(8,128)(2,1)}), bf16[16,128,128]{2,1,0:T(8,128)(2,1)S(1)}, u32[]{:S(2)}, u32[]{:S(2)}) %all-to-all-start) | async-done | bytes 524320 | tf_op jit(solution)/shard_map/all_to_all | solution.py:184
  32.2 2.6 %parent.1 = (bf16[64,16,128]{2,1,0:T(8,128)(2,1)S(1)}, bf16[64,128]{1,0:T(8,128)(2,1)S(1)}) custom-call(s32[64]{0:T(128)S(1)} %copy-done.9, s32[256]{0:T(256)S(1)} %copy-done.8, bf16[16,128,128]{2,1,0:T(8,128)(2,1)S(1)} %all-to-all-done.got, bf16[4,144,128]{2,1,0:T(8,128)(2,1)S(1)} %get-tuple-element.7.kv0, ...), custom_call_target="tpu_custom_call" | custom-call | flops 1000000000 | bytes 2000000 | tf_op jit(solution)/shard_map/parent/pallas_call | solution.py:187
  34.8 0.1 copy.17
  34.9 0.5 broadcast
  35.4 0.8 %reduce = bf16[64,2176]{1,0:T(8,128)(2,1)S(1)} reduce(bf16[64,1,2176]{2,0,1:T(8,128)(2,1)S(1)} %maximum_bitcast_fusion, bf16[]{:T(256)} %broadcast), dimensions={1}, to_apply=%copy.11.reduce_sub_computation | reduce | bytes 557058 | tf_op jit(solution)/shard_map/all_to_all | solution.py:205
  36.2 1.0 %reshape.10 = bf16[64,2,1088]{2,1,0:T(2,128)(2,1)} reshape(bf16[64,2176]{1,0:T(8,128)(2,1)S(1)} %reduce) | data formatting | bytes 557056
  37.2 8.4 %all-to-all-start.1 = ((bf16[64,2,1088]{2,1,0:T(2,128)(2,1)}), bf16[64,2,1088]{2,1,0:T(2,128)(2,1)S(1)}, u32[]{:S(2)}, u32[]{:S(2)}) async-start(bf16[64,2,1088]{2,1,0:T(2,128)(2,1)} %reshape.10), calls=%async_computation.1 | async-start | bytes 589824 | tf_op jit(solution)/shard_map/all_to_all | solution.py:205
  45.6 0.0 copy-start.1
  45.7 2.4 %collective-permute-start.2 = (bf16[16,64,128]{2,1,0:T(8,128)(2,1)S(1)}, bf16[16,64,128]{2,1,0:T(8,128)(2,1)S(1)}, u32[]{:S(2)}, u32[]{:S(2)}) collective-permute-start(bf16[16,64,128]{2,1,0:T(8,128)(2,1)S(1)} %slice.4.a0), channel_id=1, source_target_pairs={{0,12},{4,0},{8,4},{12,8},{1,13},{5,1},{9,5},{13,9},{2,14},{6,2},{... | collective-permute-start | bytes 786440 | tf_op jit(solution)/shard_map/ppermute | solution.py:181
  48.1 0.3 collective-permute-start.1
  48.4 0.7 collective-permute-start
  49.1 4.8 %collective-permute-done.2.a3 = bf16[16,64,128]{2,1,0:T(8,128)(2,1)S(1)} collective-permute-done((bf16[16,64,128]{2,1,0:T(8,128)(2,1)S(1)}, bf16[16,64,128]{2,1,0:T(8,128)(2,1)S(1)}, u32[]{:S(2)}, u32[]{:S(2)}) %collective-permute-start.2) | collective-permute-done | bytes 262176 | tf_op jit(solution)/shard_map/ppermute | solution.py:181
  53.9 2.8 %collective-permute-done.1.a2 = bf16[16,64,128]{2,1,0:T(8,128)(2,1)S(1)} collective-permute-done((bf16[16,64,128]{2,1,0:T(8,128)(2,1)S(1)}, bf16[16,64,128]{2,1,0:T(8,128)(2,1)S(1)}, u32[]{:S(2)}, u32[]{:S(2)}) %collective-permute-start.1) | collective-permute-done | bytes 262176 | tf_op jit(solution)/shard_map/ppermute | solution.py:181
  56.7 6.7 %collective-permute-done.a1 = bf16[16,64,128]{2,1,0:T(8,128)(2,1)S(1)} collective-permute-done((bf16[16,64,128]{2,1,0:T(8,128)(2,1)S(1)}, bf16[16,64,128]{2,1,0:T(8,128)(2,1)S(1)}, u32[]{:S(2)}, u32[]{:S(2)}) %collective-permute-start) | collective-permute-done | bytes 262176 | tf_op jit(solution)/shard_map/ppermute | solution.py:181
  63.4 6.1 %context.1 = bf16[128,2048]{1,0:T(8,128)(2,1)} custom-call(s32[64]{0:T(128)S(1)} %copy-done.9, s32[8]{0:T(128)S(1)} %copy-done.10, bf16[128,2048]{1,0:T(8,128)(2,1)S(1)} %copy-done.7, bf16[128,256]{1,0:T(8,128)(2,1)S(1)} %copy-done.1, bf16[128,256]{1,0:T(8,128)(2,1)S(1)} %copy-done.3, bf16[16,64,128]{2,1,0:T(8,128)(2,1)S(1)} %slice.4.a0, ...), custom_call_target="tpu_custom_call" | custom-call | flops 3000000000 | bytes 4000000 | tf_op jit(solution)/shard_map/context/pallas_call | solution.py:206
  69.6 0.3 reshape.11
  69.9 1.0 %combine.1 = bf16[1,8192]{1,0:T(2,128)(2,1)} custom-call(bf16[64,2176]{1,0:T(8,128)(2,1)S(1)} %bitcast.9), custom_call_target="tpu_custom_call" | custom-call | tf_op jit(solution)/shard_map/combine/pallas_call | solution.py:219
  (18 shorter events, 0.1 us)
Async XLA Ops:
  0.6 0.8 %copy-start = (bf16[128,256]{1,0:T(8,128)(2,1)S(1)}, bf16[128,256]{1,0:T(8,128)(2,1)}, u32[]{:S(2)}) copy-start(bf16[128,256]{1,0:T(8,128)(2,1)} %ck.3) | copy-start | bytes 196612
  1.5 0.8 %copy-start.2 = (bf16[128,256]{1,0:T(8,128)(2,1)S(1)}, bf16[128,256]{1,0:T(8,128)(2,1)}, u32[]{:S(2)}) copy-start(bf16[128,256]{1,0:T(8,128)(2,1)} %cv.3) | copy-start | bytes 196612
  2.3 0.7 %copy-start.4 = (bf16[4,2048]{1,0:T(4,128)(2,1)S(1)}, bf16[4,2048]{1,0:T(4,128)(2,1)}, u32[]{:S(2)}) copy-start(bf16[4,2048]{1,0:T(4,128)(2,1)} %pq.1) | copy-start | bytes 49156
  3.0 0.7 copy-start.5
  3.7 0.7 copy-start.6
  5.3 26.8 %all-to-all-start = ((bf16[16,128,128]{2,1,0:T(8,128)(2,1)}), bf16[16,128,128]{2,1,0:T(8,128)(2,1)S(1)}, u32[]{:S(2)}, u32[]{:S(2)}) async-start(bf16[16,128,128]{2,1,0:T(8,128)(2,1)} %get-tuple-element.6), calls=%async_computation | async-start | bytes 1048576 | tf_op jit(solution)/shard_map/all_to_all | solution.py:184
  16.9 15.2 %copy-start.8 = (s32[256]{0:T(256)S(1)}, s32[256]{0:T(256)}, u32[]{:S(2)}) copy-start(s32[256]{0:T(256)} %qp.1) | copy-start | bytes 3076
  16.9 15.2 %copy-start.9 = (s32[64]{0:T(128)S(1)}, s32[64]{0:T(128)}, u32[]{:S(2)}) copy-start(s32[64]{0:T(128)} %bos.3) | copy-start | bytes 772
  16.9 8.4 %collective-permute-start.5 = (bf16[4,144,128]{2,1,0:T(8,128)(2,1)S(1)}, bf16[4,144,128]{2,1,0:T(8,128)(2,1)S(1)}, u32[]{:S(2)}, u32[]{:S(2)}) collective-permute-start(bf16[4,144,128]{2,1,0:T(8,128)(2,1)S(1)} %get-tuple-element.7.kv0), channel_id=1, source_target_pairs={{0,12},{4,0},{8,4},{12,8},{1,13},{5,1},{9,5},{13,9},{2,14},{6,2},{... | collective-permute-start | bytes 442376 | tf_op jit(solution)/shard_map/ppermute | solution.py:181
  19.8 5.8 %collective-permute-start.4 = (bf16[4,144,128]{2,1,0:T(8,128)(2,1)S(1)}, bf16[4,144,128]{2,1,0:T(8,128)(2,1)S(1)}, u32[]{:S(2)}, u32[]{:S(2)}) collective-permute-start(bf16[4,144,128]{2,1,0:T(8,128)(2,1)S(1)} %get-tuple-element.7.kv0), channel_id=1, source_target_pairs={{0,8},{4,12},{8,0},{12,4},{1,9},{5,13},{9,1},{13,5},{2,10},{6,14},... | collective-permute-start | bytes 442376 | tf_op jit(solution)/shard_map/ppermute | solution.py:181
  20.1 9.9 %collective-permute-start.3 = (bf16[4,144,128]{2,1,0:T(8,128)(2,1)S(1)}, bf16[4,144,128]{2,1,0:T(8,128)(2,1)S(1)}, u32[]{:S(2)}, u32[]{:S(2)}) collective-permute-start(bf16[4,144,128]{2,1,0:T(8,128)(2,1)S(1)} %get-tuple-element.7.kv0), channel_id=1, source_target_pairs={{0,4},{4,8},{8,12},{12,0},{1,5},{5,9},{9,13},{13,1},{2,6},{6,10},{... | collective-permute-start | bytes 442376 | tf_op jit(solution)/shard_map/ppermute | solution.py:181
  37.1 26.3 %copy-start.7 = (bf16[128,2048]{1,0:T(8,128)(2,1)S(1)}, bf16[128,2048]{1,0:T(8,128)(2,1)}, u32[]{:S(2)}) copy-start(bf16[128,2048]{1,0:T(8,128)(2,1)} %q_ref.1) | copy-start | bytes 1572868
  37.2 32.4 %all-to-all-start.1 = ((bf16[64,2,1088]{2,1,0:T(2,128)(2,1)}), bf16[64,2,1088]{2,1,0:T(2,128)(2,1)S(1)}, u32[]{:S(2)}, u32[]{:S(2)}) async-start(bf16[64,2,1088]{2,1,0:T(2,128)(2,1)} %reshape.10), calls=%async_computation.1 | async-start | bytes 589824 | tf_op jit(solution)/shard_map/all_to_all | solution.py:205
  45.6 17.8 %copy-start.1 = (bf16[128,256]{1,0:T(8,128)(2,1)S(1)}, bf16[128,256]{1,0:T(8,128)(2,1)}, u32[]{:S(2)}) copy-start(bf16[128,256]{1,0:T(8,128)(2,1)} %ck.3) | copy-start | bytes 196612
  45.6 17.8 %copy-start.3 = (bf16[128,256]{1,0:T(8,128)(2,1)S(1)}, bf16[128,256]{1,0:T(8,128)(2,1)}, u32[]{:S(2)}) copy-start(bf16[128,256]{1,0:T(8,128)(2,1)} %cv.3) | copy-start | bytes 196612
  45.6 17.8 %copy-start.10 = (s32[8]{0:T(128)S(1)}, s32[8]{0:T(128)}, u32[]{:S(2)}) copy-start(s32[8]{0:T(128)} %lens.1) | copy-start | bytes 100
  45.7 8.3 %collective-permute-start.2 = (bf16[16,64,128]{2,1,0:T(8,128)(2,1)S(1)}, bf16[16,64,128]{2,1,0:T(8,128)(2,1)S(1)}, u32[]{:S(2)}, u32[]{:S(2)}) collective-permute-start(bf16[16,64,128]{2,1,0:T(8,128)(2,1)S(1)} %slice.4.a0), channel_id=1, source_target_pairs={{0,12},{4,0},{8,4},{12,8},{1,13},{5,1},{9,5},{13,9},{2,14},{6,2},{... | collective-permute-start | bytes 786440 | tf_op jit(solution)/shard_map/ppermute | solution.py:181
  48.1 8.7 %collective-permute-start.1 = (bf16[16,64,128]{2,1,0:T(8,128)(2,1)S(1)}, bf16[16,64,128]{2,1,0:T(8,128)(2,1)S(1)}, u32[]{:S(2)}, u32[]{:S(2)}) collective-permute-start(bf16[16,64,128]{2,1,0:T(8,128)(2,1)S(1)} %slice.4.a0), channel_id=1, source_target_pairs={{0,8},{4,12},{8,0},{12,4},{1,9},{5,13},{9,1},{13,5},{2,10},{6,14},... | collective-permute-start | bytes 786440 | tf_op jit(solution)/shard_map/ppermute | solution.py:181
  48.4 15.0 %collective-permute-start = (bf16[16,64,128]{2,1,0:T(8,128)(2,1)S(1)}, bf16[16,64,128]{2,1,0:T(8,128)(2,1)S(1)}, u32[]{:S(2)}, u32[]{:S(2)}) collective-permute-start(bf16[16,64,128]{2,1,0:T(8,128)(2,1)S(1)} %slice.4.a0), channel_id=1, source_target_pairs={{0,4},{4,8},{8,12},{12,0},{1,5},{5,9},{9,13},{13,1},{2,6},{6,10},{... | collective-permute-start | bytes 786440 | tf_op jit(solution)/shard_map/ppermute | solution.py:181

commit v2 on v1

--- a/solution.py
+++ b/solution.py
@@ -23,15 +23,16 @@
 KEYS = 640
 STRIDE = 4 * ANC
 LOG2E = 1.4426950408889634
+WIDE = PER * HD + HD
 SCALE = LOG2E / math.sqrt(HD)
 BF = jnp.bfloat16
 F32 = jnp.float32
-VMEM = pl.BlockSpec(memory_space=pltpu.VMEM)
+VMEM = pl.BlockSpec()
 SMEM = pl.BlockSpec(memory_space=pltpu.SMEM)
 
 
-def params():
-    return pltpu.CompilerParams(vmem_limit_bytes=40 * 1024 * 1024)
+def params(mib=40):
+    return pltpu.CompilerParams(vmem_limit_bytes=mib * 1024 * 1024)
 
 
 def nt(a, b):
@@ -56,7 +57,7 @@
         kv[i, TOK:, :] = parts[i]
 
 
-def parent_kernel(bos, qp, got, kv0, kv1, kv2, kv3, out, stat, keys, vals, qpos):
+def parent_kernel(bos, qp, got, kv0, kv1, kv2, kv3, out, keys, vals, qpos, turned):
     slot = (lax.axis_index("xh") * NZ + lax.axis_index("z")) * NY
     y = lax.axis_index("y")
     blocks = [kv0, kv1, kv2, kv3]
@@ -74,38 +75,39 @@
         for r in range(QR):
             row = (b * QR + r) * PER
             qpos[row : row + PER, :] = jnp.full((PER, HD), qp[(b * NY + y) * QR + r], jnp.int32)
-    lane = lax.broadcasted_iota(jnp.int32, (1, KEYS), 1)
-    kpos = jnp.where(lane < NY * KVR, -1, 1 << 30)
+    rows = NB * QR * PER
+    lane = lax.broadcasted_iota(jnp.int32, (rows, HD), 1)
+    masks = []
     for i in range(NY):
-        src = slot + lax.rem(y + NY - i, NY)
-        base = bos[src] * TOK - i * TOK
-        kpos = jnp.where((lane >= i * TOK) & (lane < (i + 1) * TOK), lane + base, kpos)
-    visible = kpos < qpos[:, :1]
-    rows = NB * QR * PER
-    parts, stats = [], jnp.zeros((NB * QR, HD), F32)
-    lanes = lax.broadcasted_iota(jnp.int32, (1, PER, HD), 2)
-    heads = lax.broadcasted_iota(jnp.int32, (1, PER, HD), 1)
+        base = bos[slot + lax.rem(y + NY - i, NY)] * TOK
+        masks.append(lane + base < qpos[...])
+    masks.append(lane < NY * ANC)
+    stats = jnp.zeros((NB * QR, HD), F32)
+    lanes = lax.broadcasted_iota(jnp.int32, (NB * QR, HD), 1)
     for g in range(GROUPS):
         lo = STRIDE + g * QR * PER
         q = got[:, lo : lo + QR * PER, :].reshape(rows, HD)
-        s = nt(q, keys[g]) * SCALE
-        s = jnp.where(visible, s, -1e30)
-        m = jnp.max(s, axis=1, keepdims=True)
-        p = jnp.exp2(s - m)
-        total = jnp.sum(p, axis=1, keepdims=True)
-        o = jnp.dot(p.astype(BF), vals[g], preferred_element_type=F32)
-        o = o / total
-        parts.append(o.reshape(NB * QR, PER, HD))
-        lse = m + jnp.log2(total)
-        hi = lse.astype(BF).astype(F32)
-        mid = (lse - hi).astype(BF).astype(F32)
-        low = lse - hi - mid
-        pick = lanes - g * PER
-        for k, part in enumerate((hi, mid, low)):
-            wide = jnp.broadcast_to(part, (rows, HD)).reshape(NB * QR, PER, HD)
-            stats = stats + jnp.sum(jnp.where(pick - k * GH == heads, wide, 0.0), axis=1)
-    out[...] = jnp.concatenate(parts, 1).astype(BF)
-    stat[...] = stats.astype(BF)
+        s = nt(q, keys[g])
+        s = [jnp.where(v, s[:, i * HD : (i + 1) * HD] * SCALE, -1e30) for i, v in enumerate(masks)]
+        m = jnp.max(functools.reduce(jnp.maximum, s), axis=1, keepdims=True)
+        p = [jnp.exp2(x - m) for x in s]
+        total = jnp.sum(sum(p[1:], p[0]), axis=1, keepdims=True)
+        p = jnp.concatenate([x.astype(BF) for x in p], 1)
+        o = jnp.dot(p, vals[g], preferred_element_type=F32)
+        turned[0] = o * (1.0 / total)
+        turned[1] = jnp.broadcast_to(m + jnp.log2(total), (rows, HD))
+        for h in range(PER):
+            col = g * PER + h
+            at = g * WIDE + h * HD
+            pick = pl.ds(h, NB * QR, stride=PER)
+            out[:, at : at + HD] = turned[0, pick, :].astype(BF)
+            stats = jnp.where(lanes == col, turned[1, pick, :], stats)
+    hi = stats.astype(BF).astype(F32)
+    mid = (stats - hi).astype(BF).astype(F32)
+    low = stats - hi - mid
+    stats = hi + pltpu.roll(mid, GH, 1) + pltpu.roll(low, 2 * GH, 1)
+    for g in range(GROUPS):
+        out[:, g * WIDE + PER * HD : (g + 1) * WIDE] = stats.astype(BF)
 
 
 def context_kernel(bos, lens, q_ref, ck, cv, a0, a1, a2, a3, out, keys, vals):
@@ -145,7 +147,7 @@
 
 
 def combine_kernel(got, out):
-    st = got[:, GH * HD :].astype(F32)
+    st = got[:, PER * HD : WIDE].astype(F32)
     lse = st + pltpu.roll(st, HD - GH, 1) + pltpu.roll(st, HD - 2 * GH, 1)
     tiles = lse.reshape(NB * NH // 8, 8, HD)
     top = jnp.max(tiles, axis=0)
@@ -155,7 +157,8 @@
     total = total + pltpu.roll(total, 4, 0)
     w = (w / total[None]).reshape(NB * NH, HD)
     for h in range(GH):
-        x = got[:, h * HD : (h + 1) * HD].astype(F32) * w[:, h : h + 1]
+        at = h // PER * WIDE + h % PER * HD
+        x = got[:, at : at + HD].astype(F32) * w[:, h : h + 1]
         x = jnp.sum(x.reshape(NB * NH // 8, 8, HD), axis=0)
         x = x + pltpu.roll(x, 4, 0)
         for k in range(NH):
@@ -173,7 +176,7 @@
         in_specs=[VMEM] * 5,
         out_specs=(VMEM, VMEM),
         scratch_shapes=[pltpu.VMEM((STRIDE, HD), F32)],
-        compiler_params=params(),
+        compiler_params=params(60),
         name="prep",
     )(ak, av, pq, ck, cv)
 
@@ -182,27 +185,26 @@
 
     kvs = [kv] + [turn(kv, s) for s in (1, 2, 3)]
     got = lax.all_to_all(send, ("xh", "z"), 0, 0, tiled=True)
+    got, *kvs = lax.optimization_barrier((got, *kvs))
     anchors = got[:, :STRIDE]
     anchors = [anchors] + [turn(anchors, s) for s in (1, 2, 3)]
-    part, stat = pl.pallas_call(
+    part = pl.pallas_call(
         parent_kernel,
-        out_shape=(
-            jax.ShapeDtypeStruct((NB * QR, GH, HD), BF),
-            jax.ShapeDtypeStruct((NB * QR, HD), BF),
-        ),
+        out_shape=jax.ShapeDtypeStruct((NB * QR, GROUPS * WIDE), BF),
         in_specs=[SMEM] * 2 + [VMEM] * 5,
-        out_specs=(VMEM, VMEM),
+        out_specs=VMEM,
         scratch_shapes=[
             pltpu.VMEM((GROUPS, KEYS, HD), BF),
             pltpu.VMEM((GROUPS, KEYS, HD), BF),
             pltpu.VMEM((NB * QR * PER, HD), jnp.int32),
+            pltpu.VMEM((2, NB * QR * PER, HD), F32),
         ],
         compiler_params=params(),
         cost_estimate=pl.CostEstimate(flops=10**9, bytes_accessed=2 * 10**6, transcendentals=10**6),
         name="parent",
     )(bos, qp, got, *kvs)
-    packed = jnp.concatenate([part.reshape(NB * QR, GH * HD), stat], 1)
-    back = lax.all_to_all(packed, ("xh", "z", "xl", "c"), 0, 0, tiled=True)
+    part = part.reshape(NB * QR, GROUPS, WIDE)
+    back = lax.all_to_all(part, ("xh", "z", "xl", "c"), 0, 0, tiled=True)
     context = pl.pallas_call(
         context_kernel,
         out_shape=jax.ShapeDtypeStruct((TOK, GH * HD), BF),
@@ -213,7 +215,7 @@
             pltpu.VMEM((GROUPS, NY * NB * ANC, HD), BF),
         ],
         compiler_params=params(),
-        cost_estimate=pl.CostEstimate(flops=3 * 10**9, bytes_accessed=4 * 10**6, transcendentals=3 * 10**6),
+        cost_estimate=pl.CostEstimate(flops=60 * 10**9, bytes_accessed=4 * 10**6, transcendentals=3 * 10**6),
         name="context",
     )(bos, lens, cq, ck, cv, *anchors)
     parent = pl.pallas_call(
@@ -223,7 +225,7 @@
         out_specs=VMEM,
         compiler_params=params(),
         name="combine",
-    )(back)
+    )(back.reshape(NB * NH, GROUPS * WIDE))
     return context, parent
 
 

time: 71.4 us -> 60.7 us (0.85)
  waiting for transfers between devices: 25.7 us -> 19.2 us
  local copies, waits for them, and re-layouts: 5.78 us -> 0.86 us
  starting transfers between devices: 27.3 us -> 28.3 us
  other arithmetic: 0.78 us -> 0 us
    ppermute x6, waiting for transfers between devices: 23.5 us -> 10.4 us  [turn(): return lax.ppermute(x, 'y', [(i, (i + shift) % NY) for i in range(NY)])]
    all_to_all x1, waiting for transfers between devices: 0.01 us -> 6.59 us  [on_device(): back = lax.all_to_all(part, ('xh', 'z', 'xl', 'c'), 0, 0, tiled=True)]
    unnamed x26 -> x15, local copies, waits for them, and re-layouts: 5.24 us -> 0.07 us
    pallas_call x1, Pallas kernels: 0.91 us -> 1.87 us  [on_device(): pl.pallas_call(prep_kernel, out_shape=(jax.ShapeDtypeStruct((NB, 2 * STRI...]
    reshape x0 -> x1, local copies, waits for them, and re-layouts: none -> 0.78 us  [on_device(): part = part.reshape(NB * QR, GROUPS, WIDE)]
    all_to_all x2 -> x0, other arithmetic: 0.78 us -> none  [on_device(): back = lax.all_to_all(packed, ('xh', 'z', 'xl', 'c'), 0, 0, tiled=True)]
  transfers between devices with their start and end apart: 8 -> 8, of which waited for: 7 -> 6; matrix products, arithmetic and copies ran while one was open for 0% -> 1% of each run, Pallas kernels for 9% -> 14%
where the time goes in v2:
time: 60.7 us; the launch traced here: 60.4 us
  starting transfers between devices  28.3 us (47%)
  waiting for transfers between devices  19.2 us (32%)
  Pallas kernels  11.3 us (19%)
  local copies, waits for them, and re-layouts  0.86 us (1%)
  between operations  0.73 us (1%)
    all_to_all x1, starting transfers between devices, on_device(): got = lax.all_to_all(send, ('xh', 'z'), 0, 0, tiled=True)  11.7 us
    ppermute x6, waiting for transfers between devices, turn(): return lax.ppermute(x, 'y', [(i, (i + shift) % NY) for i in range(NY)])  10.4 us
    all_to_all x1, starting transfers between devices, on_device(): back = lax.all_to_all(part, ('xh', 'z', 'xl', 'c'), 0, 0, tiled=True)  8.88 us
    ppermute x6, starting transfers between devices, turn(): return lax.ppermute(x, 'y', [(i, (i + shift) % NY) for i in range(NY)])  7.7 us
    all_to_all x1, waiting for transfers between devices, on_device(): back = lax.all_to_all(part, ('xh', 'z', 'xl', 'c'), 0, 0, tiled=True)  6.59 us
    pallas_call x1, Pallas kernels, on_device(): pl.pallas_call(context_kernel, out_shape=jax.ShapeDtypeStruct((TOK, GH *...  6.15 us
    pallas_call x1, Pallas kernels, on_device(): pl.pallas_call(parent_kernel, out_shape=jax.ShapeDtypeStruct((NB * QR, GR...  2.32 us
    all_to_all x1, waiting for transfers between devices, on_device(): got = lax.all_to_all(send, ('xh', 'z'), 0, 0, tiled=True)  2.19 us
  transfers between devices with their start and end apart: 8, of which 6 were waited for; matrix products, arithmetic and copies ran while one was open for 1% of the time, Pallas kernels for 14%

profile of v2, /device:TPU:1, one launch (start us, length us, event | category | flops | bytes accessed | tf_op | source)
XLA Modules:
  0.0 60.4 jit_solution(5415111479654446996)
XLA Ops:
  0.6 1.9 %prep.1 = (bf16[16,128,128]{2,1,0:T(8,128)(2,1)}, bf16[4,144,128]{2,1,0:T(8,128)(2,1)}) custom-call(bf16[16,256]{1,0:T(8,128)(2,1)} %ak.1, bf16[16,256]{1,0:T(8,128)(2,1)} %av.1, bf16[4,2048]{1,0:T(4,128)(2,1)} %pq.1, bf16[128,256]{1,0:T(8,128)(2,1)} %ck.3, bf16[128,256]{1,0:T(8,128)(2,1)} %cv.3), custom_call_target="tpu_custom_call" | custom-call | tf_op jit(solution)/shard_map/prep/pallas_call | solution.py:170
  2.5 0.0 copy-start.3
  2.5 11.7 %all-to-all-start = ((bf16[16,128,128]{2,1,0:T(8,128)(2,1)}), bf16[16,128,128]{2,1,0:T(8,128)(2,1)S(1)}, u32[]{:S(2)}, u32[]{:S(2)}) async-start(bf16[16,128,128]{2,1,0:T(8,128)(2,1)} %get-tuple-element.9), calls=%async_computation | async-start | bytes 1048576 | tf_op jit(solution)/shard_map/all_to_all | solution.py:187
  14.2 0.0 copy-done.3
  14.2 0.0 copy-start.4
  14.2 0.0 copy-start.5
  14.3 2.8 %collective-permute-start.2 = (bf16[4,144,128]{2,1,0:T(8,128)(2,1)S(1)}, bf16[4,144,128]{2,1,0:T(8,128)(2,1)S(1)}, u32[]{:S(2)}, u32[]{:S(2)}) collective-permute-start(bf16[4,144,128]{2,1,0:T(8,128)(2,1)S(1)} %copy-done.3), channel_id=1, source_target_pairs={{0,12},{4,0},{8,4},{12,8},{1,13},{5,1},{9,5},{13,9},{2,14},{6,2},{... | collective-permute-start | bytes 442376 | tf_op jit(solution)/shard_map/ppermute | solution.py:184
  17.1 0.3 collective-permute-start.1
  17.4 0.7 %collective-permute-start = (bf16[4,144,128]{2,1,0:T(8,128)(2,1)S(1)}, bf16[4,144,128]{2,1,0:T(8,128)(2,1)S(1)}, u32[]{:S(2)}, u32[]{:S(2)}) collective-permute-start(bf16[4,144,128]{2,1,0:T(8,128)(2,1)S(1)} %copy-done.3), channel_id=1, source_target_pairs={{0,4},{4,8},{8,12},{12,0},{1,5},{5,9},{9,13},{13,1},{2,6},{6,10},{... | collective-permute-start | bytes 442376 | tf_op jit(solution)/shard_map/ppermute | solution.py:184
  18.1 4.5 %collective-permute-done.2.kv3 = bf16[4,144,128]{2,1,0:T(8,128)(2,1)S(1)} collective-permute-done((bf16[4,144,128]{2,1,0:T(8,128)(2,1)S(1)}, bf16[4,144,128]{2,1,0:T(8,128)(2,1)S(1)}, u32[]{:S(2)}, u32[]{:S(2)}) %collective-permute-start.2) | collective-permute-done | bytes 147488 | tf_op jit(solution)/shard_map/ppermute | solution.py:184
  22.6 0.2 collective-permute-done.1.kv2
  22.9 4.4 %collective-permute-done.kv1 = bf16[4,144,128]{2,1,0:T(8,128)(2,1)S(1)} collective-permute-done((bf16[4,144,128]{2,1,0:T(8,128)(2,1)S(1)}, bf16[4,144,128]{2,1,0:T(8,128)(2,1)S(1)}, u32[]{:S(2)}, u32[]{:S(2)}) %collective-permute-start) | collective-permute-done | bytes 147488 | tf_op jit(solution)/shard_map/ppermute | solution.py:184
  27.3 2.2 %all-to-all-done.got = bf16[16,128,128]{2,1,0:T(8,128)(2,1)S(1)} async-done(((bf16[16,128,128]{2,1,0:T(8,128)(2,1)}), bf16[16,128,128]{2,1,0:T(8,128)(2,1)S(1)}, u32[]{:S(2)}, u32[]{:S(2)}) %all-to-all-start) | async-done | bytes 524320 | tf_op jit(solution)/shard_map/all_to_all | solution.py:187
  29.5 2.8 %collective-permute-start.5 = (bf16[16,64,128]{2,1,0:T(8,128)(2,1)S(1)}, bf16[16,64,128]{2,1,0:T(8,128)(2,1)S(1)}, u32[]{:S(2)}, u32[]{:S(2)}) collective-permute-start(bf16[16,64,128]{2,1,0:T(8,128)(2,1)S(1)} %slice.3.a0), channel_id=1, source_target_pairs={{0,12},{4,0},{8,4},{12,8},{1,13},{5,1},{9,5},{13,9},{2,14},{6,2},{... | collective-permute-start | bytes 786440 | tf_op jit(solution)/shard_map/ppermute | solution.py:184
  32.3 0.3 collective-permute-start.4
  32.7 0.7 %collective-permute-start.3 = (bf16[16,64,128]{2,1,0:T(8,128)(2,1)S(1)}, bf16[16,64,128]{2,1,0:T(8,128)(2,1)S(1)}, u32[]{:S(2)}, u32[]{:S(2)}) collective-permute-start(bf16[16,64,128]{2,1,0:T(8,128)(2,1)S(1)} %slice.3.a0), channel_id=1, source_target_pairs={{0,4},{4,8},{8,12},{12,0},{1,5},{5,9},{9,13},{13,1},{2,6},{6,10},{... | collective-permute-start | bytes 786440 | tf_op jit(solution)/shard_map/ppermute | solution.py:184
  33.3 0.0 copy-done.4
  33.4 0.0 copy-done.5
  33.4 2.3 %parent.1 = bf16[64,2304]{1,0:T(8,128)(2,1)S(1)} custom-call(s32[64]{0:T(128)S(1)} %copy-done.5, s32[256]{0:T(256)S(1)} %copy-done.4, bf16[16,128,128]{2,1,0:T(8,128)(2,1)S(1)} %all-to-all-done.got, bf16[4,144,128]{2,1,0:T(8,128)(2,1)S(1)} %copy-done.3, bf16[4,144,128]{2,1,0:T(8,128)(2,1)S(1)} %collective-permute-done.kv1, ...), custom_call_target="tpu_custom_call" | custom-call | flops 1000000000 | bytes 2000000 | tf_op jit(solution)/shard_map/parent/pallas_call | solution.py:191
  35.7 0.0 copy-start.2
  35.7 0.8 %reshape.10 = bf16[64,2,1152]{2,1,0:T(2,128)(2,1)} reshape(bf16[64,2304]{1,0:T(8,128)(2,1)S(1)} %parent.1) | data formatting | bytes 589824 | tf_op jit(solution)/shard_map/reshape | solution.py:206
  36.5 8.9 %all-to-all-start.1 = ((bf16[64,2,1152]{2,1,0:T(2,128)(2,1)}), bf16[64,2,1152]{2,1,0:T(2,128)(2,1)S(1)}, u32[]{:S(2)}, u32[]{:S(2)}) async-start(bf16[64,2,1152]{2,1,0:T(2,128)(2,1)} %reshape.10), calls=%async_computation.1 | async-start | bytes 589824 | tf_op jit(solution)/shard_map/all_to_all | solution.py:207
  45.4 0.0 collective-permute-done.5.a3
  45.4 0.0 collective-permute-done.4.a2
  45.4 1.3 %collective-permute-done.3.a1 = bf16[16,64,128]{2,1,0:T(8,128)(2,1)S(1)} collective-permute-done((bf16[16,64,128]{2,1,0:T(8,128)(2,1)S(1)}, bf16[16,64,128]{2,1,0:T(8,128)(2,1)S(1)}, u32[]{:S(2)}, u32[]{:S(2)}) %collective-permute-start.3) | collective-permute-done | bytes 262176 | tf_op jit(solution)/shard_map/ppermute | solution.py:184
  46.6 0.0 copy-done.2
  46.7 0.0 copy-done
  46.7 0.0 copy-done.1
  46.7 0.0 copy-done.6
  46.7 6.1 %context.1 = bf16[128,2048]{1,0:T(8,128)(2,1)} custom-call(s32[64]{0:T(128)S(1)} %copy-done.5, s32[8]{0:T(128)S(1)} %copy-done.6, bf16[128,2048]{1,0:T(8,128)(2,1)S(1)} %copy-done.2, bf16[128,256]{1,0:T(8,128)(2,1)S(1)} %copy-done, bf16[128,256]{1,0:T(8,128)(2,1)S(1)} %copy-done.1, bf16[16,64,128]{2,1,0:T(8,128)(2,1)S(1)} %slice.3.a0, ...), custom_call_target="tpu_custom_call" | custom-call | flops 60000002048 | bytes 4000000 | tf_op jit(solution)/shard_map/context/pallas_call | solution.py:208
  52.8 6.6 %all-to-all-done.1 = bf16[64,2,1152]{2,1,0:T(2,128)(2,1)S(1)} async-done(((bf16[64,2,1152]{2,1,0:T(2,128)(2,1)}), bf16[64,2,1152]{2,1,0:T(2,128)(2,1)S(1)}, u32[]{:S(2)}, u32[]{:S(2)}) %all-to-all-start.1) | async-done | bytes 294944 | tf_op jit(solution)/shard_map/all_to_all | solution.py:207
  59.4 1.0 %combine.1 = bf16[1,8192]{1,0:T(2,128)(2,1)} custom-call(bf16[64,2304]{1,0:T(8,128)(2,1)S(1)} %bitcast.2), custom_call_target="tpu_custom_call" | custom-call | tf_op jit(solution)/shard_map/combine/pallas_call | solution.py:221
  (5 shorter events, 0.1 us)
Async XLA Ops:
  2.5 11.7 %copy-start.3 = (bf16[4,144,128]{2,1,0:T(8,128)(2,1)S(1)}, bf16[4,144,128]{2,1,0:T(8,128)(2,1)}, u32[]{:S(2)}) copy-start(bf16[4,144,128]{2,1,0:T(8,128)(2,1)} %get-tuple-element.12.kv0) | copy-start | bytes 442372
  2.5 27.0 %all-to-all-start = ((bf16[16,128,128]{2,1,0:T(8,128)(2,1)}), bf16[16,128,128]{2,1,0:T(8,128)(2,1)S(1)}, u32[]{:S(2)}, u32[]{:S(2)}) async-start(bf16[16,128,128]{2,1,0:T(8,128)(2,1)} %get-tuple-element.9), calls=%async_computation | async-start | bytes 1048576 | tf_op jit(solution)/shard_map/all_to_all | solution.py:187
  14.2 19.1 %copy-start.4 = (s32[256]{0:T(256)S(1)}, s32[256]{0:T(256)}, u32[]{:S(2)}) copy-start(s32[256]{0:T(256)} %qp.1) | copy-start | bytes 3076
  14.2 19.1 %copy-start.5 = (s32[64]{0:T(128)S(1)}, s32[64]{0:T(128)}, u32[]{:S(2)}) copy-start(s32[64]{0:T(128)} %bos.3) | copy-start | bytes 772
  14.3 8.4 %collective-permute-start.2 = (bf16[4,144,128]{2,1,0:T(8,128)(2,1)S(1)}, bf16[4,144,128]{2,1,0:T(8,128)(2,1)S(1)}, u32[]{:S(2)}, u32[]{:S(2)}) collective-permute-start(bf16[4,144,128]{2,1,0:T(8,128)(2,1)S(1)} %copy-done.3), channel_id=1, source_target_pairs={{0,12},{4,0},{8,4},{12,8},{1,13},{5,1},{9,5},{13,9},{2,14},{6,2},{... | collective-permute-start | bytes 442376 | tf_op jit(solution)/shard_map/ppermute | solution.py:184
  17.1 5.8 %collective-permute-start.1 = (bf16[4,144,128]{2,1,0:T(8,128)(2,1)S(1)}, bf16[4,144,128]{2,1,0:T(8,128)(2,1)S(1)}, u32[]{:S(2)}, u32[]{:S(2)}) collective-permute-start(bf16[4,144,128]{2,1,0:T(8,128)(2,1)S(1)} %copy-done.3), channel_id=1, source_target_pairs={{0,8},{4,12},{8,0},{12,4},{1,9},{5,13},{9,1},{13,5},{2,10},{6,14},... | collective-permute-start | bytes 442376 | tf_op jit(solution)/shard_map/ppermute | solution.py:184
  17.4 9.9 %collective-permute-start = (bf16[4,144,128]{2,1,0:T(8,128)(2,1)S(1)}, bf16[4,144,128]{2,1,0:T(8,128)(2,1)S(1)}, u32[]{:S(2)}, u32[]{:S(2)}) collective-permute-start(bf16[4,144,128]{2,1,0:T(8,128)(2,1)S(1)} %copy-done.3), channel_id=1, source_target_pairs={{0,4},{4,8},{8,12},{12,0},{1,5},{5,9},{9,13},{13,1},{2,6},{6,10},{... | collective-permute-start | bytes 442376 | tf_op jit(solution)/shard_map/ppermute | solution.py:184
  29.5 15.9 %collective-permute-start.5 = (bf16[16,64,128]{2,1,0:T(8,128)(2,1)S(1)}, bf16[16,64,128]{2,1,0:T(8,128)(2,1)S(1)}, u32[]{:S(2)}, u32[]{:S(2)}) collective-permute-start(bf16[16,64,128]{2,1,0:T(8,128)(2,1)S(1)} %slice.3.a0), channel_id=1, source_target_pairs={{0,12},{4,0},{8,4},{12,8},{1,13},{5,1},{9,5},{13,9},{2,14},{6,2},{... | collective-permute-start | bytes 786440 | tf_op jit(solution)/shard_map/ppermute | solution.py:184
  32.3 13.1 %collective-permute-start.4 = (bf16[16,64,128]{2,1,0:T(8,128)(2,1)S(1)}, bf16[16,64,128]{2,1,0:T(8,128)(2,1)S(1)}, u32[]{:S(2)}, u32[]{:S(2)}) collective-permute-start(bf16[16,64,128]{2,1,0:T(8,128)(2,1)S(1)} %slice.3.a0), channel_id=1, source_target_pairs={{0,8},{4,12},{8,0},{12,4},{1,9},{5,13},{9,1},{13,5},{2,10},{6,14},... | collective-permute-start | bytes 786440 | tf_op jit(solution)/shard_map/ppermute | solution.py:184
  32.7 14.0 %collective-permute-start.3 = (bf16[16,64,128]{2,1,0:T(8,128)(2,1)S(1)}, bf16[16,64,128]{2,1,0:T(8,128)(2,1)S(1)}, u32[]{:S(2)}, u32[]{:S(2)}) collective-permute-start(bf16[16,64,128]{2,1,0:T(8,128)(2,1)S(1)} %slice.3.a0), channel_id=1, source_target_pairs={{0,4},{4,8},{8,12},{12,0},{1,5},{5,9},{9,13},{13,1},{2,6},{6,10},{... | collective-permute-start | bytes 786440 | tf_op jit(solution)/shard_map/ppermute | solution.py:184
  35.7 11.0 %copy-start.2 = (bf16[128,2048]{1,0:T(8,128)(2,1)S(1)}, bf16[128,2048]{1,0:T(8,128)(2,1)}, u32[]{:S(2)}) copy-start(bf16[128,2048]{1,0:T(8,128)(2,1)} %q_ref.1) | copy-start | bytes 1572868
  36.5 10.2 %copy-start = (bf16[128,256]{1,0:T(8,128)(2,1)S(1)}, bf16[128,256]{1,0:T(8,128)(2,1)}, u32[]{:S(2)}) copy-start(bf16[128,256]{1,0:T(8,128)(2,1)} %ck.3) | copy-start | bytes 196612
  36.5 10.2 %copy-start.1 = (bf16[128,256]{1,0:T(8,128)(2,1)S(1)}, bf16[128,256]{1,0:T(8,128)(2,1)}, u32[]{:S(2)}) copy-start(bf16[128,256]{1,0:T(8,128)(2,1)} %cv.3) | copy-start | bytes 196612
  36.5 10.2 %copy-start.6 = (s32[8]{0:T(128)S(1)}, s32[8]{0:T(128)}, u32[]{:S(2)}) copy-start(s32[8]{0:T(128)} %lens.1) | copy-start | bytes 100
  36.5 22.9 %all-to-all-start.1 = ((bf16[64,2,1152]{2,1,0:T(2,128)(2,1)}), bf16[64,2,1152]{2,1,0:T(2,128)(2,1)S(1)}, u32[]{:S(2)}, u32[]{:S(2)}) async-start(bf16[64,2,1152]{2,1,0:T(2,128)(2,1)} %reshape.10), calls=%async_computation.1 | async-start | bytes 589824 | tf_op jit(solution)/shard_map/all_to_all | solution.py:207

commit v3 on v2

v3 whole, which is shorter than its diff:
```python
import functools
import math

import jax
import jax.numpy as jnp
from jax import lax
from jax.experimental import pallas as pl
from jax.experimental.pallas import tpu as pltpu
from jax.sharding import Mesh
from jax.sharding import PartitionSpec as P

HD = 128
NX, NZ, NY, NL, NC = 2, 8, 4, 2, 2
NB = NX * NZ
NA = NX * NY
NH = NL * NC
GROUPS = 2
PER = 8
GH = GROUPS * PER
TOK = 128
ANC = 16
QR = 4
KVR = TOK + ANC
KEYS = NA * KVR
STRIDE = 4 * ANC
CHUNK = STRIDE + QR * PER
ROWS = NB * QR
LOG2E = 1.4426950408889634
WIDE = PER * HD + 2 * HD
SCALE = LOG2E / math.sqrt(HD)
BF = jnp.bfloat16
F32 = jnp.float32
VMEM = pl.BlockSpec()
SMEM = pl.BlockSpec(memory_space=pltpu.SMEM)


def params(mib=40):
    return pltpu.CompilerParams(vmem_limit_bytes=mib * 1024 * 1024)


def nt(a, b):
    return lax.dot_general(a, b, (((1,), (1,)), ((), ())), preferred_element_type=F32)


def half_kernel(ak, av, ck, cv, keep, give):
    first = lax.axis_index("xh") == 0
    for i, (ctx, anc) in enumerate(((ck, ak), (cv, av))):
        for rows, src in ((slice(0, TOK), ctx), (slice(TOK, KVR), anc)):
            low, high = src[:, :HD], src[:, HD:]
            keep[i, rows, :] = jnp.where(first, low, high)
            give[i, rows, :] = jnp.where(first, high, low)


def send_kernel(ak, av, pq, send, scr):
    q = pq[...].astype(F32)
    for g in range(GROUPS):
        for r in range(QR):
            for h in range(PER):
                col = (g * PER + h) * HD
                row = (g * QR + r) * PER + h
                scr[row : row + 1, :] = q[r : r + 1, col : col + HD]
    parts = [ak[:, :HD], ak[:, HD:], av[:, :HD], av[:, HD:]]
    for x in range(NX):
        lo = x * QR * PER
        chunk = jnp.concatenate(parts + [scr[lo : lo + QR * PER, :].astype(BF)], 0)
        for z in range(NZ):
            send[x * NZ + z] = chunk


def parent_kernel(bos, qp, got, kv0, kv1, kv2, kv3, out, keys, vals, qpos, turned):
    x, z, y = lax.axis_index("xh"), lax.axis_index("z"), lax.axis_index("y")
    masks = []
    for b in range(NB):
        for r in range(QR):
            row = (b * QR + r) * PER
            qpos[row : row + PER, :] = jnp.full((PER, HD), qp[(b * NY + y) * QR + r], jnp.int32)
    rows = ROWS * PER
    lane = lax.broadcasted_iota(jnp.int32, (rows, HD), 1)
    for i, kv in enumerate((kv0, kv1, kv2, kv3)):
        for k in range(NX):
            at = i * NX + k
            keys[at * TOK : (at + 1) * TOK, :] = kv[k, 0, :TOK, :]
            vals[at * TOK : (at + 1) * TOK, :] = kv[k, 1, :TOK, :]
            owner = x if k == 0 else 1 - x
            base = bos[(owner * NZ + z) * NY + lax.rem(y + NY - i, NY)] * TOK
            masks.append(lane + base < qpos[...])
            at = NA * TOK + at * ANC
            keys[at : at + ANC, :] = kv[k, 0, TOK:, :]
            vals[at : at + ANC, :] = kv[k, 1, TOK:, :]
    q = got[:, STRIDE:, :].reshape(rows, HD)
    s = nt(q, keys[...]) * SCALE
    s = [s[:, i * HD : (i + 1) * HD] for i in range(KEYS // HD)]
    s = [jnp.where(v, t, -1e30) for v, t in zip(masks, s)] + s[NA:]
    m = jnp.max(functools.reduce(jnp.maximum, s), axis=1, keepdims=True)
    p = [jnp.exp2(v - m) for v in s]
    total = jnp.sum(sum(p[1:], p[0]), axis=1, keepdims=True)
    p = jnp.concatenate([v.astype(BF) for v in p], 1)
    o = jnp.dot(p, vals[...], preferred_element_type=F32)
    turned[0] = o * (1.0 / total)
    turned[1] = jnp.broadcast_to(m + jnp.log2(total), (rows, HD))
    stats = jnp.zeros((ROWS, HD), F32)
    lanes = lax.broadcasted_iota(jnp.int32, (ROWS, HD), 1)
    for h in range(PER):
        pick = pl.ds(h, ROWS, stride=PER)
        out[:, h * HD : (h + 1) * HD] = turned[0, pick, :].astype(BF)
        stats = jnp.where(lanes == h, turned[1, pick, :], stats)
    hi = stats.astype(BF).astype(F32)
    mid = (stats - hi).astype(BF).astype(F32)
    low = stats - hi - mid
    stats = hi + pltpu.roll(mid, PER, 1) + pltpu.roll(low, 2 * PER, 1)
    out[:, PER * HD : PER * HD + HD] = stats.astype(BF)
    out[:, PER * HD + HD :] = jnp.zeros((ROWS, HD), BF)


def context_kernel(bos, lens, q_ref, ck, cv, a0, a1, a2, a3, out, keys, vals):
    slot = (lax.axis_index("xh") * NZ + lax.axis_index("z")) * NY + lax.axis_index("y")
    base = bos[slot] * TOK
    count = NB * ANC
    for i, a in enumerate((a0, a1, a2, a3)):
        for g in range(GROUPS):
            k, v = g * ANC, (GROUPS + g) * ANC
            keys[g, i * count : (i + 1) * count, :] = a[:, k : k + ANC, :].reshape(count, HD)
            vals[g, i * count : (i + 1) * count, :] = a[:, v : v + ANC, :].reshape(count, HD)
    mine = lax.broadcasted_iota(jnp.int32, (TOK, TOK), 0)
    other = lax.broadcasted_iota(jnp.int32, (TOK, TOK), 1)
    visible = other <= mine
    end = jnp.int32(0)
    for j in range(lens.shape[0]):
        end = end + lens[j]
        visible = visible & ((mine + base >= end) == (other + base >= end))
    for g in range(GROUPS):
        own_k = ck[:, g * HD : (g + 1) * HD]
        own_v = cv[:, g * HD : (g + 1) * HD]
        for half in range(4):
            hs = [g * PER + half * 2 + j for j in range(2)]
            q = jnp.concatenate([q_ref[:, h * HD : (h + 1) * HD] for h in hs], 0)
            sa = nt(q, keys[g]) * SCALE
            so = nt(q, own_k) * SCALE
            so = jnp.where(visible[None], so.reshape(2, TOK, TOK), -1e30).reshape(2 * TOK, TOK)
            m = jnp.maximum(jnp.max(sa, axis=1, keepdims=True), jnp.max(so, axis=1, keepdims=True))
            pa = jnp.exp2(sa - m)
            po = jnp.exp2(so - m)
            total = jnp.sum(pa, axis=1, keepdims=True) + jnp.sum(po, axis=1, keepdims=True)
            o = jnp.dot(pa.astype(BF), vals[g], preferred_element_type=F32)
            o = o + jnp.dot(po.astype(BF), own_v, preferred_element_type=F32)
            o = (o / total).astype(BF)
            for j, h in enumerate(hs):
                out[:, h * HD : (h + 1) * HD] = o[j * TOK : (j + 1) * TOK]


def combine_kernel(got, out):
    st = got[:, PER * HD : PER * HD + HD].astype(F32)
    lse = st + pltpu.roll(st, HD - PER, 1) + pltpu.roll(st, HD - 2 * PER, 1)
    count = NZ * NH // 8
    tiles = lse.reshape(GROUPS, count, 8, HD)
    top = jnp.max(tiles, axis=1)
    top = jnp.maximum(top, pltpu.roll(top, 4, 1))
    w = jnp.exp2(tiles - top[:, None])
    total = jnp.sum(w, axis=1)
    total = total + pltpu.roll(total, 4, 1)
    w = (w / total[:, None]).reshape(GROUPS * NZ * NH, HD)
    for h in range(PER):
        x = got[:, h * HD : (h + 1) * HD].astype(F32) * w[:, h : h + 1]
        x = jnp.sum(x.reshape(GROUPS, count, 8, HD), axis=1)
        x = x + pltpu.roll(x, 4, 1)
        for k in range(NH):
            for g in range(GROUPS):
                at = (k * GH + g * PER + h) * HD
                out[:, at : at + HD] = x[g, k : k + 1].astype(BF)


def on_device(cq, ck, cv, ak, av, pq, bos, lens, qp):
    half = jax.ShapeDtypeStruct((2, KVR, HD), BF)
    keep, give = pl.pallas_call(
        half_kernel,
        out_shape=(half, half),
        in_specs=[VMEM] * 4,
        out_specs=(VMEM,) * 2,
        compiler_params=params(60),
        name="half",
    )(ak, av, ck, cv)
    send = pl.pallas_call(
        send_kernel,
        out_shape=jax.ShapeDtypeStruct((NB, CHUNK, HD), BF),
        in_specs=[VMEM] * 3,
        out_specs=VMEM,
        scratch_shapes=[pltpu.VMEM((GROUPS * QR * PER, HD), F32)],
        compiler_params=params(60),
        cost_estimate=pl.CostEstimate(flops=3 * 10**9, bytes_accessed=10**6, transcendentals=0),
        name="send",
    )(ak, av, pq)

    def turn(x, shift):
        return lax.ppermute(x, "y", [(i, (i + shift) % NY) for i in range(NY)])

    other = lax.ppermute(give, "xh", [(0, 1), (1, 0)])
    send, other = lax.optimization_barrier((send, other))
    kv = jnp.stack([keep, other])
    kvs = [kv] + [turn(kv, s) for s in (1, 2, 3)]
    got = lax.all_to_all(send, ("xh", "z"), 0, 0, tiled=True)
    got, *kvs = lax.optimization_barrier((got, *kvs))
    anchors = got[:, :STRIDE]
    anchors = [anchors] + [turn(anchors, s) for s in (1, 2, 3)]
    part = pl.pallas_call(
        parent_kernel,
        out_shape=jax.ShapeDtypeStruct((ROWS, WIDE), BF),
        in_specs=[SMEM] * 2 + [VMEM] * 5,
        out_specs=VMEM,
        scratch_shapes=[
            pltpu.VMEM((KEYS, HD), BF),
            pltpu.VMEM((KEYS, HD), BF),
            pltpu.VMEM((ROWS * PER, HD), jnp.int32),
            pltpu.VMEM((2, ROWS * PER, HD), F32),
        ],
        compiler_params=params(),
        cost_estimate=pl.CostEstimate(flops=10**9, bytes_accessed=2 * 10**6, transcendentals=10**6),
        name="parent",
    )(bos, qp, got, *kvs)
    part = part.reshape(ROWS, 2, WIDE // 2)
    back = lax.all_to_all(part, ("xh", "z", "xl", "c"), 0, 0, tiled=True)
    context = pl.pallas_call(
        context_kernel,
        out_shape=jax.ShapeDtypeStruct((TOK, GH * HD), BF),
        in_specs=[SMEM] * 2 + [VMEM] * 7,
        out_specs=VMEM,
        scratch_shapes=[
            pltpu.VMEM((GROUPS, NY * NB * ANC, HD), BF),
            pltpu.VMEM((GROUPS, NY * NB * ANC, HD), BF),
        ],
        compiler_params=params(),
        cost_estimate=pl.CostEstimate(flops=60 * 10**9, bytes_accessed=4 * 10**6, transcendentals=3 * 10**6),
        name="context",
    )(bos, lens, cq, ck, cv, *anchors)
    parent = pl.pallas_call(
        combine_kernel,
        out_shape=jax.ShapeDtypeStruct((1, NH * GH * HD), BF),
        in_specs=[VMEM],
        out_specs=VMEM,
        compiler_params=params(),
        name="combine",
    )(back.reshape(NB * NH, WIDE))
    return context, parent


def solution(mesh):
    fine = Mesh(mesh.devices.reshape(NX, NZ, NY, NL, NC), ("xh", "z", "y", "xl", "c"))
    blk, head = ("xh", "z", "y"), ("xl", "c")
    both = P(blk, head)
    return jax.shard_map(
        on_device,
        mesh=fine,
        in_specs=(both,) * 6 + (P(), P(), P()),
        out_specs=(both, P(blk + head, None)),
        check_vma=False,
    )
```

time: 60.7 us -> 60.9 us (level)
  waiting for transfers between devices: 19.2 us -> 13 us
  starting transfers between devices: 28.3 us -> 33.3 us
  Pallas kernels: 11.3 us -> 12.6 us
    ppermute x6, waiting for transfers between devices: 10.4 us -> 6.65 us  [turn(): return lax.ppermute(x, 'y', [(i, (i + shift) % NY) for i in range(NY)])]
    ppermute x0 -> x1, starting transfers between devices: none -> 3.57 us  [on_device(): other = lax.ppermute(give, 'xh', [(0, 1), (1, 0)])]
    all_to_all x1, starting transfers between devices: 8.88 us -> 11.1 us  [on_device(): back = lax.all_to_all(part, ('xh', 'z', 'xl', 'c'), 0, 0, tiled=True)]
    all_to_all x1, waiting for transfers between devices: 2.19 us -> 0.38 us  [on_device(): got = lax.all_to_all(send, ('xh', 'z'), 0, 0, tiled=True)]
    pallas_call x2 -> x3, Pallas kernels: 4.19 us -> 5.54 us  [the longest x1 2.37 us: on_device(): pl.pallas_call(parent_kernel, out_shape=jax.ShapeDtypeStruct((ROWS, WIDE)...]
    all_to_all x1, waiting for transfers between devices: 6.59 us -> 5.57 us  [on_device(): back = lax.all_to_all(part, ('xh', 'z', 'xl', 'c'), 0, 0, tiled=True)]
    all_to_all x1, starting transfers between devices: 11.7 us -> 11 us  [on_device(): got = lax.all_to_all(send, ('xh', 'z'), 0, 0, tiled=True)]
  transfers between devices with their start and end apart: 8 -> 9, of which waited for: 6 -> 6; matrix products, arithmetic and copies ran while one was open for 1% -> 1% of each run, Pallas kernels for 14% -> 14%
where the time goes in v3:
time: 60.9 us; the launch traced here: 60.4 us
  starting transfers between devices  33.3 us (55%)
  waiting for transfers between devices  13 us (21%)
  Pallas kernels  12.6 us (21%)
  local copies, waits for them, and re-layouts  0.78 us (1%)
  between operations  0.77 us (1%)
    all_to_all x1, starting transfers between devices, on_device(): back = lax.all_to_all(part, ('xh', 'z', 'xl', 'c'), 0, 0, tiled=True)  11.1 us
    all_to_all x1, starting transfers between devices, on_device(): got = lax.all_to_all(send, ('xh', 'z'), 0, 0, tiled=True)  11 us
    ppermute x6, starting transfers between devices, turn(): return lax.ppermute(x, 'y', [(i, (i + shift) % NY) for i in range(NY)])  7.7 us
    ppermute x6, waiting for transfers between devices, turn(): return lax.ppermute(x, 'y', [(i, (i + shift) % NY) for i in range(NY)])  6.65 us
    pallas_call x1, Pallas kernels, on_device(): pl.pallas_call(context_kernel, out_shape=jax.ShapeDtypeStruct((TOK, GH *...  6.15 us
    all_to_all x1, waiting for transfers between devices, on_device(): back = lax.all_to_all(part, ('xh', 'z', 'xl', 'c'), 0, 0, tiled=True)  5.57 us
    ppermute x1, starting transfers between devices, on_device(): other = lax.ppermute(give, 'xh', [(0, 1), (1, 0)])  3.57 us
    pallas_call x1, Pallas kernels, on_device(): pl.pallas_call(parent_kernel, out_shape=jax.ShapeDtypeStruct((ROWS, WIDE)...  2.37 us
  transfers between devices with their start and end apart: 9, of which 6 were waited for; matrix products, arithmetic and copies ran while one was open for 1% of the time, Pallas kernels for 14%

profile of v3, /device:TPU:1, one launch (start us, length us, event | category | flops | bytes accessed | tf_op | source)
XLA Modules:
  0.0 60.4 jit_solution(7257821074988180279)
XLA Ops:
  0.6 1.6 %half.1 = (bf16[2,144,128]{2,1,0:T(8,128)(2,1)}, bf16[2,144,128]{2,1,0:T(8,128)(2,1)}) custom-call(bf16[16,256]{1,0:T(8,128)(2,1)} %ak.3, bf16[16,256]{1,0:T(8,128)(2,1)} %av.3, bf16[128,256]{1,0:T(8,128)(2,1)} %ck.3, bf16[128,256]{1,0:T(8,128)(2,1)} %cv.3), custom_call_target="tpu_custom_call" | custom-call | tf_op jit(solution)/shard_map/half/pallas_call | solution.py:174
  2.2 3.6 %collective-permute-start = (bf16[2,144,128]{2,1,0:T(8,128)(2,1)}, bf16[2,144,128]{2,1,0:T(8,128)(2,1)S(1)}, u32[]{:S(2)}, u32[]{:S(2)}) collective-permute-start(bf16[2,144,128]{2,1,0:T(8,128)(2,1)} %get-tuple-element.11), channel_id=1, source_target_pairs={{0,128},{128,0},{1,129},{129,1},{2,130},{130,2},{3,131},{131,3},{4... | collective-permute-start | bytes 221192 | tf_op jit(solution)/shard_map/ppermute | solution.py:196
  5.8 1.6 %send.1 = bf16[16,96,128]{2,1,0:T(8,128)(2,1)} custom-call(bf16[16,256]{1,0:T(8,128)(2,1)} %ak.3, bf16[16,256]{1,0:T(8,128)(2,1)} %av.3, bf16[4,2048]{1,0:T(4,128)(2,1)} %pq.1), custom_call_target="tpu_custom_call" | custom-call | flops 3000000000 | bytes 1000000 | tf_op jit(solution)/shard_map/send/pallas_call | solution.py:182
  7.4 0.4 collective-permute-done
  7.8 11.0 %all-to-all-start = ((bf16[16,96,128]{2,1,0:T(8,128)(2,1)}), bf16[16,96,128]{2,1,0:T(8,128)(2,1)S(1)}, u32[]{:S(2)}, u32[]{:S(2)}) async-start(bf16[16,96,128]{2,1,0:T(8,128)(2,1)} %send.1), calls=%async_computation | async-start | bytes 786432 | tf_op jit(solution)/shard_map/all_to_all | solution.py:200
  18.7 0.0 copy-done.6
  18.8 0.0 copy-start.3
  18.8 0.0 copy-start.4
  18.8 2.8 %collective-permute-start.3 = (bf16[2,2,144,128]{3,2,1,0:T(8,128)(2,1)S(1)}, bf16[2,2,144,128]{3,2,1,0:T(8,128)(2,1)S(1)}, u32[]{:S(2)}, u32[]{:S(2)}) collective-permute-start(bf16[2,2,144,128]{3,2,1,0:T(8,128)(2,1)S(1)} %pad_maximum_fusion.kv0), channel_id=1, source_target_pairs={{0,12},{4,0},{8,4},{12,8},{1,13},{5,1},{9,5},{13,9},{2,14},{6,2},{... | collective-permute-start | bytes 442376 | tf_op jit(solution)/shard_map/ppermute | solution.py:194
  21.6 0.3 collective-permute-start.2
  22.0 0.7 %collective-permute-start.1 = (bf16[2,2,144,128]{3,2,1,0:T(8,128)(2,1)S(1)}, bf16[2,2,144,128]{3,2,1,0:T(8,128)(2,1)S(1)}, u32[]{:S(2)}, u32[]{:S(2)}) collective-permute-start(bf16[2,2,144,128]{3,2,1,0:T(8,128)(2,1)S(1)} %pad_maximum_fusion.kv0), channel_id=1, source_target_pairs={{0,4},{4,8},{8,12},{12,0},{1,5},{5,9},{9,13},{13,1},{2,6},{6,10},{... | collective-permute-start | bytes 442376 | tf_op jit(solution)/shard_map/ppermute | solution.py:194
  22.7 2.0 %collective-permute-done.3.kv3 = bf16[2,2,144,128]{3,2,1,0:T(8,128)(2,1)S(1)} collective-permute-done((bf16[2,2,144,128]{3,2,1,0:T(8,128)(2,1)S(1)}, bf16[2,2,144,128]{3,2,1,0:T(8,128)(2,1)S(1)}, u32[]{:S(2)}, u32[]{:S(2)}) %collective-permute-start.3) | collective-permute-done | bytes 147488 | tf_op jit(solution)/shard_map/ppermute | solution.py:194
  24.6 2.8 %collective-permute-done.2.kv2 = bf16[2,2,144,128]{3,2,1,0:T(8,128)(2,1)S(1)} collective-permute-done((bf16[2,2,144,128]{3,2,1,0:T(8,128)(2,1)S(1)}, bf16[2,2,144,128]{3,2,1,0:T(8,128)(2,1)S(1)}, u32[]{:S(2)}, u32[]{:S(2)}) %collective-permute-start.2) | collective-permute-done | bytes 147488 | tf_op jit(solution)/shard_map/ppermute | solution.py:194
  27.4 1.9 %collective-permute-done.1.kv1 = bf16[2,2,144,128]{3,2,1,0:T(8,128)(2,1)S(1)} collective-permute-done((bf16[2,2,144,128]{3,2,1,0:T(8,128)(2,1)S(1)}, bf16[2,2,144,128]{3,2,1,0:T(8,128)(2,1)S(1)}, u32[]{:S(2)}, u32[]{:S(2)}) %collective-permute-start.1) | collective-permute-done | bytes 147488 | tf_op jit(solution)/shard_map/ppermute | solution.py:194
  29.3 0.4 all-to-all-done.got
  29.7 2.8 %collective-permute-start.6 = (bf16[16,64,128]{2,1,0:T(8,128)(2,1)S(1)}, bf16[16,64,128]{2,1,0:T(8,128)(2,1)S(1)}, u32[]{:S(2)}, u32[]{:S(2)}) collective-permute-start(bf16[16,64,128]{2,1,0:T(8,128)(2,1)S(1)} %slice.3.a0), channel_id=1, source_target_pairs={{0,12},{4,0},{8,4},{12,8},{1,13},{5,1},{9,5},{13,9},{2,14},{6,2},{... | collective-permute-start | bytes 786440 | tf_op jit(solution)/shard_map/ppermute | solution.py:194
  32.5 0.3 collective-permute-start.5
  32.9 0.7 %collective-permute-start.4 = (bf16[16,64,128]{2,1,0:T(8,128)(2,1)S(1)}, bf16[16,64,128]{2,1,0:T(8,128)(2,1)S(1)}, u32[]{:S(2)}, u32[]{:S(2)}) collective-permute-start(bf16[16,64,128]{2,1,0:T(8,128)(2,1)S(1)} %slice.3.a0), channel_id=1, source_target_pairs={{0,4},{4,8},{8,12},{12,0},{1,5},{5,9},{9,13},{13,1},{2,6},{6,10},{... | collective-permute-start | bytes 786440 | tf_op jit(solution)/shard_map/ppermute | solution.py:194
  33.6 0.0 copy-done.3
  33.6 0.0 copy-done.4
  33.6 2.4 %parent.1 = bf16[64,1280]{1,0:T(8,128)(2,1)S(1)} custom-call(s32[64]{0:T(128)S(1)} %copy-done.4, s32[256]{0:T(256)S(1)} %copy-done.3, bf16[16,96,128]{2,1,0:T(8,128)(2,1)S(1)} %all-to-all-done.got, bf16[2,2,144,128]{3,2,1,0:T(8,128)(2,1)S(1)} %pad_maximum_fusion.kv0, bf16[2,2,144,128]{3,2,1,0:T(8,128)(2,1)S(1)} %collective-permute-done.1.kv1, ...), custom_call_target="tpu_custom_call" | custom-call | flops 1000000000 | bytes 2000000 | tf_op jit(solution)/shard_map/parent/pallas_call | solution.py:204
  35.9 0.0 copy-start.2
  36.0 0.7 %reshape.10 = bf16[64,2,640]{2,1,0:T(2,128)(2,1)} reshape(bf16[64,1280]{1,0:T(8,128)(2,1)S(1)} %parent.1) | data formatting | bytes 327680 | tf_op jit(solution)/shard_map/reshape | solution.py:219
  36.7 11.1 %all-to-all-start.1 = ((bf16[64,2,640]{2,1,0:T(2,128)(2,1)}), bf16[64,2,640]{2,1,0:T(2,128)(2,1)S(1)}, u32[]{:S(2)}, u32[]{:S(2)}) async-start(bf16[64,2,640]{2,1,0:T(2,128)(2,1)} %reshape.10), calls=%async_computation.1 | async-start | bytes 327680 | tf_op jit(solution)/shard_map/all_to_all | solution.py:220
  47.8 0.0 collective-permute-done.6.a3
  47.8 0.0 collective-permute-done.5.a2
  47.8 0.0 collective-permute-done.4.a1
  47.8 0.0 copy-done.5
  47.8 0.0 copy-done.2
  47.8 6.1 %context.1 = bf16[128,2048]{1,0:T(8,128)(2,1)} custom-call(s32[64]{0:T(128)S(1)} %copy-done.4, s32[8]{0:T(128)S(1)} %copy-done.5, bf16[128,2048]{1,0:T(8,128)(2,1)S(1)} %copy-done.2, bf16[128,256]{1,0:T(8,128)(2,1)S(1)} %copy-done, bf16[128,256]{1,0:T(8,128)(2,1)S(1)} %copy-done.1, bf16[16,64,128]{2,1,0:T(8,128)(2,1)S(1)} %slice.3.a0, ...), custom_call_target="tpu_custom_call" | custom-call | flops 60000002048 | bytes 4000000 | tf_op jit(solution)/shard_map/context/pallas_call | solution.py:221
  54.0 5.6 %all-to-all-done.1 = bf16[64,2,640]{2,1,0:T(2,128)(2,1)S(1)} async-done(((bf16[64,2,640]{2,1,0:T(2,128)(2,1)}), bf16[64,2,640]{2,1,0:T(2,128)(2,1)S(1)}, u32[]{:S(2)}, u32[]{:S(2)}) %all-to-all-start.1) | async-done | bytes 163872 | tf_op jit(solution)/shard_map/all_to_all | solution.py:220
  59.6 0.9 %combine.1 = bf16[1,8192]{1,0:T(2,128)(2,1)} custom-call(bf16[64,1280]{1,0:T(8,128)(2,1)S(1)} %bitcast.4), custom_call_target="tpu_custom_call" | custom-call | tf_op jit(solution)/shard_map/combine/pallas_call | solution.py:234
  (9 shorter events, 0.1 us)
Async XLA Ops:
  2.2 5.5 %collective-permute-start = (bf16[2,144,128]{2,1,0:T(8,128)(2,1)}, bf16[2,144,128]{2,1,0:T(8,128)(2,1)S(1)}, u32[]{:S(2)}, u32[]{:S(2)}) collective-permute-start(bf16[2,144,128]{2,1,0:T(8,128)(2,1)} %get-tuple-element.11), channel_id=1, source_target_pairs={{0,128},{128,0},{1,129},{129,1},{2,130},{130,2},{3,131},{131,3},{4... | collective-permute-start | bytes 221192 | tf_op jit(solution)/shard_map/ppermute | solution.py:196
  7.4 11.4 %copy-start.6 = (bf16[2,144,128]{2,1,0:T(8,128)(2,1)S(1)}, bf16[2,144,128]{2,1,0:T(8,128)(2,1)}, u32[]{:S(2)}) copy-start(bf16[2,144,128]{2,1,0:T(8,128)(2,1)} %get-tuple-element.13) | copy-start | bytes 221188
  7.8 21.9 %all-to-all-start = ((bf16[16,96,128]{2,1,0:T(8,128)(2,1)}), bf16[16,96,128]{2,1,0:T(8,128)(2,1)S(1)}, u32[]{:S(2)}, u32[]{:S(2)}) async-start(bf16[16,96,128]{2,1,0:T(8,128)(2,1)} %send.1), calls=%async_computation | async-start | bytes 786432 | tf_op jit(solution)/shard_map/all_to_all | solution.py:200
  18.8 14.8 %copy-start.3 = (s32[256]{0:T(256)S(1)}, s32[256]{0:T(256)}, u32[]{:S(2)}) copy-start(s32[256]{0:T(256)} %qp.1) | copy-start | bytes 3076
  18.8 14.8 %copy-start.4 = (s32[64]{0:T(128)S(1)}, s32[64]{0:T(128)}, u32[]{:S(2)}) copy-start(s32[64]{0:T(128)} %bos.3) | copy-start | bytes 772
  18.8 5.8 %collective-permute-start.3 = (bf16[2,2,144,128]{3,2,1,0:T(8,128)(2,1)S(1)}, bf16[2,2,144,128]{3,2,1,0:T(8,128)(2,1)S(1)}, u32[]{:S(2)}, u32[]{:S(2)}) collective-permute-start(bf16[2,2,144,128]{3,2,1,0:T(8,128)(2,1)S(1)} %pad_maximum_fusion.kv0), channel_id=1, source_target_pairs={{0,12},{4,0},{8,4},{12,8},{1,13},{5,1},{9,5},{13,9},{2,14},{6,2},{... | collective-permute-start | bytes 442376 | tf_op jit(solution)/shard_map/ppermute | solution.py:194
  21.6 5.8 %collective-permute-start.2 = (bf16[2,2,144,128]{3,2,1,0:T(8,128)(2,1)S(1)}, bf16[2,2,144,128]{3,2,1,0:T(8,128)(2,1)S(1)}, u32[]{:S(2)}, u32[]{:S(2)}) collective-permute-start(bf16[2,2,144,128]{3,2,1,0:T(8,128)(2,1)S(1)} %pad_maximum_fusion.kv0), channel_id=1, source_target_pairs={{0,8},{4,12},{8,0},{12,4},{1,9},{5,13},{9,1},{13,5},{2,10},{6,14},... | collective-permute-start | bytes 442376 | tf_op jit(solution)/shard_map/ppermute | solution.py:194
  22.0 7.3 %collective-permute-start.1 = (bf16[2,2,144,128]{3,2,1,0:T(8,128)(2,1)S(1)}, bf16[2,2,144,128]{3,2,1,0:T(8,128)(2,1)S(1)}, u32[]{:S(2)}, u32[]{:S(2)}) collective-permute-start(bf16[2,2,144,128]{3,2,1,0:T(8,128)(2,1)S(1)} %pad_maximum_fusion.kv0), channel_id=1, source_target_pairs={{0,4},{4,8},{8,12},{12,0},{1,5},{5,9},{9,13},{13,1},{2,6},{6,10},{... | collective-permute-start | bytes 442376 | tf_op jit(solution)/shard_map/ppermute | solution.py:194
  29.7 18.0 %collective-permute-start.6 = (bf16[16,64,128]{2,1,0:T(8,128)(2,1)S(1)}, bf16[16,64,128]{2,1,0:T(8,128)(2,1)S(1)}, u32[]{:S(2)}, u32[]{:S(2)}) collective-permute-start(bf16[16,64,128]{2,1,0:T(8,128)(2,1)S(1)} %slice.3.a0), channel_id=1, source_target_pairs={{0,12},{4,0},{8,4},{12,8},{1,13},{5,1},{9,5},{13,9},{2,14},{6,2},{... | collective-permute-start | bytes 786440 | tf_op jit(solution)/shard_map/ppermute | solution.py:194
  32.5 15.2 %collective-permute-start.5 = (bf16[16,64,128]{2,1,0:T(8,128)(2,1)S(1)}, bf16[16,64,128]{2,1,0:T(8,128)(2,1)S(1)}, u32[]{:S(2)}, u32[]{:S(2)}) collective-permute-start(bf16[16,64,128]{2,1,0:T(8,128)(2,1)S(1)} %slice.3.a0), channel_id=1, source_target_pairs={{0,8},{4,12},{8,0},{12,4},{1,9},{5,13},{9,1},{13,5},{2,10},{6,14},... | collective-permute-start | bytes 786440 | tf_op jit(solution)/shard_map/ppermute | solution.py:194
  32.9 14.9 %collective-permute-start.4 = (bf16[16,64,128]{2,1,0:T(8,128)(2,1)S(1)}, bf16[16,64,128]{2,1,0:T(8,128)(2,1)S(1)}, u32[]{:S(2)}, u32[]{:S(2)}) collective-permute-start(bf16[16,64,128]{2,1,0:T(8,128)(2,1)S(1)} %slice.3.a0), channel_id=1, source_target_pairs={{0,4},{4,8},{8,12},{12,0},{1,5},{5,9},{9,13},{13,1},{2,6},{6,10},{... | collective-permute-start | bytes 786440 | tf_op jit(solution)/shard_map/ppermute | solution.py:194
  33.6 14.2 %copy-start.5 = (s32[8]{0:T(128)S(1)}, s32[8]{0:T(128)}, u32[]{:S(2)}) copy-start(s32[8]{0:T(128)} %lens.1) | copy-start | bytes 100
  35.9 11.9 %copy-start.2 = (bf16[128,2048]{1,0:T(8,128)(2,1)S(1)}, bf16[128,2048]{1,0:T(8,128)(2,1)}, u32[]{:S(2)}) copy-start(bf16[128,2048]{1,0:T(8,128)(2,1)} %q_ref.1) | copy-start | bytes 1572868
  36.7 11.1 %copy-start = (bf16[128,256]{1,0:T(8,128)(2,1)S(1)}, bf16[128,256]{1,0:T(8,128)(2,1)}, u32[]{:S(2)}) copy-start(bf16[128,256]{1,0:T(8,128)(2,1)} %ck.3) | copy-start | bytes 196612
  36.7 11.1 %copy-start.1 = (bf16[128,256]{1,0:T(8,128)(2,1)S(1)}, bf16[128,256]{1,0:T(8,128)(2,1)}, u32[]{:S(2)}) copy-start(bf16[128,256]{1,0:T(8,128)(2,1)} %cv.3) | copy-start | bytes 196612
  36.7 22.9 %all-to-all-start.1 = ((bf16[64,2,640]{2,1,0:T(2,128)(2,1)}), bf16[64,2,640]{2,1,0:T(2,128)(2,1)S(1)}, u32[]{:S(2)}, u32[]{:S(2)}) async-start(bf16[64,2,640]{2,1,0:T(2,128)(2,1)} %reshape.10), calls=%async_computation.1 | async-start | bytes 327680 | tf_op jit(solution)/shard_map/all_to_all | solution.py:220

commit v4 on v3

--- a/solution.py
+++ b/solution.py
@@ -42,16 +42,7 @@
     return lax.dot_general(a, b, (((1,), (1,)), ((), ())), preferred_element_type=F32)
 
 
-def half_kernel(ak, av, ck, cv, keep, give):
-    first = lax.axis_index("xh") == 0
-    for i, (ctx, anc) in enumerate(((ck, ak), (cv, av))):
-        for rows, src in ((slice(0, TOK), ctx), (slice(TOK, KVR), anc)):
-            low, high = src[:, :HD], src[:, HD:]
-            keep[i, rows, :] = jnp.where(first, low, high)
-            give[i, rows, :] = jnp.where(first, high, low)
-
-
-def send_kernel(ak, av, pq, send, scr):
+def half_kernel(mine, ak, av, pq, ck, cv, out, scr):
     q = pq[...].astype(F32)
     for g in range(GROUPS):
         for r in range(QR):
@@ -59,12 +50,28 @@
                 col = (g * PER + h) * HD
                 row = (g * QR + r) * PER + h
                 scr[row : row + 1, :] = q[r : r + 1, col : col + HD]
-    parts = [ak[:, :HD], ak[:, HD:], av[:, :HD], av[:, HD:]]
-    for x in range(NX):
-        lo = x * QR * PER
-        chunk = jnp.concatenate(parts + [scr[lo : lo + QR * PER, :].astype(BF)], 0)
-        for z in range(NZ):
-            send[x * NZ + z] = chunk
+    low = lax.axis_index("xh") == (0 if mine else 1)
+    at = 0
+    for ctx, anc in ((ck, ak), (cv, av)):
+        for src in (ctx, anc):
+            out[at : at + src.shape[0], :] = jnp.where(low, src[:, :HD], src[:, HD:])
+            at = at + src.shape[0]
+    for part in (ak[:, :HD], ak[:, HD:], av[:, :HD], av[:, HD:]):
+        out[at : at + ANC, :] = part
+        at = at + ANC
+    q = jnp.where(low, scr[: QR * PER, :], scr[QR * PER :, :])
+    out[at:, :] = q.astype(BF)
+
+
+def send_kernel(own, other, send, kv):
+    first = lax.axis_index("xh") == 0
+    a, b = own[2 * KVR :, :], other[2 * KVR :, :]
+    chunk = jnp.concatenate([jnp.where(first, a, b), jnp.where(first, b, a)], 0)
+    for z in range(NZ):
+        send[z] = chunk
+    for i in range(2):
+        kv[0, i] = own[i * KVR : (i + 1) * KVR, :]
+        kv[1, i] = other[i * KVR : (i + 1) * KVR, :]
 
 
 def parent_kernel(bos, qp, got, kv0, kv1, kv2, kv3, out, keys, vals, qpos, turned):
@@ -73,7 +80,8 @@
     for b in range(NB):
         for r in range(QR):
             row = (b * QR + r) * PER
-            qpos[row : row + PER, :] = jnp.full((PER, HD), qp[(b * NY + y) * QR + r], jnp.int32)
+            at = ((b % NX * NZ + b // NX) * NY + y) * QR + r
+            qpos[row : row + PER, :] = jnp.full((PER, HD), qp[at], jnp.int32)
     rows = ROWS * PER
     lane = lax.broadcasted_iota(jnp.int32, (rows, HD), 1)
     for i, kv in enumerate((kv0, kv1, kv2, kv3)):
@@ -151,53 +159,53 @@
 def combine_kernel(got, out):
     st = got[:, PER * HD : PER * HD + HD].astype(F32)
     lse = st + pltpu.roll(st, HD - PER, 1) + pltpu.roll(st, HD - 2 * PER, 1)
-    count = NZ * NH // 8
-    tiles = lse.reshape(GROUPS, count, 8, HD)
-    top = jnp.max(tiles, axis=1)
-    top = jnp.maximum(top, pltpu.roll(top, 4, 1))
-    w = jnp.exp2(tiles - top[:, None])
-    total = jnp.sum(w, axis=1)
-    total = total + pltpu.roll(total, 4, 1)
-    w = (w / total[:, None]).reshape(GROUPS * NZ * NH, HD)
+    lse = lse.reshape(NZ, GROUPS * NH, HD)
+    w = jnp.exp2(lse - jnp.max(lse, axis=0, keepdims=True))
+    w = (w / jnp.sum(w, axis=0, keepdims=True)).reshape(NZ * GROUPS * NH, HD)
     for h in range(PER):
         x = got[:, h * HD : (h + 1) * HD].astype(F32) * w[:, h : h + 1]
-        x = jnp.sum(x.reshape(GROUPS, count, 8, HD), axis=1)
-        x = x + pltpu.roll(x, 4, 1)
-        for k in range(NH):
-            for g in range(GROUPS):
+        x = jnp.sum(x.reshape(NZ, GROUPS * NH, HD), axis=0)
+        for g in range(GROUPS):
+            for k in range(NH):
                 at = (k * GH + g * PER + h) * HD
-                out[:, at : at + HD] = x[g, k : k + 1].astype(BF)
+                out[:, at : at + HD] = x[g * NH + k : g * NH + k + 1].astype(BF)
 
 
 def on_device(cq, ck, cv, ak, av, pq, bos, lens, qp):
-    half = jax.ShapeDtypeStruct((2, KVR, HD), BF)
-    keep, give = pl.pallas_call(
-        half_kernel,
-        out_shape=(half, half),
-        in_specs=[VMEM] * 4,
+    half = jax.ShapeDtypeStruct((2 * KVR + CHUNK, HD), BF)
+    own, give = [
+        pl.pallas_call(
+            functools.partial(half_kernel, mine),
+            out_shape=half,
+            in_specs=[VMEM] * 5,
+            out_specs=VMEM,
+            scratch_shapes=[pltpu.VMEM((GROUPS * QR * PER, HD), F32)],
+            compiler_params=params(40 if mine else 60),
+            cost_estimate=pl.CostEstimate(
+                flops=3 * 10**9, bytes_accessed=10**6, transcendentals=0
+            ),
+            name="own" if mine else "give",
+        )(ak, av, pq, ck, cv)
+        for mine in (True, False)
+    ]
+    other = lax.ppermute(give, "xh", [(0, 1), (1, 0)])
+    send, kv = pl.pallas_call(
+        send_kernel,
+        out_shape=(
+            jax.ShapeDtypeStruct((NZ, NX * CHUNK, HD), BF),
+            jax.ShapeDtypeStruct((NX, 2, KVR, HD), BF),
+        ),
+        in_specs=[VMEM] * 2,
         out_specs=(VMEM,) * 2,
-        compiler_params=params(60),
-        name="half",
-    )(ak, av, ck, cv)
-    send = pl.pallas_call(
-        send_kernel,
-        out_shape=jax.ShapeDtypeStruct((NB, CHUNK, HD), BF),
-        in_specs=[VMEM] * 3,
-        out_specs=VMEM,
-        scratch_shapes=[pltpu.VMEM((GROUPS * QR * PER, HD), F32)],
-        compiler_params=params(60),
-        cost_estimate=pl.CostEstimate(flops=3 * 10**9, bytes_accessed=10**6, transcendentals=0),
+        compiler_params=params(),
         name="send",
-    )(ak, av, pq)
+    )(own, other)
 
     def turn(x, shift):
         return lax.ppermute(x, "y", [(i, (i + shift) % NY) for i in range(NY)])
 
-    other = lax.ppermute(give, "xh", [(0, 1), (1, 0)])
-    send, other = lax.optimization_barrier((send, other))
-    kv = jnp.stack([keep, other])
     kvs = [kv] + [turn(kv, s) for s in (1, 2, 3)]
-    got = lax.all_to_all(send, ("xh", "z"), 0, 0, tiled=True)
+    got = lax.all_to_all(send, "z", 0, 0, tiled=True).reshape(NB, CHUNK, HD)
     got, *kvs = lax.optimization_barrier((got, *kvs))
     anchors = got[:, :STRIDE]
     anchors = [anchors] + [turn(anchors, s) for s in (1, 2, 3)]
@@ -217,7 +225,7 @@
         name="parent",
     )(bos, qp, got, *kvs)
     part = part.reshape(ROWS, 2, WIDE // 2)
-    back = lax.all_to_all(part, ("xh", "z", "xl", "c"), 0, 0, tiled=True)
+    back = lax.all_to_all(part, ("z", "xh", "xl", "c"), 0, 0, tiled=True)
     context = pl.pallas_call(
         context_kernel,
         out_shape=jax.ShapeDtypeStruct((TOK, GH * HD), BF),

time: 60.9 us -> 59.3 us (0.974)
  starting transfers between devices: 33.3 us -> 29.4 us
  waiting for transfers between devices: 13 us -> 16.1 us
  Pallas kernels: 12.6 us -> 11.9 us
    all_to_all x2, starting transfers between devices: 22 us -> 18.2 us  [the longest x1 9.83 us: on_device(): back = lax.all_to_all(part, ('z', 'xh', 'xl', 'c'), 0, 0, tiled=True)]
    ppermute x1, waiting for transfers between devices: 0.39 us -> 2.14 us  [on_device(): other = lax.ppermute(give, 'xh', [(0, 1), (1, 0)])]
    all_to_all x2, waiting for transfers between devices: 5.95 us -> 7.29 us  [the longest x1 5.52 us: on_device(): back = lax.all_to_all(part, ('z', 'xh', 'xl', 'c'), 0, 0, tiled=True)]
    pallas_call x2 -> x3, Pallas kernels: 3.17 us -> 2.52 us  [the longest x2 1.71 us: on_device(): pl.pallas_call(functools.partial(half_kernel, mine), out_shape=half, in_s...]
where the time goes in v4:
time: 59.3 us; the launch traced here: 58.9 us
  starting transfers between devices  29.4 us (50%)
  waiting for transfers between devices  16.1 us (27%)
  Pallas kernels  11.9 us (20%)
  local copies, waits for them, and re-layouts  0.78 us (1%)
  between operations  0.77 us (1%)
    all_to_all x1, starting transfers between devices, on_device(): back = lax.all_to_all(part, ('z', 'xh', 'xl', 'c'), 0, 0, tiled=True)  9.83 us
    all_to_all x1, starting transfers between devices, on_device(): got = lax.all_to_all(send, 'z', 0, 0, tiled=True).reshape(NB, CHUNK, HD)  8.41 us
    ppermute x6, starting transfers between devices, turn(): return lax.ppermute(x, 'y', [(i, (i + shift) % NY) for i in range(NY)])  7.63 us
    ppermute x6, waiting for transfers between devices, turn(): return lax.ppermute(x, 'y', [(i, (i + shift) % NY) for i in range(NY)])  6.65 us
    pallas_call x1, Pallas kernels, on_device(): pl.pallas_call(context_kernel, out_shape=jax.ShapeDtypeStruct((TOK, GH *...  6.11 us
    all_to_all x1, waiting for transfers between devices, on_device(): back = lax.all_to_all(part, ('z', 'xh', 'xl', 'c'), 0, 0, tiled=True)  5.52 us
    ppermute x1, starting transfers between devices, on_device(): other = lax.ppermute(give, 'xh', [(0, 1), (1, 0)])  3.57 us
    pallas_call x1, Pallas kernels, on_device(): pl.pallas_call(parent_kernel, out_shape=jax.ShapeDtypeStruct((ROWS, WIDE)...  2.36 us
  transfers between devices with their start and end apart: 9, of which 6 were waited for; matrix products, arithmetic and copies ran while one was open for 1% of the time, Pallas kernels for 14%

profile of v4, /device:TPU:1, one launch (start us, length us, event | category | flops | bytes accessed | tf_op | source)
XLA Modules:
  0.0 58.9 jit_solution(5854169029000564019)
XLA Ops:
  0.6 0.0 copy-start.2
  0.6 0.0 copy-start.1
  0.7 1.7 %give.1 = bf16[384,128]{1,0:T(8,128)(2,1)} custom-call(bf16[16,256]{1,0:T(8,128)(2,1)} %ak.3, bf16[16,256]{1,0:T(8,128)(2,1)} %av.3, bf16[4,2048]{1,0:T(4,128)(2,1)} %pq.3, bf16[128,256]{1,0:T(8,128)(2,1)} %ck.5, bf16[128,256]{1,0:T(8,128)(2,1)} %cv.5), custom_call_target="tpu_custom_call" | custom-call | flops 3000000000 | bytes 1000000 | tf_op jit(solution)/shard_map/give/pallas_call | solution.py:177
  2.3 3.6 %collective-permute-start = (bf16[384,128]{1,0:T(8,128)(2,1)}, bf16[384,128]{1,0:T(8,128)(2,1)S(1)}, u32[]{:S(2)}, u32[]{:S(2)}) collective-permute-start(bf16[384,128]{1,0:T(8,128)(2,1)} %give.1), channel_id=1, source_target_pairs={{0,128},{128,0},{1,129},{129,1},{2,130},{130,2},{3,131},{131,3},{4... | collective-permute-start | bytes 294920 | tf_op jit(solution)/shard_map/ppermute | solution.py:191
  5.9 0.0 copy-done.5
  5.9 0.0 copy-done.4
  6.0 2.1 %collective-permute-done.other = bf16[384,128]{1,0:T(8,128)(2,1)S(1)} collective-permute-done((bf16[384,128]{1,0:T(8,128)(2,1)}, bf16[384,128]{1,0:T(8,128)(2,1)S(1)}, u32[]{:S(2)}, u32[]{:S(2)}) %collective-permute-start) | collective-permute-done | bytes 98336 | tf_op jit(solution)/shard_map/ppermute | solution.py:191
  8.1 0.8 %send.1 = (bf16[8,192,128]{2,1,0:T(8,128)(2,1)}, bf16[2,2,144,128]{3,2,1,0:T(8,128)(2,1)S(1)}) custom-call(bf16[384,128]{1,0:T(8,128)(2,1)S(1)} %own.1, bf16[384,128]{1,0:T(8,128)(2,1)S(1)} %collective-permute-done.other), custom_call_target="tpu_custom_call" | custom-call | tf_op jit(solution)/shard_map/send/pallas_call | solution.py:192
  8.9 8.4 %all-to-all-start = ((bf16[8,192,128]{2,1,0:T(8,128)(2,1)}), bf16[8,192,128]{2,1,0:T(8,128)(2,1)S(1)}, u32[]{:S(2)}, u32[]{:S(2)}) async-start(bf16[8,192,128]{2,1,0:T(8,128)(2,1)} %get-tuple-element.9), calls=%async_computation | async-start | bytes 786432 | tf_op jit(solution)/shard_map/all_to_all | solution.py:208
  17.4 2.7 %collective-permute-start.3 = (bf16[2,2,144,128]{3,2,1,0:T(8,128)(2,1)S(1)}, bf16[2,2,144,128]{3,2,1,0:T(8,128)(2,1)S(1)}, u32[]{:S(2)}, u32[]{:S(2)}) collective-permute-start(bf16[2,2,144,128]{3,2,1,0:T(8,128)(2,1)S(1)} %get-tuple-element.12.kv0), channel_id=1, source_target_pairs={{0,12},{4,0},{8,4},{12,8},{1,13},{5,1},{9,5},{13,9},{2,14},{6,2},{... | collective-permute-start | bytes 442376 | tf_op jit(solution)/shard_map/ppermute | solution.py:205
  20.1 0.3 collective-permute-start.2
  20.4 0.7 %collective-permute-start.1 = (bf16[2,2,144,128]{3,2,1,0:T(8,128)(2,1)S(1)}, bf16[2,2,144,128]{3,2,1,0:T(8,128)(2,1)S(1)}, u32[]{:S(2)}, u32[]{:S(2)}) collective-permute-start(bf16[2,2,144,128]{3,2,1,0:T(8,128)(2,1)S(1)} %get-tuple-element.12.kv0), channel_id=1, source_target_pairs={{0,4},{4,8},{8,12},{12,0},{1,5},{5,9},{9,13},{13,1},{2,6},{6,10},{... | collective-permute-start | bytes 442376 | tf_op jit(solution)/shard_map/ppermute | solution.py:205
  21.1 2.0 %collective-permute-done.3.kv3 = bf16[2,2,144,128]{3,2,1,0:T(8,128)(2,1)S(1)} collective-permute-done((bf16[2,2,144,128]{3,2,1,0:T(8,128)(2,1)S(1)}, bf16[2,2,144,128]{3,2,1,0:T(8,128)(2,1)S(1)}, u32[]{:S(2)}, u32[]{:S(2)}) %collective-permute-start.3) | collective-permute-done | bytes 147488 | tf_op jit(solution)/shard_map/ppermute | solution.py:205
  23.1 2.6 %collective-permute-done.2.kv2 = bf16[2,2,144,128]{3,2,1,0:T(8,128)(2,1)S(1)} collective-permute-done((bf16[2,2,144,128]{3,2,1,0:T(8,128)(2,1)S(1)}, bf16[2,2,144,128]{3,2,1,0:T(8,128)(2,1)S(1)}, u32[]{:S(2)}, u32[]{:S(2)}) %collective-permute-start.2) | collective-permute-done | bytes 147488 | tf_op jit(solution)/shard_map/ppermute | solution.py:205
  25.7 2.1 %collective-permute-done.1.kv1 = bf16[2,2,144,128]{3,2,1,0:T(8,128)(2,1)S(1)} collective-permute-done((bf16[2,2,144,128]{3,2,1,0:T(8,128)(2,1)S(1)}, bf16[2,2,144,128]{3,2,1,0:T(8,128)(2,1)S(1)}, u32[]{:S(2)}, u32[]{:S(2)}) %collective-permute-start.1) | collective-permute-done | bytes 147488 | tf_op jit(solution)/shard_map/ppermute | solution.py:205
  27.8 1.8 %all-to-all-done = bf16[8,192,128]{2,1,0:T(8,128)(2,1)S(1)} async-done(((bf16[8,192,128]{2,1,0:T(8,128)(2,1)}), bf16[8,192,128]{2,1,0:T(8,128)(2,1)S(1)}, u32[]{:S(2)}, u32[]{:S(2)}) %all-to-all-start) | async-done | bytes 393248 | tf_op jit(solution)/shard_map/all_to_all | solution.py:208
  29.6 2.8 %collective-permute-start.6 = (bf16[16,64,128]{2,1,0:T(8,128)(2,1)S(1)}, bf16[16,64,128]{2,1,0:T(8,128)(2,1)S(1)}, u32[]{:S(2)}, u32[]{:S(2)}) collective-permute-start(bf16[16,64,128]{2,1,0:T(8,128)(2,1)S(1)} %slice.3.a0), channel_id=1, source_target_pairs={{0,12},{4,0},{8,4},{12,8},{1,13},{5,1},{9,5},{13,9},{2,14},{6,2},{... | collective-permute-start | bytes 786440 | tf_op jit(solution)/shard_map/ppermute | solution.py:205
  32.4 0.3 collective-permute-start.5
  32.7 0.7 %collective-permute-start.4 = (bf16[16,64,128]{2,1,0:T(8,128)(2,1)S(1)}, bf16[16,64,128]{2,1,0:T(8,128)(2,1)S(1)}, u32[]{:S(2)}, u32[]{:S(2)}) collective-permute-start(bf16[16,64,128]{2,1,0:T(8,128)(2,1)S(1)} %slice.3.a0), channel_id=1, source_target_pairs={{0,4},{4,8},{8,12},{12,0},{1,5},{5,9},{9,13},{13,1},{2,6},{6,10},{... | collective-permute-start | bytes 786440 | tf_op jit(solution)/shard_map/ppermute | solution.py:205
  33.4 0.0 copy-done.6
  33.4 2.4 %parent.1 = bf16[64,1280]{1,0:T(8,128)(2,1)S(1)} custom-call(s32[64]{0:T(128)S(1)} %copy-done.7, s32[256]{0:T(256)S(1)} %copy-done.6, bf16[16,96,128]{2,1,0:T(8,128)(2,1)S(1)} %bitcast.4, bf16[2,2,144,128]{3,2,1,0:T(8,128)(2,1)S(1)} %get-tuple-element.12.kv0, bf16[2,2,144,128]{3,2,1,0:T(8,128)(2,1)S(1)} %collective-permute-done.1.kv1, ...), custom_call_target="tpu_custom_call" | custom-call | flops 1000000000 | bytes 2000000 | tf_op jit(solution)/shard_map/parent/pallas_call | solution.py:212
  35.8 0.0 copy-start
  35.8 0.7 %reshape.14 = bf16[64,2,640]{2,1,0:T(2,128)(2,1)} reshape(bf16[64,1280]{1,0:T(8,128)(2,1)S(1)} %parent.1) | data formatting | bytes 327680 | tf_op jit(solution)/shard_map/reshape | solution.py:227
  36.5 9.8 %all-to-all-start.1 = ((bf16[64,2,640]{2,1,0:T(2,128)(2,1)}), bf16[64,2,640]{2,1,0:T(2,128)(2,1)S(1)}, u32[]{:S(2)}, u32[]{:S(2)}) async-start(bf16[64,2,640]{2,1,0:T(2,128)(2,1)} %reshape.14), calls=%async_computation.1 | async-start | bytes 327680 | tf_op jit(solution)/shard_map/all_to_all | solution.py:228
  46.4 0.0 collective-permute-done.6.a3
  46.4 0.0 collective-permute-done.5.a2
  46.4 0.0 collective-permute-done.4.a1
  46.4 0.0 copy-done
  46.4 0.0 copy-done.8
  46.4 6.1 %context.1 = bf16[128,2048]{1,0:T(8,128)(2,1)} custom-call(s32[64]{0:T(128)S(1)} %copy-done.7, s32[8]{0:T(128)S(1)} %copy-done.8, bf16[128,2048]{1,0:T(8,128)(2,1)S(1)} %copy-done, bf16[128,256]{1,0:T(8,128)(2,1)S(1)} %copy-done.1, bf16[128,256]{1,0:T(8,128)(2,1)S(1)} %copy-done.2, bf16[16,64,128]{2,1,0:T(8,128)(2,1)S(1)} %slice.3.a0, ...), custom_call_target="tpu_custom_call" | custom-call | flops 60000002048 | bytes 4000000 | tf_op jit(solution)/shard_map/context/pallas_call | solution.py:229
  52.5 5.5 %all-to-all-done.1 = bf16[64,2,640]{2,1,0:T(2,128)(2,1)S(1)} async-done(((bf16[64,2,640]{2,1,0:T(2,128)(2,1)}), bf16[64,2,640]{2,1,0:T(2,128)(2,1)S(1)}, u32[]{:S(2)}, u32[]{:S(2)}) %all-to-all-start.1) | async-done | bytes 163872 | tf_op jit(solution)/shard_map/all_to_all | solution.py:228
  58.1 0.9 %combine.1 = bf16[1,8192]{1,0:T(2,128)(2,1)} custom-call(bf16[64,1280]{1,0:T(8,128)(2,1)S(1)} %bitcast.5), custom_call_target="tpu_custom_call" | custom-call | tf_op jit(solution)/shard_map/combine/pallas_call | solution.py:242
  (13 shorter events, 0.1 us)
Async XLA Ops:
  0.6 5.3 %copy-start.2 = (bf16[128,256]{1,0:T(8,128)(2,1)S(1)}, bf16[128,256]{1,0:T(8,128)(2,1)}, u32[]{:S(2)}) copy-start(bf16[128,256]{1,0:T(8,128)(2,1)} %cv.5) | copy-start | bytes 196612
  0.6 5.3 %copy-start.1 = (bf16[128,256]{1,0:T(8,128)(2,1)S(1)}, bf16[128,256]{1,0:T(8,128)(2,1)}, u32[]{:S(2)}) copy-start(bf16[128,256]{1,0:T(8,128)(2,1)} %ck.5) | copy-start | bytes 196612
  0.7 5.3 %copy-start.3 = (bf16[4,2048]{1,0:T(4,128)(2,1)S(1)}, bf16[4,2048]{1,0:T(4,128)(2,1)}, u32[]{:S(2)}) copy-start(bf16[4,2048]{1,0:T(4,128)(2,1)} %pq.3) | copy-start | bytes 49156
  0.7 5.3 %copy-start.5 = (bf16[16,256]{1,0:T(8,128)(2,1)S(1)}, bf16[16,256]{1,0:T(8,128)(2,1)}, u32[]{:S(2)}) copy-start(bf16[16,256]{1,0:T(8,128)(2,1)} %av.3) | copy-start | bytes 24580
  0.7 5.3 %copy-start.4 = (bf16[16,256]{1,0:T(8,128)(2,1)S(1)}, bf16[16,256]{1,0:T(8,128)(2,1)}, u32[]{:S(2)}) copy-start(bf16[16,256]{1,0:T(8,128)(2,1)} %ak.3) | copy-start | bytes 24580
  2.3 5.8 %collective-permute-start = (bf16[384,128]{1,0:T(8,128)(2,1)}, bf16[384,128]{1,0:T(8,128)(2,1)S(1)}, u32[]{:S(2)}, u32[]{:S(2)}) collective-permute-start(bf16[384,128]{1,0:T(8,128)(2,1)} %give.1), channel_id=1, source_target_pairs={{0,128},{128,0},{1,129},{129,1},{2,130},{130,2},{3,131},{131,3},{4... | collective-permute-start | bytes 294920 | tf_op jit(solution)/shard_map/ppermute | solution.py:191
  8.9 20.6 %all-to-all-start = ((bf16[8,192,128]{2,1,0:T(8,128)(2,1)}), bf16[8,192,128]{2,1,0:T(8,128)(2,1)S(1)}, u32[]{:S(2)}, u32[]{:S(2)}) async-start(bf16[8,192,128]{2,1,0:T(8,128)(2,1)} %get-tuple-element.9), calls=%async_computation | async-start | bytes 786432 | tf_op jit(solution)/shard_map/all_to_all | solution.py:208
  17.4 5.8 %collective-permute-start.3 = (bf16[2,2,144,128]{3,2,1,0:T(8,128)(2,1)S(1)}, bf16[2,2,144,128]{3,2,1,0:T(8,128)(2,1)S(1)}, u32[]{:S(2)}, u32[]{:S(2)}) collective-permute-start(bf16[2,2,144,128]{3,2,1,0:T(8,128)(2,1)S(1)} %get-tuple-element.12.kv0), channel_id=1, source_target_pairs={{0,12},{4,0},{8,4},{12,8},{1,13},{5,1},{9,5},{13,9},{2,14},{6,2},{... | collective-permute-start | bytes 442376 | tf_op jit(solution)/shard_map/ppermute | solution.py:205
  20.1 5.6 %collective-permute-start.2 = (bf16[2,2,144,128]{3,2,1,0:T(8,128)(2,1)S(1)}, bf16[2,2,144,128]{3,2,1,0:T(8,128)(2,1)S(1)}, u32[]{:S(2)}, u32[]{:S(2)}) collective-permute-start(bf16[2,2,144,128]{3,2,1,0:T(8,128)(2,1)S(1)} %get-tuple-element.12.kv0), channel_id=1, source_target_pairs={{0,8},{4,12},{8,0},{12,4},{1,9},{5,13},{9,1},{13,5},{2,10},{6,14},... | collective-permute-start | bytes 442376 | tf_op jit(solution)/shard_map/ppermute | solution.py:205
  20.4 7.3 %collective-permute-start.1 = (bf16[2,2,144,128]{3,2,1,0:T(8,128)(2,1)S(1)}, bf16[2,2,144,128]{3,2,1,0:T(8,128)(2,1)S(1)}, u32[]{:S(2)}, u32[]{:S(2)}) collective-permute-start(bf16[2,2,144,128]{3,2,1,0:T(8,128)(2,1)S(1)} %get-tuple-element.12.kv0), channel_id=1, source_target_pairs={{0,4},{4,8},{8,12},{12,0},{1,5},{5,9},{9,13},{13,1},{2,6},{6,10},{... | collective-permute-start | bytes 442376 | tf_op jit(solution)/shard_map/ppermute | solution.py:205
  29.5 3.9 %copy-start.6 = (s32[256]{0:T(256)S(1)}, s32[256]{0:T(256)}, u32[]{:S(2)}) copy-start(s32[256]{0:T(256)} %qp.1) | copy-start | bytes 3076
  29.6 3.9 %copy-start.7 = (s32[64]{0:T(128)S(1)}, s32[64]{0:T(128)}, u32[]{:S(2)}) copy-start(s32[64]{0:T(128)} %bos.3) | copy-start | bytes 772
  29.6 16.8 %collective-permute-start.6 = (bf16[16,64,128]{2,1,0:T(8,128)(2,1)S(1)}, bf16[16,64,128]{2,1,0:T(8,128)(2,1)S(1)}, u32[]{:S(2)}, u32[]{:S(2)}) collective-permute-start(bf16[16,64,128]{2,1,0:T(8,128)(2,1)S(1)} %slice.3.a0), channel_id=1, source_target_pairs={{0,12},{4,0},{8,4},{12,8},{1,13},{5,1},{9,5},{13,9},{2,14},{6,2},{... | collective-permute-start | bytes 786440 | tf_op jit(solution)/shard_map/ppermute | solution.py:205
  32.4 14.0 %collective-permute-start.5 = (bf16[16,64,128]{2,1,0:T(8,128)(2,1)S(1)}, bf16[16,64,128]{2,1,0:T(8,128)(2,1)S(1)}, u32[]{:S(2)}, u32[]{:S(2)}) collective-permute-start(bf16[16,64,128]{2,1,0:T(8,128)(2,1)S(1)} %slice.3.a0), channel_id=1, source_target_pairs={{0,8},{4,12},{8,0},{12,4},{1,9},{5,13},{9,1},{13,5},{2,10},{6,14},... | collective-permute-start | bytes 786440 | tf_op jit(solution)/shard_map/ppermute | solution.py:205
  32.7 13.6 %collective-permute-start.4 = (bf16[16,64,128]{2,1,0:T(8,128)(2,1)S(1)}, bf16[16,64,128]{2,1,0:T(8,128)(2,1)S(1)}, u32[]{:S(2)}, u32[]{:S(2)}) collective-permute-start(bf16[16,64,128]{2,1,0:T(8,128)(2,1)S(1)} %slice.3.a0), channel_id=1, source_target_pairs={{0,4},{4,8},{8,12},{12,0},{1,5},{5,9},{9,13},{13,1},{2,6},{6,10},{... | collective-permute-start | bytes 786440 | tf_op jit(solution)/shard_map/ppermute | solution.py:205
  35.8 10.6 %copy-start = (bf16[128,2048]{1,0:T(8,128)(2,1)S(1)}, bf16[128,2048]{1,0:T(8,128)(2,1)}, u32[]{:S(2)}) copy-start(bf16[128,2048]{1,0:T(8,128)(2,1)} %q_ref.1) | copy-start | bytes 1572868
  36.5 9.9 %copy-start.8 = (s32[8]{0:T(128)S(1)}, s32[8]{0:T(128)}, u32[]{:S(2)}) copy-start(s32[8]{0:T(128)} %lens.1) | copy-start | bytes 100
  36.5 21.5 %all-to-all-start.1 = ((bf16[64,2,640]{2,1,0:T(2,128)(2,1)}), bf16[64,2,640]{2,1,0:T(2,128)(2,1)S(1)}, u32[]{:S(2)}, u32[]{:S(2)}) async-start(bf16[64,2,640]{2,1,0:T(2,128)(2,1)} %reshape.14), calls=%async_computation.1 | async-start | bytes 327680 | tf_op jit(solution)/shard_map/all_to_all | solution.py:228

commit v5 on v4

--- a/solution.py
+++ b/solution.py
@@ -25,6 +25,7 @@
 STRIDE = 4 * ANC
 CHUNK = STRIDE + QR * PER
 ROWS = NB * QR
+SPLIT = 2
 LOG2E = 1.4426950408889634
 WIDE = PER * HD + 2 * HD
 SCALE = LOG2E / math.sqrt(HD)
@@ -76,36 +77,38 @@
 
 def parent_kernel(bos, qp, got, kv0, kv1, kv2, kv3, out, keys, vals, qpos, turned):
     x, z, y = lax.axis_index("xh"), lax.axis_index("z"), lax.axis_index("y")
-    masks = []
     for b in range(NB):
         for r in range(QR):
             row = (b * QR + r) * PER
             at = ((b % NX * NZ + b // NX) * NY + y) * QR + r
             qpos[row : row + PER, :] = jnp.full((PER, HD), qp[at], jnp.int32)
-    rows = ROWS * PER
-    lane = lax.broadcasted_iota(jnp.int32, (rows, HD), 1)
+    bases = []
     for i, kv in enumerate((kv0, kv1, kv2, kv3)):
         for k in range(NX):
             at = i * NX + k
             keys[at * TOK : (at + 1) * TOK, :] = kv[k, 0, :TOK, :]
             vals[at * TOK : (at + 1) * TOK, :] = kv[k, 1, :TOK, :]
             owner = x if k == 0 else 1 - x
-            base = bos[(owner * NZ + z) * NY + lax.rem(y + NY - i, NY)] * TOK
-            masks.append(lane + base < qpos[...])
+            bases.append(bos[(owner * NZ + z) * NY + lax.bitwise_xor(y, jnp.int32(i))] * TOK)
             at = NA * TOK + at * ANC
             keys[at : at + ANC, :] = kv[k, 0, TOK:, :]
             vals[at : at + ANC, :] = kv[k, 1, TOK:, :]
-    q = got[:, STRIDE:, :].reshape(rows, HD)
-    s = nt(q, keys[...]) * SCALE
-    s = [s[:, i * HD : (i + 1) * HD] for i in range(KEYS // HD)]
-    s = [jnp.where(v, t, -1e30) for v, t in zip(masks, s)] + s[NA:]
-    m = jnp.max(functools.reduce(jnp.maximum, s), axis=1, keepdims=True)
-    p = [jnp.exp2(v - m) for v in s]
-    total = jnp.sum(sum(p[1:], p[0]), axis=1, keepdims=True)
-    p = jnp.concatenate([v.astype(BF) for v in p], 1)
-    o = jnp.dot(p, vals[...], preferred_element_type=F32)
-    turned[0] = o * (1.0 / total)
-    turned[1] = jnp.broadcast_to(m + jnp.log2(total), (rows, HD))
+    rows = ROWS * PER // SPLIT
+    lane = lax.broadcasted_iota(jnp.int32, (rows, HD), 1)
+    for t in range(SPLIT):
+        mine = slice(t * rows, (t + 1) * rows)
+        reach = qpos[mine, :] - lane
+        q = got[t * NB // SPLIT : (t + 1) * NB // SPLIT, STRIDE:, :].reshape(rows, HD)
+        s = nt(q, keys[...])
+        s = [s[:, i * HD : (i + 1) * HD] for i in range(KEYS // HD)]
+        s = [jnp.where(v < reach, u, -1e30) for v, u in zip(bases, s)] + s[NA:]
+        m = jnp.max(functools.reduce(jnp.maximum, s), axis=1, keepdims=True)
+        p = [jnp.exp2((v - m) * SCALE) for v in s]
+        total = jnp.sum(sum(p[1:], p[0]), axis=1, keepdims=True)
+        p = jnp.concatenate([v.astype(BF) for v in p], 1)
+        o = jnp.dot(p, vals[...], preferred_element_type=F32)
+        turned[0, mine, :] = o * (1.0 / total)
+        turned[1, mine, :] = jnp.broadcast_to(m * SCALE + jnp.log2(total), (rows, HD))
     stats = jnp.zeros((ROWS, HD), F32)
     lanes = lax.broadcasted_iota(jnp.int32, (ROWS, HD), 1)
     for h in range(PER):
@@ -202,7 +205,7 @@
     )(own, other)
 
     def turn(x, shift):
-        return lax.ppermute(x, "y", [(i, (i + shift) % NY) for i in range(NY)])
+        return lax.ppermute(x, "y", [(i, i ^ shift) for i in range(NY)])
 
     kvs = [kv] + [turn(kv, s) for s in (1, 2, 3)]
     got = lax.all_to_all(send, "z", 0, 0, tiled=True).reshape(NB, CHUNK, HD)

time: 59.3 us -> 59.5 us (level)
    all_to_all x1, waiting for transfers between devices: 1.77 us -> 3.85 us  [on_device(): got = lax.all_to_all(send, 'z', 0, 0, tiled=True).reshape(NB, CHUNK, HD)]
    ppermute x6, waiting for transfers between devices: 6.65 us -> 4.94 us  [turn(): return lax.ppermute(x, 'y', [(i, i ^ shift) for i in range(NY)])]
    all_to_all x1, starting transfers between devices: 9.83 us -> 10.7 us  [on_device(): back = lax.all_to_all(part, ('z', 'xh', 'xl', 'c'), 0, 0, tiled=True)]
    ppermute x6, starting transfers between devices: 7.63 us -> 6.91 us  [turn(): return lax.ppermute(x, 'y', [(i, i ^ shift) for i in range(NY)])]
  transfers between devices with their start and end apart: 9 -> 9, of which waited for: 6 -> 5; matrix products, arithmetic and copies ran while one was open for 1% -> 1% of each run, Pallas kernels for 14% -> 14%
where the time goes in v5:
time: 59.5 us; the launch traced here: 59.2 us
  starting transfers between devices  29.6 us (50%)
  waiting for transfers between devices  16.5 us (28%)
  Pallas kernels  11.6 us (19%)
  local copies, waits for them, and re-layouts  0.78 us (1%)
  between operations  0.77 us (1%)
    all_to_all x1, starting transfers between devices, on_device(): back = lax.all_to_all(part, ('z', 'xh', 'xl', 'c'), 0, 0, tiled=True)  10.7 us
    all_to_all x1, starting transfers between devices, on_device(): got = lax.all_to_all(send, 'z', 0, 0, tiled=True).reshape(NB, CHUNK, HD)  8.41 us
    ppermute x6, starting transfers between devices, turn(): return lax.ppermute(x, 'y', [(i, i ^ shift) for i in range(NY)])  6.91 us
    pallas_call x1, Pallas kernels, on_device(): pl.pallas_call(context_kernel, out_shape=jax.ShapeDtypeStruct((TOK, GH *...  6.11 us
    all_to_all x1, waiting for transfers between devices, on_device(): back = lax.all_to_all(part, ('z', 'xh', 'xl', 'c'), 0, 0, tiled=True)  5.52 us
    ppermute x6, waiting for transfers between devices, turn(): return lax.ppermute(x, 'y', [(i, i ^ shift) for i in range(NY)])  4.94 us
    all_to_all x1, waiting for transfers between devices, on_device(): got = lax.all_to_all(send, 'z', 0, 0, tiled=True).reshape(NB, CHUNK, HD)  3.85 us
    ppermute x1, starting transfers between devices, on_device(): other = lax.ppermute(give, 'xh', [(0, 1), (1, 0)])  3.57 us
  transfers between devices with their start and end apart: 9, of which 5 were waited for; matrix products, arithmetic and copies ran while one was open for 1% of the time, Pallas kernels for 14%

profile of v5, /device:TPU:1, one launch (start us, length us, event | category | flops | bytes accessed | tf_op | source)
XLA Modules:
  0.0 59.2 jit_solution(8083205777458247777)
XLA Ops:
  0.6 0.0 copy-start.2
  0.6 0.0 copy-start.1
  0.7 0.0 copy-start.3
  0.7 0.0 copy-start.5
  0.7 0.0 copy-start.4
  0.7 1.7 %give.1 = bf16[384,128]{1,0:T(8,128)(2,1)} custom-call(bf16[16,256]{1,0:T(8,128)(2,1)} %ak.3, bf16[16,256]{1,0:T(8,128)(2,1)} %av.3, bf16[4,2048]{1,0:T(4,128)(2,1)} %pq.3, bf16[128,256]{1,0:T(8,128)(2,1)} %ck.5, bf16[128,256]{1,0:T(8,128)(2,1)} %cv.5), custom_call_target="tpu_custom_call" | custom-call | flops 3000000000 | bytes 1000000 | tf_op jit(solution)/shard_map/give/pallas_call | solution.py:180
  2.3 3.6 %collective-permute-start = (bf16[384,128]{1,0:T(8,128)(2,1)}, bf16[384,128]{1,0:T(8,128)(2,1)S(1)}, u32[]{:S(2)}, u32[]{:S(2)}) collective-permute-start(bf16[384,128]{1,0:T(8,128)(2,1)} %give.1), channel_id=1, source_target_pairs={{0,128},{128,0},{1,129},{129,1},{2,130},{130,2},{3,131},{131,3},{4... | collective-permute-start | bytes 294920 | tf_op jit(solution)/shard_map/ppermute | solution.py:194
  5.9 0.0 copy-done.1
  5.9 0.0 copy-done.5
  6.0 2.1 %collective-permute-done.other = bf16[384,128]{1,0:T(8,128)(2,1)S(1)} collective-permute-done((bf16[384,128]{1,0:T(8,128)(2,1)}, bf16[384,128]{1,0:T(8,128)(2,1)S(1)}, u32[]{:S(2)}, u32[]{:S(2)}) %collective-permute-start) | collective-permute-done | bytes 98336 | tf_op jit(solution)/shard_map/ppermute | solution.py:194
  8.1 0.8 %send.1 = (bf16[8,192,128]{2,1,0:T(8,128)(2,1)}, bf16[2,2,144,128]{3,2,1,0:T(8,128)(2,1)S(1)}) custom-call(bf16[384,128]{1,0:T(8,128)(2,1)S(1)} %own.1, bf16[384,128]{1,0:T(8,128)(2,1)S(1)} %collective-permute-done.other), custom_call_target="tpu_custom_call" | custom-call | tf_op jit(solution)/shard_map/send/pallas_call | solution.py:195
  8.9 8.4 %all-to-all-start = ((bf16[8,192,128]{2,1,0:T(8,128)(2,1)}), bf16[8,192,128]{2,1,0:T(8,128)(2,1)S(1)}, u32[]{:S(2)}, u32[]{:S(2)}) async-start(bf16[8,192,128]{2,1,0:T(8,128)(2,1)} %get-tuple-element.9), calls=%async_computation | async-start | bytes 786432 | tf_op jit(solution)/shard_map/all_to_all | solution.py:211
  17.4 2.7 %collective-permute-start.3 = (bf16[2,2,144,128]{3,2,1,0:T(8,128)(2,1)S(1)}, bf16[2,2,144,128]{3,2,1,0:T(8,128)(2,1)S(1)}, u32[]{:S(2)}, u32[]{:S(2)}) collective-permute-start(bf16[2,2,144,128]{3,2,1,0:T(8,128)(2,1)S(1)} %get-tuple-element.12.kv0), channel_id=1, source_target_pairs={{0,12},{4,8},{8,4},{12,0},{1,13},{5,9},{9,5},{13,1},{2,14},{6,10},... | collective-permute-start | bytes 442376 | tf_op jit(solution)/shard_map/ppermute | solution.py:208
  20.1 0.3 collective-permute-start.2
  20.4 0.3 collective-permute-start.1
  20.8 3.6 %collective-permute-done.3.kv3 = bf16[2,2,144,128]{3,2,1,0:T(8,128)(2,1)S(1)} collective-permute-done((bf16[2,2,144,128]{3,2,1,0:T(8,128)(2,1)S(1)}, bf16[2,2,144,128]{3,2,1,0:T(8,128)(2,1)S(1)}, u32[]{:S(2)}, u32[]{:S(2)}) %collective-permute-start.3) | collective-permute-done | bytes 147488 | tf_op jit(solution)/shard_map/ppermute | solution.py:208
  24.3 1.4 %collective-permute-done.2.kv2 = bf16[2,2,144,128]{3,2,1,0:T(8,128)(2,1)S(1)} collective-permute-done((bf16[2,2,144,128]{3,2,1,0:T(8,128)(2,1)S(1)}, bf16[2,2,144,128]{3,2,1,0:T(8,128)(2,1)S(1)}, u32[]{:S(2)}, u32[]{:S(2)}) %collective-permute-start.2) | collective-permute-done | bytes 147488 | tf_op jit(solution)/shard_map/ppermute | solution.py:208
  25.7 0.0 collective-permute-done.1.kv1
  25.7 3.9 %all-to-all-done = bf16[8,192,128]{2,1,0:T(8,128)(2,1)S(1)} async-done(((bf16[8,192,128]{2,1,0:T(8,128)(2,1)}), bf16[8,192,128]{2,1,0:T(8,128)(2,1)S(1)}, u32[]{:S(2)}, u32[]{:S(2)}) %all-to-all-start) | async-done | bytes 393248 | tf_op jit(solution)/shard_map/all_to_all | solution.py:211
  29.6 2.8 %collective-permute-start.6 = (bf16[16,64,128]{2,1,0:T(8,128)(2,1)S(1)}, bf16[16,64,128]{2,1,0:T(8,128)(2,1)S(1)}, u32[]{:S(2)}, u32[]{:S(2)}) collective-permute-start(bf16[16,64,128]{2,1,0:T(8,128)(2,1)S(1)} %slice.3.a0), channel_id=1, source_target_pairs={{0,12},{4,8},{8,4},{12,0},{1,13},{5,9},{9,5},{13,1},{2,14},{6,10},... | collective-permute-start | bytes 786440 | tf_op jit(solution)/shard_map/ppermute | solution.py:208
  32.4 0.3 collective-permute-start.5
  32.7 0.3 collective-permute-start.4
  33.1 2.1 %parent.1 = bf16[64,1280]{1,0:T(8,128)(2,1)S(1)} custom-call(s32[64]{0:T(128)S(1)} %copy-done.7, s32[256]{0:T(256)S(1)} %copy-done.6, bf16[16,96,128]{2,1,0:T(8,128)(2,1)S(1)} %bitcast.4, bf16[2,2,144,128]{3,2,1,0:T(8,128)(2,1)S(1)} %get-tuple-element.12.kv0, bf16[2,2,144,128]{3,2,1,0:T(8,128)(2,1)S(1)} %collective-permute-done.1.kv1, ...), custom_call_target="tpu_custom_call" | custom-call | flops 1000000000 | bytes 2000000 | tf_op jit(solution)/shard_map/parent/pallas_call | solution.py:215
  35.1 0.0 copy-start
  35.2 0.7 %reshape.14 = bf16[64,2,640]{2,1,0:T(2,128)(2,1)} reshape(bf16[64,1280]{1,0:T(8,128)(2,1)S(1)} %parent.1) | data formatting | bytes 327680 | tf_op jit(solution)/shard_map/reshape | solution.py:230
  35.9 10.7 %all-to-all-start.1 = ((bf16[64,2,640]{2,1,0:T(2,128)(2,1)}), bf16[64,2,640]{2,1,0:T(2,128)(2,1)S(1)}, u32[]{:S(2)}, u32[]{:S(2)}) async-start(bf16[64,2,640]{2,1,0:T(2,128)(2,1)} %reshape.14), calls=%async_computation.1 | async-start | bytes 327680 | tf_op jit(solution)/shard_map/all_to_all | solution.py:231
  46.6 0.0 collective-permute-done.6.a3
  46.6 0.0 collective-permute-done.5.a2
  46.6 0.0 collective-permute-done.4.a1
  46.6 6.1 %context.1 = bf16[128,2048]{1,0:T(8,128)(2,1)} custom-call(s32[64]{0:T(128)S(1)} %copy-done.7, s32[8]{0:T(128)S(1)} %copy-done.8, bf16[128,2048]{1,0:T(8,128)(2,1)S(1)} %copy-done, bf16[128,256]{1,0:T(8,128)(2,1)S(1)} %copy-done.1, bf16[128,256]{1,0:T(8,128)(2,1)S(1)} %copy-done.2, bf16[16,64,128]{2,1,0:T(8,128)(2,1)S(1)} %slice.3.a0, ...), custom_call_target="tpu_custom_call" | custom-call | flops 60000002048 | bytes 4000000 | tf_op jit(solution)/shard_map/context/pallas_call | solution.py:232
  52.7 5.5 %all-to-all-done.1 = bf16[64,2,640]{2,1,0:T(2,128)(2,1)S(1)} async-done(((bf16[64,2,640]{2,1,0:T(2,128)(2,1)}), bf16[64,2,640]{2,1,0:T(2,128)(2,1)S(1)}, u32[]{:S(2)}, u32[]{:S(2)}) %all-to-all-start.1) | async-done | bytes 163872 | tf_op jit(solution)/shard_map/all_to_all | solution.py:231
  58.3 0.9 %combine.1 = bf16[1,8192]{1,0:T(2,128)(2,1)} custom-call(bf16[64,1280]{1,0:T(8,128)(2,1)S(1)} %bitcast.5), custom_call_target="tpu_custom_call" | custom-call | tf_op jit(solution)/shard_map/combine/pallas_call | solution.py:245
  (13 shorter events, 0.1 us)
Async XLA Ops:
  0.6 5.3 %copy-start.2 = (bf16[128,256]{1,0:T(8,128)(2,1)S(1)}, bf16[128,256]{1,0:T(8,128)(2,1)}, u32[]{:S(2)}) copy-start(bf16[128,256]{1,0:T(8,128)(2,1)} %cv.5) | copy-start | bytes 196612
  0.6 5.3 %copy-start.1 = (bf16[128,256]{1,0:T(8,128)(2,1)S(1)}, bf16[128,256]{1,0:T(8,128)(2,1)}, u32[]{:S(2)}) copy-start(bf16[128,256]{1,0:T(8,128)(2,1)} %ck.5) | copy-start | bytes 196612
  0.7 5.3 %copy-start.3 = (bf16[4,2048]{1,0:T(4,128)(2,1)S(1)}, bf16[4,2048]{1,0:T(4,128)(2,1)}, u32[]{:S(2)}) copy-start(bf16[4,2048]{1,0:T(4,128)(2,1)} %pq.3) | copy-start | bytes 49156
  0.7 5.3 %copy-start.5 = (bf16[16,256]{1,0:T(8,128)(2,1)S(1)}, bf16[16,256]{1,0:T(8,128)(2,1)}, u32[]{:S(2)}) copy-start(bf16[16,256]{1,0:T(8,128)(2,1)} %av.3) | copy-start | bytes 24580
  0.7 5.3 %copy-start.4 = (bf16[16,256]{1,0:T(8,128)(2,1)S(1)}, bf16[16,256]{1,0:T(8,128)(2,1)}, u32[]{:S(2)}) copy-start(bf16[16,256]{1,0:T(8,128)(2,1)} %ak.3) | copy-start | bytes 24580
  2.3 5.8 %collective-permute-start = (bf16[384,128]{1,0:T(8,128)(2,1)}, bf16[384,128]{1,0:T(8,128)(2,1)S(1)}, u32[]{:S(2)}, u32[]{:S(2)}) collective-permute-start(bf16[384,128]{1,0:T(8,128)(2,1)} %give.1), channel_id=1, source_target_pairs={{0,128},{128,0},{1,129},{129,1},{2,130},{130,2},{3,131},{131,3},{4... | collective-permute-start | bytes 294920 | tf_op jit(solution)/shard_map/ppermute | solution.py:194
  8.9 20.6 %all-to-all-start = ((bf16[8,192,128]{2,1,0:T(8,128)(2,1)}), bf16[8,192,128]{2,1,0:T(8,128)(2,1)S(1)}, u32[]{:S(2)}, u32[]{:S(2)}) async-start(bf16[8,192,128]{2,1,0:T(8,128)(2,1)} %get-tuple-element.9), calls=%async_computation | async-start | bytes 786432 | tf_op jit(solution)/shard_map/all_to_all | solution.py:211
  17.4 7.0 %collective-permute-start.3 = (bf16[2,2,144,128]{3,2,1,0:T(8,128)(2,1)S(1)}, bf16[2,2,144,128]{3,2,1,0:T(8,128)(2,1)S(1)}, u32[]{:S(2)}, u32[]{:S(2)}) collective-permute-start(bf16[2,2,144,128]{3,2,1,0:T(8,128)(2,1)S(1)} %get-tuple-element.12.kv0), channel_id=1, source_target_pairs={{0,12},{4,8},{8,4},{12,0},{1,13},{5,9},{9,5},{13,1},{2,14},{6,10},... | collective-permute-start | bytes 442376 | tf_op jit(solution)/shard_map/ppermute | solution.py:208
  20.1 5.6 %collective-permute-start.2 = (bf16[2,2,144,128]{3,2,1,0:T(8,128)(2,1)S(1)}, bf16[2,2,144,128]{3,2,1,0:T(8,128)(2,1)S(1)}, u32[]{:S(2)}, u32[]{:S(2)}) collective-permute-start(bf16[2,2,144,128]{3,2,1,0:T(8,128)(2,1)S(1)} %get-tuple-element.12.kv0), channel_id=1, source_target_pairs={{0,8},{4,12},{8,0},{12,4},{1,9},{5,13},{9,1},{13,5},{2,10},{6,14},... | collective-permute-start | bytes 442376 | tf_op jit(solution)/shard_map/ppermute | solution.py:208
  20.4 5.3 %collective-permute-start.1 = (bf16[2,2,144,128]{3,2,1,0:T(8,128)(2,1)S(1)}, bf16[2,2,144,128]{3,2,1,0:T(8,128)(2,1)S(1)}, u32[]{:S(2)}, u32[]{:S(2)}) collective-permute-start(bf16[2,2,144,128]{3,2,1,0:T(8,128)(2,1)S(1)} %get-tuple-element.12.kv0), channel_id=1, source_target_pairs={{0,4},{4,0},{8,12},{12,8},{1,5},{5,1},{9,13},{13,9},{2,6},{6,2},{1... | collective-permute-start | bytes 442376 | tf_op jit(solution)/shard_map/ppermute | solution.py:208
  29.5 3.5 %copy-start.6 = (s32[256]{0:T(256)S(1)}, s32[256]{0:T(256)}, u32[]{:S(2)}) copy-start(s32[256]{0:T(256)} %qp.1) | copy-start | bytes 3076
  29.6 3.5 %copy-start.7 = (s32[64]{0:T(128)S(1)}, s32[64]{0:T(128)}, u32[]{:S(2)}) copy-start(s32[64]{0:T(128)} %bos.3) | copy-start | bytes 772
  29.6 17.0 %collective-permute-start.6 = (bf16[16,64,128]{2,1,0:T(8,128)(2,1)S(1)}, bf16[16,64,128]{2,1,0:T(8,128)(2,1)S(1)}, u32[]{:S(2)}, u32[]{:S(2)}) collective-permute-start(bf16[16,64,128]{2,1,0:T(8,128)(2,1)S(1)} %slice.3.a0), channel_id=1, source_target_pairs={{0,12},{4,8},{8,4},{12,0},{1,13},{5,9},{9,5},{13,1},{2,14},{6,10},... | collective-permute-start | bytes 786440 | tf_op jit(solution)/shard_map/ppermute | solution.py:208
  32.4 14.2 %collective-permute-start.5 = (bf16[16,64,128]{2,1,0:T(8,128)(2,1)S(1)}, bf16[16,64,128]{2,1,0:T(8,128)(2,1)S(1)}, u32[]{:S(2)}, u32[]{:S(2)}) collective-permute-start(bf16[16,64,128]{2,1,0:T(8,128)(2,1)S(1)} %slice.3.a0), channel_id=1, source_target_pairs={{0,8},{4,12},{8,0},{12,4},{1,9},{5,13},{9,1},{13,5},{2,10},{6,14},... | collective-permute-start | bytes 786440 | tf_op jit(solution)/shard_map/ppermute | solution.py:208
  32.7 13.9 %collective-permute-start.4 = (bf16[16,64,128]{2,1,0:T(8,128)(2,1)S(1)}, bf16[16,64,128]{2,1,0:T(8,128)(2,1)S(1)}, u32[]{:S(2)}, u32[]{:S(2)}) collective-permute-start(bf16[16,64,128]{2,1,0:T(8,128)(2,1)S(1)} %slice.3.a0), channel_id=1, source_target_pairs={{0,4},{4,0},{8,12},{12,8},{1,5},{5,1},{9,13},{13,9},{2,6},{6,2},{1... | collective-permute-start | bytes 786440 | tf_op jit(solution)/shard_map/ppermute | solution.py:208
  35.1 11.5 %copy-start = (bf16[128,2048]{1,0:T(8,128)(2,1)S(1)}, bf16[128,2048]{1,0:T(8,128)(2,1)}, u32[]{:S(2)}) copy-start(bf16[128,2048]{1,0:T(8,128)(2,1)} %q_ref.1) | copy-start | bytes 1572868
  35.9 10.8 %copy-start.8 = (s32[8]{0:T(128)S(1)}, s32[8]{0:T(128)}, u32[]{:S(2)}) copy-start(s32[8]{0:T(128)} %lens.1) | copy-start | bytes 100
  35.9 22.4 %all-to-all-start.1 = ((bf16[64,2,640]{2,1,0:T(2,128)(2,1)}), bf16[64,2,640]{2,1,0:T(2,128)(2,1)S(1)}, u32[]{:S(2)}, u32[]{:S(2)}) async-start(bf16[64,2,640]{2,1,0:T(2,128)(2,1)} %reshape.14), calls=%async_computation.1 | async-start | bytes 327680 | tf_op jit(solution)/shard_map/all_to_all | solution.py:231

commit v6 on v5

--- a/solution.py
+++ b/solution.py
@@ -44,14 +44,12 @@
 
 
 def half_kernel(mine, ak, av, pq, ck, cv, out, scr):
-    q = pq[...].astype(F32)
-    for g in range(GROUPS):
-        for r in range(QR):
-            for h in range(PER):
-                col = (g * PER + h) * HD
-                row = (g * QR + r) * PER + h
-                scr[row : row + 1, :] = q[r : r + 1, col : col + HD]
     low = lax.axis_index("xh") == (0 if mine else 1)
+    q = jnp.where(low, pq[:, : PER * HD], pq[:, PER * HD :]).astype(F32)
+    for r in range(QR):
+        for h in range(PER):
+            row = r * PER + h
+            scr[row : row + 1, :] = q[r : r + 1, h * HD : (h + 1) * HD]
     at = 0
     for ctx, anc in ((ck, ak), (cv, av)):
         for src in (ctx, anc):
@@ -60,8 +58,7 @@
     for part in (ak[:, :HD], ak[:, HD:], av[:, :HD], av[:, HD:]):
         out[at : at + ANC, :] = part
         at = at + ANC
-    q = jnp.where(low, scr[: QR * PER, :], scr[QR * PER :, :])
-    out[at:, :] = q.astype(BF)
+    out[at:, :] = scr[...].astype(BF)
 
 
 def send_kernel(own, other, send, kv):
@@ -182,7 +179,7 @@
             out_shape=half,
             in_specs=[VMEM] * 5,
             out_specs=VMEM,
-            scratch_shapes=[pltpu.VMEM((GROUPS * QR * PER, HD), F32)],
+            scratch_shapes=[pltpu.VMEM((QR * PER, HD), F32)],
             compiler_params=params(40 if mine else 60),
             cost_estimate=pl.CostEstimate(
                 flops=3 * 10**9, bytes_accessed=10**6, transcendentals=0

time: 59.5 us -> 59.5 us (level)
  no operation moved by 1% of the time
where the time goes in v6:
time: 59.5 us; the launch traced here: 59.2 us
  starting transfers between devices  29.6 us (50%)
  waiting for transfers between devices  16.5 us (28%)
  Pallas kernels  11.6 us (19%)
  local copies, waits for them, and re-layouts  0.78 us (1%)
  between operations  0.77 us (1%)
    all_to_all x1, starting transfers between devices, on_device(): back = lax.all_to_all(part, ('z', 'xh', 'xl', 'c'), 0, 0, tiled=True)  10.7 us
    all_to_all x1, starting transfers between devices, on_device(): got = lax.all_to_all(send, 'z', 0, 0, tiled=True).reshape(NB, CHUNK, HD)  8.41 us
    ppermute x6, starting transfers between devices, turn(): return lax.ppermute(x, 'y', [(i, i ^ shift) for i in range(NY)])  6.91 us
    pallas_call x1, Pallas kernels, on_device(): pl.pallas_call(context_kernel, out_shape=jax.ShapeDtypeStruct((TOK, GH *...  6.11 us
    all_to_all x1, waiting for transfers between devices, on_device(): back = lax.all_to_all(part, ('z', 'xh', 'xl', 'c'), 0, 0, tiled=True)  5.52 us
    ppermute x6, waiting for transfers between devices, turn(): return lax.ppermute(x, 'y', [(i, i ^ shift) for i in range(NY)])  4.94 us
    all_to_all x1, waiting for transfers between devices, on_device(): got = lax.all_to_all(send, 'z', 0, 0, tiled=True).reshape(NB, CHUNK, HD)  3.85 us
    ppermute x1, starting transfers between devices, on_device(): other = lax.ppermute(give, 'xh', [(0, 1), (1, 0)])  3.57 us
  transfers between devices with their start and end apart: 9, of which 5 were waited for; matrix products, arithmetic and copies ran while one was open for 1% of the time, Pallas kernels for 14%

profile of v6, /device:TPU:1, one launch (start us, length us, event | category | flops | bytes accessed | tf_op | source)
XLA Modules:
  0.0 59.2 jit_solution(3300110909771077338)
XLA Ops:
  0.6 0.0 copy-start.2
  0.6 0.0 copy-start.1
  0.7 0.0 copy-start.3
  0.7 0.0 copy-start.5
  0.7 0.0 copy-start.4
  0.7 1.7 %give.1 = bf16[384,128]{1,0:T(8,128)(2,1)} custom-call(bf16[16,256]{1,0:T(8,128)(2,1)} %ak.3, bf16[16,256]{1,0:T(8,128)(2,1)} %av.3, bf16[4,2048]{1,0:T(4,128)(2,1)} %pq.3, bf16[128,256]{1,0:T(8,128)(2,1)} %ck.5, bf16[128,256]{1,0:T(8,128)(2,1)} %cv.5), custom_call_target="tpu_custom_call" | custom-call | flops 3000000000 | bytes 1000000 | tf_op jit(solution)/shard_map/give/pallas_call | solution.py:177
  2.3 3.6 %collective-permute-start = (bf16[384,128]{1,0:T(8,128)(2,1)}, bf16[384,128]{1,0:T(8,128)(2,1)S(1)}, u32[]{:S(2)}, u32[]{:S(2)}) collective-permute-start(bf16[384,128]{1,0:T(8,128)(2,1)} %give.1), channel_id=1, source_target_pairs={{0,128},{128,0},{1,129},{129,1},{2,130},{130,2},{3,131},{131,3},{4... | collective-permute-start | bytes 294920 | tf_op jit(solution)/shard_map/ppermute | solution.py:191
  5.9 0.0 copy-done.2
  6.0 2.1 %collective-permute-done.other = bf16[384,128]{1,0:T(8,128)(2,1)S(1)} collective-permute-done((bf16[384,128]{1,0:T(8,128)(2,1)}, bf16[384,128]{1,0:T(8,128)(2,1)S(1)}, u32[]{:S(2)}, u32[]{:S(2)}) %collective-permute-start) | collective-permute-done | bytes 98336 | tf_op jit(solution)/shard_map/ppermute | solution.py:191
  8.1 0.8 %send.1 = (bf16[8,192,128]{2,1,0:T(8,128)(2,1)}, bf16[2,2,144,128]{3,2,1,0:T(8,128)(2,1)S(1)}) custom-call(bf16[384,128]{1,0:T(8,128)(2,1)S(1)} %own.1, bf16[384,128]{1,0:T(8,128)(2,1)S(1)} %collective-permute-done.other), custom_call_target="tpu_custom_call" | custom-call | tf_op jit(solution)/shard_map/send/pallas_call | solution.py:192
  8.9 8.4 %all-to-all-start = ((bf16[8,192,128]{2,1,0:T(8,128)(2,1)}), bf16[8,192,128]{2,1,0:T(8,128)(2,1)S(1)}, u32[]{:S(2)}, u32[]{:S(2)}) async-start(bf16[8,192,128]{2,1,0:T(8,128)(2,1)} %get-tuple-element.9), calls=%async_computation | async-start | bytes 786432 | tf_op jit(solution)/shard_map/all_to_all | solution.py:208
  17.3 2.7 %collective-permute-start.3 = (bf16[2,2,144,128]{3,2,1,0:T(8,128)(2,1)S(1)}, bf16[2,2,144,128]{3,2,1,0:T(8,128)(2,1)S(1)}, u32[]{:S(2)}, u32[]{:S(2)}) collective-permute-start(bf16[2,2,144,128]{3,2,1,0:T(8,128)(2,1)S(1)} %get-tuple-element.12.kv0), channel_id=1, source_target_pairs={{0,12},{4,8},{8,4},{12,0},{1,13},{5,9},{9,5},{13,1},{2,14},{6,10},... | collective-permute-start | bytes 442376 | tf_op jit(solution)/shard_map/ppermute | solution.py:205
  20.1 0.3 collective-permute-start.2
  20.4 0.3 collective-permute-start.1
  20.8 3.6 %collective-permute-done.3.kv3 = bf16[2,2,144,128]{3,2,1,0:T(8,128)(2,1)S(1)} collective-permute-done((bf16[2,2,144,128]{3,2,1,0:T(8,128)(2,1)S(1)}, bf16[2,2,144,128]{3,2,1,0:T(8,128)(2,1)S(1)}, u32[]{:S(2)}, u32[]{:S(2)}) %collective-permute-start.3) | collective-permute-done | bytes 147488 | tf_op jit(solution)/shard_map/ppermute | solution.py:205
  24.3 1.4 %collective-permute-done.2.kv2 = bf16[2,2,144,128]{3,2,1,0:T(8,128)(2,1)S(1)} collective-permute-done((bf16[2,2,144,128]{3,2,1,0:T(8,128)(2,1)S(1)}, bf16[2,2,144,128]{3,2,1,0:T(8,128)(2,1)S(1)}, u32[]{:S(2)}, u32[]{:S(2)}) %collective-permute-start.2) | collective-permute-done | bytes 147488 | tf_op jit(solution)/shard_map/ppermute | solution.py:205
  25.7 0.0 collective-permute-done.1.kv1
  25.7 3.9 %all-to-all-done = bf16[8,192,128]{2,1,0:T(8,128)(2,1)S(1)} async-done(((bf16[8,192,128]{2,1,0:T(8,128)(2,1)}), bf16[8,192,128]{2,1,0:T(8,128)(2,1)S(1)}, u32[]{:S(2)}, u32[]{:S(2)}) %all-to-all-start) | async-done | bytes 393248 | tf_op jit(solution)/shard_map/all_to_all | solution.py:208
  29.6 2.8 %collective-permute-start.6 = (bf16[16,64,128]{2,1,0:T(8,128)(2,1)S(1)}, bf16[16,64,128]{2,1,0:T(8,128)(2,1)S(1)}, u32[]{:S(2)}, u32[]{:S(2)}) collective-permute-start(bf16[16,64,128]{2,1,0:T(8,128)(2,1)S(1)} %slice.3.a0), channel_id=1, source_target_pairs={{0,12},{4,8},{8,4},{12,0},{1,13},{5,9},{9,5},{13,1},{2,14},{6,10},... | collective-permute-start | bytes 786440 | tf_op jit(solution)/shard_map/ppermute | solution.py:205
  32.4 0.3 collective-permute-start.5
  32.7 0.3 collective-permute-start.4
  33.1 0.0 copy-done.7
  33.1 2.0 %parent.1 = bf16[64,1280]{1,0:T(8,128)(2,1)S(1)} custom-call(s32[64]{0:T(128)S(1)} %copy-done.7, s32[256]{0:T(256)S(1)} %copy-done.6, bf16[16,96,128]{2,1,0:T(8,128)(2,1)S(1)} %bitcast.4, bf16[2,2,144,128]{3,2,1,0:T(8,128)(2,1)S(1)} %get-tuple-element.12.kv0, bf16[2,2,144,128]{3,2,1,0:T(8,128)(2,1)S(1)} %collective-permute-done.1.kv1, ...), custom_call_target="tpu_custom_call" | custom-call | flops 1000000000 | bytes 2000000 | tf_op jit(solution)/shard_map/parent/pallas_call | solution.py:212
  35.1 0.0 copy-start
  35.1 0.7 %reshape.14 = bf16[64,2,640]{2,1,0:T(2,128)(2,1)} reshape(bf16[64,1280]{1,0:T(8,128)(2,1)S(1)} %parent.1) | data formatting | bytes 327680 | tf_op jit(solution)/shard_map/reshape | solution.py:227
  35.8 10.7 %all-to-all-start.1 = ((bf16[64,2,640]{2,1,0:T(2,128)(2,1)}), bf16[64,2,640]{2,1,0:T(2,128)(2,1)S(1)}, u32[]{:S(2)}, u32[]{:S(2)}) async-start(bf16[64,2,640]{2,1,0:T(2,128)(2,1)} %reshape.14), calls=%async_computation.1 | async-start | bytes 327680 | tf_op jit(solution)/shard_map/all_to_all | solution.py:228
  46.6 0.0 collective-permute-done.6.a3
  46.6 0.0 collective-permute-done.5.a2
  46.6 0.0 collective-permute-done.4.a1
  46.6 6.1 %context.1 = bf16[128,2048]{1,0:T(8,128)(2,1)} custom-call(s32[64]{0:T(128)S(1)} %copy-done.7, s32[8]{0:T(128)S(1)} %copy-done.8, bf16[128,2048]{1,0:T(8,128)(2,1)S(1)} %copy-done, bf16[128,256]{1,0:T(8,128)(2,1)S(1)} %copy-done.1, bf16[128,256]{1,0:T(8,128)(2,1)S(1)} %copy-done.2, bf16[16,64,128]{2,1,0:T(8,128)(2,1)S(1)} %slice.3.a0, ...), custom_call_target="tpu_custom_call" | custom-call | flops 60000002048 | bytes 4000000 | tf_op jit(solution)/shard_map/context/pallas_call | solution.py:229
  52.7 5.5 %all-to-all-done.1 = bf16[64,2,640]{2,1,0:T(2,128)(2,1)S(1)} async-done(((bf16[64,2,640]{2,1,0:T(2,128)(2,1)}), bf16[64,2,640]{2,1,0:T(2,128)(2,1)S(1)}, u32[]{:S(2)}, u32[]{:S(2)}) %all-to-all-start.1) | async-done | bytes 163872 | tf_op jit(solution)/shard_map/all_to_all | solution.py:228
  58.3 0.9 %combine.1 = bf16[1,8192]{1,0:T(2,128)(2,1)} custom-call(bf16[64,1280]{1,0:T(8,128)(2,1)S(1)} %bitcast.5), custom_call_target="tpu_custom_call" | custom-call | tf_op jit(solution)/shard_map/combine/pallas_call | solution.py:242
  (13 shorter events, 0.1 us)
Async XLA Ops:
  0.6 5.3 %copy-start.2 = (bf16[128,256]{1,0:T(8,128)(2,1)S(1)}, bf16[128,256]{1,0:T(8,128)(2,1)}, u32[]{:S(2)}) copy-start(bf16[128,256]{1,0:T(8,128)(2,1)} %cv.5) | copy-start | bytes 196612
  0.6 5.3 %copy-start.1 = (bf16[128,256]{1,0:T(8,128)(2,1)S(1)}, bf16[128,256]{1,0:T(8,128)(2,1)}, u32[]{:S(2)}) copy-start(bf16[128,256]{1,0:T(8,128)(2,1)} %ck.5) | copy-start | bytes 196612
  0.7 5.3 %copy-start.3 = (bf16[4,2048]{1,0:T(4,128)(2,1)S(1)}, bf16[4,2048]{1,0:T(4,128)(2,1)}, u32[]{:S(2)}) copy-start(bf16[4,2048]{1,0:T(4,128)(2,1)} %pq.3) | copy-start | bytes 49156
  0.7 5.3 %copy-start.5 = (bf16[16,256]{1,0:T(8,128)(2,1)S(1)}, bf16[16,256]{1,0:T(8,128)(2,1)}, u32[]{:S(2)}) copy-start(bf16[16,256]{1,0:T(8,128)(2,1)} %av.3) | copy-start | bytes 24580
  0.7 5.3 %copy-start.4 = (bf16[16,256]{1,0:T(8,128)(2,1)S(1)}, bf16[16,256]{1,0:T(8,128)(2,1)}, u32[]{:S(2)}) copy-start(bf16[16,256]{1,0:T(8,128)(2,1)} %ak.3) | copy-start | bytes 24580
  2.3 5.8 %collective-permute-start = (bf16[384,128]{1,0:T(8,128)(2,1)}, bf16[384,128]{1,0:T(8,128)(2,1)S(1)}, u32[]{:S(2)}, u32[]{:S(2)}) collective-permute-start(bf16[384,128]{1,0:T(8,128)(2,1)} %give.1), channel_id=1, source_target_pairs={{0,128},{128,0},{1,129},{129,1},{2,130},{130,2},{3,131},{131,3},{4... | collective-permute-start | bytes 294920 | tf_op jit(solution)/shard_map/ppermute | solution.py:191
  8.9 20.6 %all-to-all-start = ((bf16[8,192,128]{2,1,0:T(8,128)(2,1)}), bf16[8,192,128]{2,1,0:T(8,128)(2,1)S(1)}, u32[]{:S(2)}, u32[]{:S(2)}) async-start(bf16[8,192,128]{2,1,0:T(8,128)(2,1)} %get-tuple-element.9), calls=%async_computation | async-start | bytes 786432 | tf_op jit(solution)/shard_map/all_to_all | solution.py:208
  17.3 7.0 %collective-permute-start.3 = (bf16[2,2,144,128]{3,2,1,0:T(8,128)(2,1)S(1)}, bf16[2,2,144,128]{3,2,1,0:T(8,128)(2,1)S(1)}, u32[]{:S(2)}, u32[]{:S(2)}) collective-permute-start(bf16[2,2,144,128]{3,2,1,0:T(8,128)(2,1)S(1)} %get-tuple-element.12.kv0), channel_id=1, source_target_pairs={{0,12},{4,8},{8,4},{12,0},{1,13},{5,9},{9,5},{13,1},{2,14},{6,10},... | collective-permute-start | bytes 442376 | tf_op jit(solution)/shard_map/ppermute | solution.py:205
  20.1 5.6 %collective-permute-start.2 = (bf16[2,2,144,128]{3,2,1,0:T(8,128)(2,1)S(1)}, bf16[2,2,144,128]{3,2,1,0:T(8,128)(2,1)S(1)}, u32[]{:S(2)}, u32[]{:S(2)}) collective-permute-start(bf16[2,2,144,128]{3,2,1,0:T(8,128)(2,1)S(1)} %get-tuple-element.12.kv0), channel_id=1, source_target_pairs={{0,8},{4,12},{8,0},{12,4},{1,9},{5,13},{9,1},{13,5},{2,10},{6,14},... | collective-permute-start | bytes 442376 | tf_op jit(solution)/shard_map/ppermute | solution.py:205
  20.4 5.3 %collective-permute-start.1 = (bf16[2,2,144,128]{3,2,1,0:T(8,128)(2,1)S(1)}, bf16[2,2,144,128]{3,2,1,0:T(8,128)(2,1)S(1)}, u32[]{:S(2)}, u32[]{:S(2)}) collective-permute-start(bf16[2,2,144,128]{3,2,1,0:T(8,128)(2,1)S(1)} %get-tuple-element.12.kv0), channel_id=1, source_target_pairs={{0,4},{4,0},{8,12},{12,8},{1,5},{5,1},{9,13},{13,9},{2,6},{6,2},{1... | collective-permute-start | bytes 442376 | tf_op jit(solution)/shard_map/ppermute | solution.py:205
  29.5 3.5 %copy-start.6 = (s32[256]{0:T(256)S(1)}, s32[256]{0:T(256)}, u32[]{:S(2)}) copy-start(s32[256]{0:T(256)} %qp.1) | copy-start | bytes 3076
  29.5 3.5 %copy-start.7 = (s32[64]{0:T(128)S(1)}, s32[64]{0:T(128)}, u32[]{:S(2)}) copy-start(s32[64]{0:T(128)} %bos.3) | copy-start | bytes 772
  29.6 17.0 %collective-permute-start.6 = (bf16[16,64,128]{2,1,0:T(8,128)(2,1)S(1)}, bf16[16,64,128]{2,1,0:T(8,128)(2,1)S(1)}, u32[]{:S(2)}, u32[]{:S(2)}) collective-permute-start(bf16[16,64,128]{2,1,0:T(8,128)(2,1)S(1)} %slice.3.a0), channel_id=1, source_target_pairs={{0,12},{4,8},{8,4},{12,0},{1,13},{5,9},{9,5},{13,1},{2,14},{6,10},... | collective-permute-start | bytes 786440 | tf_op jit(solution)/shard_map/ppermute | solution.py:205
  32.4 14.2 %collective-permute-start.5 = (bf16[16,64,128]{2,1,0:T(8,128)(2,1)S(1)}, bf16[16,64,128]{2,1,0:T(8,128)(2,1)S(1)}, u32[]{:S(2)}, u32[]{:S(2)}) collective-permute-start(bf16[16,64,128]{2,1,0:T(8,128)(2,1)S(1)} %slice.3.a0), channel_id=1, source_target_pairs={{0,8},{4,12},{8,0},{12,4},{1,9},{5,13},{9,1},{13,5},{2,10},{6,14},... | collective-permute-start | bytes 786440 | tf_op jit(solution)/shard_map/ppermute | solution.py:205
  32.7 13.9 %collective-permute-start.4 = (bf16[16,64,128]{2,1,0:T(8,128)(2,1)S(1)}, bf16[16,64,128]{2,1,0:T(8,128)(2,1)S(1)}, u32[]{:S(2)}, u32[]{:S(2)}) collective-permute-start(bf16[16,64,128]{2,1,0:T(8,128)(2,1)S(1)} %slice.3.a0), channel_id=1, source_target_pairs={{0,4},{4,0},{8,12},{12,8},{1,5},{5,1},{9,13},{13,9},{2,6},{6,2},{1... | collective-permute-start | bytes 786440 | tf_op jit(solution)/shard_map/ppermute | solution.py:205
  35.1 11.5 %copy-start = (bf16[128,2048]{1,0:T(8,128)(2,1)S(1)}, bf16[128,2048]{1,0:T(8,128)(2,1)}, u32[]{:S(2)}) copy-start(bf16[128,2048]{1,0:T(8,128)(2,1)} %q_ref.1) | copy-start | bytes 1572868
  35.8 10.8 %copy-start.8 = (s32[8]{0:T(128)S(1)}, s32[8]{0:T(128)}, u32[]{:S(2)}) copy-start(s32[8]{0:T(128)} %lens.1) | copy-start | bytes 100
  35.8 22.4 %all-to-all-start.1 = ((bf16[64,2,640]{2,1,0:T(2,128)(2,1)}), bf16[64,2,640]{2,1,0:T(2,128)(2,1)S(1)}, u32[]{:S(2)}, u32[]{:S(2)}) async-start(bf16[64,2,640]{2,1,0:T(2,128)(2,1)} %reshape.14), calls=%async_computation.1 | async-start | bytes 327680 | tf_op jit(solution)/shard_map/all_to_all | solution.py:228

commit v7 on v6

--- a/solution.py
+++ b/solution.py
@@ -86,7 +86,7 @@
             keys[at * TOK : (at + 1) * TOK, :] = kv[k, 0, :TOK, :]
             vals[at * TOK : (at + 1) * TOK, :] = kv[k, 1, :TOK, :]
             owner = x if k == 0 else 1 - x
-            bases.append(bos[(owner * NZ + z) * NY + lax.bitwise_xor(y, jnp.int32(i))] * TOK)
+            bases.append(bos[(owner * NZ + z) * NY + lax.rem(y + NY - i, NY)] * TOK)
             at = NA * TOK + at * ANC
             keys[at : at + ANC, :] = kv[k, 0, TOK:, :]
             vals[at : at + ANC, :] = kv[k, 1, TOK:, :]
@@ -202,7 +202,7 @@
     )(own, other)
 
     def turn(x, shift):
-        return lax.ppermute(x, "y", [(i, i ^ shift) for i in range(NY)])
+        return lax.ppermute(x, "y", [(i, (i + shift) % NY) for i in range(NY)])
 
     kvs = [kv] + [turn(kv, s) for s in (1, 2, 3)]
     got = lax.all_to_all(send, "z", 0, 0, tiled=True).reshape(NB, CHUNK, HD)

time: 59.5 us -> 59 us (level)
    all_to_all x1, waiting for transfers between devices: 3.85 us -> 1.77 us  [on_device(): got = lax.all_to_all(send, 'z', 0, 0, tiled=True).reshape(NB, CHUNK, HD)]
    ppermute x6, waiting for transfers between devices: 4.94 us -> 6.77 us  [turn(): return lax.ppermute(x, 'y', [(i, (i + shift) % NY) for i in range(NY)])]
    all_to_all x1, starting transfers between devices: 10.7 us -> 9.83 us  [on_device(): back = lax.all_to_all(part, ('z', 'xh', 'xl', 'c'), 0, 0, tiled=True)]
    ppermute x6, starting transfers between devices: 6.91 us -> 7.63 us  [turn(): return lax.ppermute(x, 'y', [(i, (i + shift) % NY) for i in range(NY)])]
  transfers between devices with their start and end apart: 9 -> 9, of which waited for: 5 -> 7; matrix products, arithmetic and copies ran while one was open for 1% -> 1% of each run, Pallas kernels for 14% -> 14%
where the time goes in v7:
time: 59 us; the launch traced here: 58.6 us
  starting transfers between devices  29.4 us (50%)
  waiting for transfers between devices  16.1 us (27%)
  Pallas kernels  11.6 us (20%)
  local copies, waits for them, and re-layouts  0.78 us (1%)
  between operations  0.75 us (1%)
    all_to_all x1, starting transfers between devices, on_device(): back = lax.all_to_all(part, ('z', 'xh', 'xl', 'c'), 0, 0, tiled=True)  9.83 us
    all_to_all x1, starting transfers between devices, on_device(): got = lax.all_to_all(send, 'z', 0, 0, tiled=True).reshape(NB, CHUNK, HD)  8.41 us
    ppermute x6, starting transfers between devices, turn(): return lax.ppermute(x, 'y', [(i, (i + shift) % NY) for i in range(NY)])  7.63 us
    ppermute x6, waiting for transfers between devices, turn(): return lax.ppermute(x, 'y', [(i, (i + shift) % NY) for i in range(NY)])  6.77 us
    pallas_call x1, Pallas kernels, on_device(): pl.pallas_call(context_kernel, out_shape=jax.ShapeDtypeStruct((TOK, GH *...  6.11 us
    all_to_all x1, waiting for transfers between devices, on_device(): back = lax.all_to_all(part, ('z', 'xh', 'xl', 'c'), 0, 0, tiled=True)  5.42 us
    ppermute x1, starting transfers between devices, on_device(): other = lax.ppermute(give, 'xh', [(0, 1), (1, 0)])  3.57 us
    ppermute x1, waiting for transfers between devices, on_device(): other = lax.ppermute(give, 'xh', [(0, 1), (1, 0)])  2.14 us
  transfers between devices with their start and end apart: 9, of which 7 were waited for; matrix products, arithmetic and copies ran while one was open for 1% of the time, Pallas kernels for 14%

profile of v7, /device:TPU:1, one launch (start us, length us, event | category | flops | bytes accessed | tf_op | source)
XLA Modules:
  0.0 58.6 jit_solution(11447097697522163777)
XLA Ops:
  0.6 0.0 copy-start.2
  0.6 0.0 copy-start.1
  0.7 0.0 copy-start.3
  0.7 0.0 copy-start.5
  0.7 0.0 copy-start.4
  0.7 1.7 %give.1 = bf16[384,128]{1,0:T(8,128)(2,1)} custom-call(bf16[16,256]{1,0:T(8,128)(2,1)} %ak.3, bf16[16,256]{1,0:T(8,128)(2,1)} %av.3, bf16[4,2048]{1,0:T(4,128)(2,1)} %pq.3, bf16[128,256]{1,0:T(8,128)(2,1)} %ck.5, bf16[128,256]{1,0:T(8,128)(2,1)} %cv.5), custom_call_target="tpu_custom_call" | custom-call | flops 3000000000 | bytes 1000000 | tf_op jit(solution)/shard_map/give/pallas_call | solution.py:177
  2.3 3.6 %collective-permute-start = (bf16[384,128]{1,0:T(8,128)(2,1)}, bf16[384,128]{1,0:T(8,128)(2,1)S(1)}, u32[]{:S(2)}, u32[]{:S(2)}) collective-permute-start(bf16[384,128]{1,0:T(8,128)(2,1)} %give.1), channel_id=1, source_target_pairs={{0,128},{128,0},{1,129},{129,1},{2,130},{130,2},{3,131},{131,3},{4... | collective-permute-start | bytes 294920 | tf_op jit(solution)/shard_map/ppermute | solution.py:191
  5.9 0.0 copy-done.2
  5.9 0.0 copy-done.3
  6.0 2.1 %collective-permute-done.other = bf16[384,128]{1,0:T(8,128)(2,1)S(1)} collective-permute-done((bf16[384,128]{1,0:T(8,128)(2,1)}, bf16[384,128]{1,0:T(8,128)(2,1)S(1)}, u32[]{:S(2)}, u32[]{:S(2)}) %collective-permute-start) | collective-permute-done | bytes 98336 | tf_op jit(solution)/shard_map/ppermute | solution.py:191
  8.1 0.8 %send.1 = (bf16[8,192,128]{2,1,0:T(8,128)(2,1)}, bf16[2,2,144,128]{3,2,1,0:T(8,128)(2,1)S(1)}) custom-call(bf16[384,128]{1,0:T(8,128)(2,1)S(1)} %own.1, bf16[384,128]{1,0:T(8,128)(2,1)S(1)} %collective-permute-done.other), custom_call_target="tpu_custom_call" | custom-call | tf_op jit(solution)/shard_map/send/pallas_call | solution.py:192
  8.9 8.4 %all-to-all-start = ((bf16[8,192,128]{2,1,0:T(8,128)(2,1)}), bf16[8,192,128]{2,1,0:T(8,128)(2,1)S(1)}, u32[]{:S(2)}, u32[]{:S(2)}) async-start(bf16[8,192,128]{2,1,0:T(8,128)(2,1)} %get-tuple-element.9), calls=%async_computation | async-start | bytes 786432 | tf_op jit(solution)/shard_map/all_to_all | solution.py:208
  17.3 2.7 %collective-permute-start.3 = (bf16[2,2,144,128]{3,2,1,0:T(8,128)(2,1)S(1)}, bf16[2,2,144,128]{3,2,1,0:T(8,128)(2,1)S(1)}, u32[]{:S(2)}, u32[]{:S(2)}) collective-permute-start(bf16[2,2,144,128]{3,2,1,0:T(8,128)(2,1)S(1)} %get-tuple-element.12.kv0), channel_id=1, source_target_pairs={{0,12},{4,0},{8,4},{12,8},{1,13},{5,1},{9,5},{13,9},{2,14},{6,2},{... | collective-permute-start | bytes 442376 | tf_op jit(solution)/shard_map/ppermute | solution.py:205
  20.1 0.3 collective-permute-start.2
  20.4 0.7 %collective-permute-start.1 = (bf16[2,2,144,128]{3,2,1,0:T(8,128)(2,1)S(1)}, bf16[2,2,144,128]{3,2,1,0:T(8,128)(2,1)S(1)}, u32[]{:S(2)}, u32[]{:S(2)}) collective-permute-start(bf16[2,2,144,128]{3,2,1,0:T(8,128)(2,1)S(1)} %get-tuple-element.12.kv0), channel_id=1, source_target_pairs={{0,4},{4,8},{8,12},{12,0},{1,5},{5,9},{9,13},{13,1},{2,6},{6,10},{... | collective-permute-start | bytes 442376 | tf_op jit(solution)/shard_map/ppermute | solution.py:205
  21.1 2.0 %collective-permute-done.3.kv3 = bf16[2,2,144,128]{3,2,1,0:T(8,128)(2,1)S(1)} collective-permute-done((bf16[2,2,144,128]{3,2,1,0:T(8,128)(2,1)S(1)}, bf16[2,2,144,128]{3,2,1,0:T(8,128)(2,1)S(1)}, u32[]{:S(2)}, u32[]{:S(2)}) %collective-permute-start.3) | collective-permute-done | bytes 147488 | tf_op jit(solution)/shard_map/ppermute | solution.py:205
  23.1 2.6 %collective-permute-done.2.kv2 = bf16[2,2,144,128]{3,2,1,0:T(8,128)(2,1)S(1)} collective-permute-done((bf16[2,2,144,128]{3,2,1,0:T(8,128)(2,1)S(1)}, bf16[2,2,144,128]{3,2,1,0:T(8,128)(2,1)S(1)}, u32[]{:S(2)}, u32[]{:S(2)}) %collective-permute-start.2) | collective-permute-done | bytes 147488 | tf_op jit(solution)/shard_map/ppermute | solution.py:205
  25.7 2.1 %collective-permute-done.1.kv1 = bf16[2,2,144,128]{3,2,1,0:T(8,128)(2,1)S(1)} collective-permute-done((bf16[2,2,144,128]{3,2,1,0:T(8,128)(2,1)S(1)}, bf16[2,2,144,128]{3,2,1,0:T(8,128)(2,1)S(1)}, u32[]{:S(2)}, u32[]{:S(2)}) %collective-permute-start.1) | collective-permute-done | bytes 147488 | tf_op jit(solution)/shard_map/ppermute | solution.py:205
  27.8 1.8 %all-to-all-done = bf16[8,192,128]{2,1,0:T(8,128)(2,1)S(1)} async-done(((bf16[8,192,128]{2,1,0:T(8,128)(2,1)}), bf16[8,192,128]{2,1,0:T(8,128)(2,1)S(1)}, u32[]{:S(2)}, u32[]{:S(2)}) %all-to-all-start) | async-done | bytes 393248 | tf_op jit(solution)/shard_map/all_to_all | solution.py:208
  29.6 2.8 %collective-permute-start.6 = (bf16[16,64,128]{2,1,0:T(8,128)(2,1)S(1)}, bf16[16,64,128]{2,1,0:T(8,128)(2,1)S(1)}, u32[]{:S(2)}, u32[]{:S(2)}) collective-permute-start(bf16[16,64,128]{2,1,0:T(8,128)(2,1)S(1)} %slice.3.a0), channel_id=1, source_target_pairs={{0,12},{4,0},{8,4},{12,8},{1,13},{5,1},{9,5},{13,9},{2,14},{6,2},{... | collective-permute-start | bytes 786440 | tf_op jit(solution)/shard_map/ppermute | solution.py:205
  32.4 0.3 collective-permute-start.5
  32.7 0.7 %collective-permute-start.4 = (bf16[16,64,128]{2,1,0:T(8,128)(2,1)S(1)}, bf16[16,64,128]{2,1,0:T(8,128)(2,1)S(1)}, u32[]{:S(2)}, u32[]{:S(2)}) collective-permute-start(bf16[16,64,128]{2,1,0:T(8,128)(2,1)S(1)} %slice.3.a0), channel_id=1, source_target_pairs={{0,4},{4,8},{8,12},{12,0},{1,5},{5,9},{9,13},{13,1},{2,6},{6,10},{... | collective-permute-start | bytes 786440 | tf_op jit(solution)/shard_map/ppermute | solution.py:205
  33.4 2.1 %parent.1 = bf16[64,1280]{1,0:T(8,128)(2,1)S(1)} custom-call(s32[64]{0:T(128)S(1)} %copy-done.7, s32[256]{0:T(256)S(1)} %copy-done.6, bf16[16,96,128]{2,1,0:T(8,128)(2,1)S(1)} %bitcast.4, bf16[2,2,144,128]{3,2,1,0:T(8,128)(2,1)S(1)} %get-tuple-element.12.kv0, bf16[2,2,144,128]{3,2,1,0:T(8,128)(2,1)S(1)} %collective-permute-done.1.kv1, ...), custom_call_target="tpu_custom_call" | custom-call | flops 1000000000 | bytes 2000000 | tf_op jit(solution)/shard_map/parent/pallas_call | solution.py:212
  35.5 0.0 copy-start
  35.5 0.7 %reshape.14 = bf16[64,2,640]{2,1,0:T(2,128)(2,1)} reshape(bf16[64,1280]{1,0:T(8,128)(2,1)S(1)} %parent.1) | data formatting | bytes 327680 | tf_op jit(solution)/shard_map/reshape | solution.py:227
  36.2 9.8 %all-to-all-start.1 = ((bf16[64,2,640]{2,1,0:T(2,128)(2,1)}), bf16[64,2,640]{2,1,0:T(2,128)(2,1)S(1)}, u32[]{:S(2)}, u32[]{:S(2)}) async-start(bf16[64,2,640]{2,1,0:T(2,128)(2,1)} %reshape.14), calls=%async_computation.1 | async-start | bytes 327680 | tf_op jit(solution)/shard_map/all_to_all | solution.py:228
  46.0 0.0 collective-permute-done.6.a3
  46.1 0.0 collective-permute-done.5.a2
  46.1 0.1 collective-permute-done.4.a1
  46.2 6.1 %context.1 = bf16[128,2048]{1,0:T(8,128)(2,1)} custom-call(s32[64]{0:T(128)S(1)} %copy-done.7, s32[8]{0:T(128)S(1)} %copy-done.8, bf16[128,2048]{1,0:T(8,128)(2,1)S(1)} %copy-done, bf16[128,256]{1,0:T(8,128)(2,1)S(1)} %copy-done.1, bf16[128,256]{1,0:T(8,128)(2,1)S(1)} %copy-done.2, bf16[16,64,128]{2,1,0:T(8,128)(2,1)S(1)} %slice.3.a0, ...), custom_call_target="tpu_custom_call" | custom-call | flops 60000002048 | bytes 4000000 | tf_op jit(solution)/shard_map/context/pallas_call | solution.py:229
  52.3 5.4 %all-to-all-done.1 = bf16[64,2,640]{2,1,0:T(2,128)(2,1)S(1)} async-done(((bf16[64,2,640]{2,1,0:T(2,128)(2,1)}), bf16[64,2,640]{2,1,0:T(2,128)(2,1)S(1)}, u32[]{:S(2)}, u32[]{:S(2)}) %all-to-all-start.1) | async-done | bytes 163872 | tf_op jit(solution)/shard_map/all_to_all | solution.py:228
  57.8 0.9 %combine.1 = bf16[1,8192]{1,0:T(2,128)(2,1)} custom-call(bf16[64,1280]{1,0:T(8,128)(2,1)S(1)} %bitcast.5), custom_call_target="tpu_custom_call" | custom-call | tf_op jit(solution)/shard_map/combine/pallas_call | solution.py:242
  (13 shorter events, 0.1 us)
Async XLA Ops:
  0.6 5.3 %copy-start.2 = (bf16[128,256]{1,0:T(8,128)(2,1)S(1)}, bf16[128,256]{1,0:T(8,128)(2,1)}, u32[]{:S(2)}) copy-start(bf16[128,256]{1,0:T(8,128)(2,1)} %cv.5) | copy-start | bytes 196612
  0.6 5.3 %copy-start.1 = (bf16[128,256]{1,0:T(8,128)(2,1)S(1)}, bf16[128,256]{1,0:T(8,128)(2,1)}, u32[]{:S(2)}) copy-start(bf16[128,256]{1,0:T(8,128)(2,1)} %ck.5) | copy-start | bytes 196612
  0.7 5.3 %copy-start.3 = (bf16[4,2048]{1,0:T(4,128)(2,1)S(1)}, bf16[4,2048]{1,0:T(4,128)(2,1)}, u32[]{:S(2)}) copy-start(bf16[4,2048]{1,0:T(4,128)(2,1)} %pq.3) | copy-start | bytes 49156
  0.7 5.3 %copy-start.5 = (bf16[16,256]{1,0:T(8,128)(2,1)S(1)}, bf16[16,256]{1,0:T(8,128)(2,1)}, u32[]{:S(2)}) copy-start(bf16[16,256]{1,0:T(8,128)(2,1)} %av.3) | copy-start | bytes 24580
  0.7 5.3 %copy-start.4 = (bf16[16,256]{1,0:T(8,128)(2,1)S(1)}, bf16[16,256]{1,0:T(8,128)(2,1)}, u32[]{:S(2)}) copy-start(bf16[16,256]{1,0:T(8,128)(2,1)} %ak.3) | copy-start | bytes 24580
  2.3 5.8 %collective-permute-start = (bf16[384,128]{1,0:T(8,128)(2,1)}, bf16[384,128]{1,0:T(8,128)(2,1)S(1)}, u32[]{:S(2)}, u32[]{:S(2)}) collective-permute-start(bf16[384,128]{1,0:T(8,128)(2,1)} %give.1), channel_id=1, source_target_pairs={{0,128},{128,0},{1,129},{129,1},{2,130},{130,2},{3,131},{131,3},{4... | collective-permute-start | bytes 294920 | tf_op jit(solution)/shard_map/ppermute | solution.py:191
  8.9 20.6 %all-to-all-start = ((bf16[8,192,128]{2,1,0:T(8,128)(2,1)}), bf16[8,192,128]{2,1,0:T(8,128)(2,1)S(1)}, u32[]{:S(2)}, u32[]{:S(2)}) async-start(bf16[8,192,128]{2,1,0:T(8,128)(2,1)} %get-tuple-element.9), calls=%async_computation | async-start | bytes 786432 | tf_op jit(solution)/shard_map/all_to_all | solution.py:208
  17.3 5.8 %collective-permute-start.3 = (bf16[2,2,144,128]{3,2,1,0:T(8,128)(2,1)S(1)}, bf16[2,2,144,128]{3,2,1,0:T(8,128)(2,1)S(1)}, u32[]{:S(2)}, u32[]{:S(2)}) collective-permute-start(bf16[2,2,144,128]{3,2,1,0:T(8,128)(2,1)S(1)} %get-tuple-element.12.kv0), channel_id=1, source_target_pairs={{0,12},{4,0},{8,4},{12,8},{1,13},{5,1},{9,5},{13,9},{2,14},{6,2},{... | collective-permute-start | bytes 442376 | tf_op jit(solution)/shard_map/ppermute | solution.py:205
  20.1 5.6 %collective-permute-start.2 = (bf16[2,2,144,128]{3,2,1,0:T(8,128)(2,1)S(1)}, bf16[2,2,144,128]{3,2,1,0:T(8,128)(2,1)S(1)}, u32[]{:S(2)}, u32[]{:S(2)}) collective-permute-start(bf16[2,2,144,128]{3,2,1,0:T(8,128)(2,1)S(1)} %get-tuple-element.12.kv0), channel_id=1, source_target_pairs={{0,8},{4,12},{8,0},{12,4},{1,9},{5,13},{9,1},{13,5},{2,10},{6,14},... | collective-permute-start | bytes 442376 | tf_op jit(solution)/shard_map/ppermute | solution.py:205
  20.4 7.3 %collective-permute-start.1 = (bf16[2,2,144,128]{3,2,1,0:T(8,128)(2,1)S(1)}, bf16[2,2,144,128]{3,2,1,0:T(8,128)(2,1)S(1)}, u32[]{:S(2)}, u32[]{:S(2)}) collective-permute-start(bf16[2,2,144,128]{3,2,1,0:T(8,128)(2,1)S(1)} %get-tuple-element.12.kv0), channel_id=1, source_target_pairs={{0,4},{4,8},{8,12},{12,0},{1,5},{5,9},{9,13},{13,1},{2,6},{6,10},{... | collective-permute-start | bytes 442376 | tf_op jit(solution)/shard_map/ppermute | solution.py:205
  29.5 3.9 %copy-start.6 = (s32[256]{0:T(256)S(1)}, s32[256]{0:T(256)}, u32[]{:S(2)}) copy-start(s32[256]{0:T(256)} %qp.1) | copy-start | bytes 3076
  29.5 3.9 %copy-start.7 = (s32[64]{0:T(128)S(1)}, s32[64]{0:T(128)}, u32[]{:S(2)}) copy-start(s32[64]{0:T(128)} %bos.3) | copy-start | bytes 772
  29.6 16.5 %collective-permute-start.6 = (bf16[16,64,128]{2,1,0:T(8,128)(2,1)S(1)}, bf16[16,64,128]{2,1,0:T(8,128)(2,1)S(1)}, u32[]{:S(2)}, u32[]{:S(2)}) collective-permute-start(bf16[16,64,128]{2,1,0:T(8,128)(2,1)S(1)} %slice.3.a0), channel_id=1, source_target_pairs={{0,12},{4,0},{8,4},{12,8},{1,13},{5,1},{9,5},{13,9},{2,14},{6,2},{... | collective-permute-start | bytes 786440 | tf_op jit(solution)/shard_map/ppermute | solution.py:205
  32.4 13.7 %collective-permute-start.5 = (bf16[16,64,128]{2,1,0:T(8,128)(2,1)S(1)}, bf16[16,64,128]{2,1,0:T(8,128)(2,1)S(1)}, u32[]{:S(2)}, u32[]{:S(2)}) collective-permute-start(bf16[16,64,128]{2,1,0:T(8,128)(2,1)S(1)} %slice.3.a0), channel_id=1, source_target_pairs={{0,8},{4,12},{8,0},{12,4},{1,9},{5,13},{9,1},{13,5},{2,10},{6,14},... | collective-permute-start | bytes 786440 | tf_op jit(solution)/shard_map/ppermute | solution.py:205
  32.7 13.5 %collective-permute-start.4 = (bf16[16,64,128]{2,1,0:T(8,128)(2,1)S(1)}, bf16[16,64,128]{2,1,0:T(8,128)(2,1)S(1)}, u32[]{:S(2)}, u32[]{:S(2)}) collective-permute-start(bf16[16,64,128]{2,1,0:T(8,128)(2,1)S(1)} %slice.3.a0), channel_id=1, source_target_pairs={{0,4},{4,8},{8,12},{12,0},{1,5},{5,9},{9,13},{13,1},{2,6},{6,10},{... | collective-permute-start | bytes 786440 | tf_op jit(solution)/shard_map/ppermute | solution.py:205
  35.5 10.7 %copy-start = (bf16[128,2048]{1,0:T(8,128)(2,1)S(1)}, bf16[128,2048]{1,0:T(8,128)(2,1)}, u32[]{:S(2)}) copy-start(bf16[128,2048]{1,0:T(8,128)(2,1)} %q_ref.1) | copy-start | bytes 1572868
  36.2 10.0 %copy-start.8 = (s32[8]{0:T(128)S(1)}, s32[8]{0:T(128)}, u32[]{:S(2)}) copy-start(s32[8]{0:T(128)} %lens.1) | copy-start | bytes 100
  36.2 21.5 %all-to-all-start.1 = ((bf16[64,2,640]{2,1,0:T(2,128)(2,1)}), bf16[64,2,640]{2,1,0:T(2,128)(2,1)S(1)}, u32[]{:S(2)}, u32[]{:S(2)}) async-start(bf16[64,2,640]{2,1,0:T(2,128)(2,1)} %reshape.14), calls=%async_computation.1 | async-start | bytes 327680 | tf_op jit(solution)/shard_map/all_to_all | solution.py:228
